TPU v7x, 128 devices: a whole 4x4x4 slice. The times are simulated.
128 devices in a mesh: tok: 64 (over x, y, z), head: 2 (over core).
Axes of the slice: x: 4, y: 4, z: 4, core: 2. Of those that a mesh axis runs over, the one named last changes fastest.
Arguments:
- queries: bfloat16 [2, 16384, 512], P('head', 'tok'), may hold values from -6 to 6
- key_rows: bfloat16 [2, 16384, 512], P('head', 'tok'), may hold values from -6 to 6
- value_rows: bfloat16 [2, 16384, 512], P('head', 'tok'), may hold values from -6 to 6
- step_rates: float32 [2, 16384], P('head', 'tok'), may hold values from 0.1 to 1
- w_gate: bfloat16 [2, 512, 512], P('head'), may hold values from -0.25 to 0.25
- w_up: bfloat16 [2, 512, 512], P('head'), may hold values from -0.25 to 0.25
- w_down: bfloat16 [2, 512, 512], P('head'), may hold values from -0.25 to 0.25
- out_gain: float32 [2, 512], P('head'), may hold values from 0.1 to 1.9
- cotangent: bfloat16 [2, 16384, 512], P('head', 'tok'), may hold values from -6 to 6
Outputs:
- grad_queries: bfloat16 [2, 16384, 512], P('head', 'tok')
- grad_keys: bfloat16 [2, 16384, 512], P('head', 'tok')
- grad_values: bfloat16 [2, 16384, 512], P('head', 'tok')
- grad_gate: float32 [2, 512, 512], P('head', 'tok')
- grad_up: float32 [2, 512, 512], P('head', 'tok')
- grad_down: float32 [2, 512, 512], P('head', 'tok')
All inputs are finite; a program needn't handle non-finite values.
Results may differ from a plain program's by a relative error of at most 0.03.
Values sent between devices are 32-bit elements; how exact they have to be, the bound alone decides.
No kernel may reach another device: no remote copies, remote signals or barrier semaphores. Data moves between devices by JAX's collectives and lax.ppermute only.
A program may use at most 128 MiB of HBM per device.

v0:
```python
import functools

import jax
import jax.numpy as jnp
from jax import lax
from jax.experimental import pallas as pl
from jax.experimental.pallas import tpu as pltpu
from jax.sharding import Mesh
from jax.sharding import PartitionSpec as P

TOK = ("tok_0", "tok_1", "tok_2")
ALL = TOK + ("head",)
NS_STEPS = 3
DH = 512
WIDE = 3 * DH
BF = jnp.bfloat16
F32 = jnp.float32
coef_first = 3.4445
coef_second = -4.775
coef_third = 2.0315
inner_step = 0.5
VMEM_BYTES = 48 * 1024 * 1024


def flat_at(x, y, z, c):
    return ((x * 4 + y) * 4 + z) * 2 + c


def links(move):
    out = []
    for x in range(4):
        for y in range(4):
            for z in range(4):
                for c in range(2):
                    out.append((flat_at(x, y, z, c), flat_at(*move(x, y, z, c), c)))
    return out


def partner_links(level, step):
    if level == 3:
        flips = {1: lambda i: 3 - i, 2: lambda i: i ^ 1, 3: lambda i: i ^ 2}[step]
        return links(lambda x, y, z, c: (flips(x), flips(y), flips(z)))
    axis = 3 - step

    def move(x, y, z, c):
        at = [x, y, z]
        at[axis] = at[axis] ^ 1 if (level == 1) != (c == 1) else 3 - at[axis]
        return at

    return links(move)


PARTNERS = {(level, step): partner_links(level, step) for level in (1, 2, 3) for step in (1, 2, 3)}


def sent(value, level, step):
    return lax.ppermute(value, ALL, PARTNERS[level, step])


def low_bit(i):
    return ((i + 1) // 2) % 2


def high_bit(i):
    return i // 2


def colour(bit, x, y, z):
    code = bit(x) * 4 + bit(y) * 2 + bit(z)
    if isinstance(code, int):
        return (7 - code, 1) if code >= 4 else (code, 0)
    far = code // 4
    return jnp.where(far == 1, 7 - code, code), far


def own_colours():
    x, y, z = (lax.axis_index(a) for a in TOK)
    core = lax.axis_index("head")
    low, low_far = colour(low_bit, x, y, z)
    high, high_far = colour(high_bit, x, y, z)
    first = jnp.where(core == 0, low, high)
    second = jnp.where(core == 0, high, low)
    token = (x * 4 + y) * 4 + z
    return jnp.stack([first, second, low_far * 2 + high_far, token, core]).astype(jnp.int32)


def rows_order():
    orders = []
    for core in range(2):
        order = []
        for x in range(4):
            for y in range(4):
                for z in range(4):
                    low, low_far = colour(low_bit, x, y, z)
                    high, high_far = colour(high_bit, x, y, z)
                    first, second = (low, high) if core == 0 else (high, low)
                    order.append(first * 16 + second * 4 + low_far * 2 + high_far)
        orders.append(order)
    return orders


ORDERS = rows_order()


def call(body, outs, *args, scratch=(), scalars=None, flops=0):
    specs = [pl.BlockSpec(memory_space=pltpu.VMEM)] * len(args)
    if scalars is not None:
        specs = [pl.BlockSpec(memory_space=pltpu.SMEM)] + specs
        args = (scalars, *args)
    moved = sum(a.size * a.dtype.itemsize for a in args) + sum(
        o.size * o.dtype.itemsize for o in outs
    )
    return pl.pallas_call(
        body,
        out_shape=list(outs),
        in_specs=specs,
        out_specs=[pl.BlockSpec(memory_space=pltpu.VMEM)] * len(outs),
        scratch_shapes=list(scratch),
        compiler_params=pltpu.CompilerParams(vmem_limit_bytes=VMEM_BYTES),
        cost_estimate=pl.CostEstimate(flops=flops, bytes_accessed=moved, transcendentals=0),
    )(*args)


def shape(*dims, dtype=F32):
    return jax.ShapeDtypeStruct(dims, dtype)


def nn(a, b):
    return jnp.dot(a, b, preferred_element_type=F32)


def nt(a, b):
    return lax.dot_general(a, b, (((1,), (1,)), ((), ())), preferred_element_type=F32)


def tn(a, b):
    return lax.dot_general(a, b, (((0,), (0,)), ((), ())), preferred_element_type=F32)


def part(ref, index, rows):
    return ref[pl.ds(pl.multiple_of(index * rows, rows), rows), :]


def hand_out(own, whole, outs, rows):
    for step in range(4):
        outs[step][...] = part(whole, own ^ step, rows)


def fold_body(slot, rows, own, a, b, c, d, *outs):
    for step in range(4):
        at = own[slot] ^ step
        outs[step][...] = (part(a, at, rows) + part(b, at, rows)) + (
            part(c, at, rows) + part(d, at, rows)
        )


def total_body(a, b, c, d, out):
    out[...] = (a[...] + b[...]) + (c[...] + d[...])


def join_body(own, a, b, c, d, out):
    rows = a.shape[0]
    for step, piece in enumerate((a, b, c, d)):
        out[pl.ds(pl.multiple_of((own[1] ^ step) * rows, rows), rows), :] = piece[...]


def received(blocks, level):
    return [blocks[0]] + [sent(blocks[step], level, step) for step in (1, 2, 3)]


def sum_of_32(blocks, own):
    blocks = received(blocks, 1)
    blocks = call(
        functools.partial(fold_body, 1, 32), [shape(32, WIDE)] * 4, *blocks, scalars=own
    )
    return received(blocks, 2)


def sum_everywhere(blocks, own):
    blocks = sum_of_32(blocks, own)
    (piece,) = call(total_body, [shape(32, WIDE)], *blocks)
    (piece,) = call(total_body, [shape(32, WIDE)], *received([piece] * 4, 3))
    (piece,) = call(join_body, [shape(128, WIDE)], *received([piece] * 4, 2), scalars=own)
    return received([piece] * 4, 1)


def silu_parts(pre_gate):
    sigma_gate = jax.nn.sigmoid(pre_gate)
    act_gate = pre_gate * sigma_gate
    slope_gate = sigma_gate * (1.0 + pre_gate * (1.0 - sigma_gate))
    return (act_gate, slope_gate, sigma_gate)


def as_column(row):
    return jnp.transpose(jnp.broadcast_to(row, (128, row.shape[1])))[:, :1]


def key_body(own, w_gate, w_up, w_down, keys, values, rates, *refs):
    outs, stored, (whole,) = refs[:4], refs[4:11], refs[11:]
    gate, up, mid, mixed, target, dgate, dup = stored
    k = keys[...]
    t = (-as_column(rates[...]) * values[...].astype(F32)).astype(BF)
    target[...] = t
    g = nn(k, w_gate[...])
    u = nn(k, w_up[...])
    m = nt(t, w_down[...])
    gate[...] = g
    up[...] = u
    mid[...] = m
    act, slope, _ = silu_parts(g)
    mix = (act * u).astype(BF)
    dg = (m * u * slope).astype(BF)
    du = (m * act).astype(BF)
    mixed[...] = mix
    dgate[...] = dg
    dup[...] = du
    whole[:, :DH] = tn(k, dg)
    whole[:, DH : 2 * DH] = tn(k, du)
    whole[:, 2 * DH :] = tn(mix, t)
    hand_out(own[0], whole, outs, DH // 4)


def query_forward_body(new, queries, cotangent, gain, stats, output, act_out, slope_out, mixed):
    q = queries[...]
    g = nn(q, new[0])
    u = nn(q, new[1])
    act, slope, _ = silu_parts(g)
    mix = (act * u).astype(BF)
    out = nn(mix, new[2])
    squares = jnp.sum(out * out, axis=1, keepdims=True)
    aligned = jnp.sum(cotangent[...].astype(F32) * gain[...] * out, axis=1, keepdims=True)
    lane = lax.broadcasted_iota(jnp.int32, stats.shape, 1)
    stats[...] = jnp.where(lane == 0, squares, aligned)
    output[...] = out
    act_out[...] = act
    slope_out[...] = u * slope
    mixed[...] = mix


def query_backward_body(
    own, new, queries, cotangent, gain, stats, other, output, act, slope, mixed, *refs
):
    query_grad, outs, (whole,) = refs[0], refs[1:5], refs[5:]
    both = stats[...] + other[...]
    inverse_rms = lax.rsqrt(both[:, :1] / (2 * DH) + 1e-05)
    aligned = both[:, 1:2]
    grad_output = (
        gain[...] * cotangent[...].astype(F32) * inverse_rms
        - output[...] * (aligned * inverse_rms * inverse_rms * inverse_rms / (2 * DH))
    ).astype(BF)
    mid = nt(grad_output, new[2])
    dgate = (mid * slope[...]).astype(BF)
    dup = (mid * act[...]).astype(BF)
    query_grad[...] = (nt(dgate, new[0]) + nt(dup, new[1])).astype(BF)
    q = queries[...]
    whole[:, :DH] = tn(q, dgate)
    whole[:, DH : 2 * DH] = tn(q, dup)
    whole[:, 2 * DH :] = tn(mixed[...], grad_output)
    hand_out(own[0], whole, outs, DH // 4)


def key_backward_body(
    own, cots, w_gate, w_up, w_down, keys, rates, gate, up, mid, mixed, target, dgate, dup, *refs
):
    key_grad, value_grad, outs, (whole,) = refs[0], refs[1], refs[2:6], refs[6:]
    k = keys[...]
    t = target[...]
    cot_a, cot_b, cot_c = cots[0], cots[1], cots[2]
    back_gate = nn(k, cot_a)
    back_up = nn(k, cot_b)
    back_mixed = nt(t, cot_c)
    g = gate[...]
    u = up[...]
    m = mid[...]
    act, slope, sigma = silu_parts(g)
    curve = sigma * (1.0 - sigma) * (2.0 + g * (1.0 - 2.0 * sigma))
    back_mid = (back_gate * u * slope + back_up * act).astype(BF)
    gate_back = (
        back_gate * m * u * curve + back_up * m * slope + back_mixed * u * slope
    ).astype(BF)
    up_back = (back_gate * m * slope + back_mixed * act).astype(BF)
    whole[:, :DH] = tn(k, gate_back)
    whole[:, DH : 2 * DH] = tn(k, up_back)
    whole[:, 2 * DH :] = tn(back_mid, t)
    key_grad[...] = (
        nt(dgate[...], cot_a)
        + nt(dup[...], cot_b)
        + nt(gate_back, w_gate[...])
        + nt(up_back, w_up[...])
    ).astype(BF)
    value_sum = nn(mixed[...], cot_c) + nn(back_mid, w_down[...])
    value_grad[...] = (-as_column(rates[...]) * value_sum).astype(BF)
    first = own[0]
    for step in range(4):
        for t_in in range(16):
            block = (first ^ step) * 16 + t_in
            source = own[8 + block]
            outs[step][8 * t_in : 8 * t_in + 8, :] = part(whole, source, 8)


def share_body(share, a, b, c, d, out_a, out_b, out_c):
    value = share[...] + ((a[...] + b[...]) + (c[...] + d[...]))
    out_a[0] = value[:, :DH]
    out_b[0] = value[:, DH : 2 * DH]
    out_c[0] = value[:, 2 * DH :]


def gather_in(own, blocks, whole):
    rows = DH // 4
    for step, block in enumerate(blocks):
        whole[pl.ds(pl.multiple_of((own[0] ^ step) * rows, rows), rows), :] = block[...]


def ortho_body(own, a, b, c, d, w_gate, w_up, w_down, new, kept, norm, whole):
    gather_in(own, (a, b, c, d), whole)
    matrix = whole[...]
    root = jnp.sqrt(jnp.sum(matrix * matrix, keepdims=True) + 1e-06)
    current = matrix * (1.0 / root)
    for step in range(NS_STEPS):
        narrow = current.astype(BF)
        gram = nt(narrow, narrow)
        gram_low = gram.astype(BF)
        poly = (coef_second * gram + coef_third * nn(gram_low, gram_low)).astype(BF)
        kept[3 * step] = narrow
        kept[3 * step + 1] = gram_low
        kept[3 * step + 2] = poly
        current = coef_first * current + nn(poly, narrow)
    norm[...] = jnp.broadcast_to(root, norm.shape)
    for index, weight in enumerate((w_gate, w_up, w_down)):

        @pl.when(pl.program_id(0) == index)
        def _():
            new[...] = (weight[...].astype(F32) - inner_step * current).astype(BF)


def ortho_back_body(own, a, b, c, d, kept, norm, cots, share, whole):
    gather_in(own, (a, b, c, d), whole)
    share[...] = part(whole, own[3], 8)
    grad = whole[...] * (-inner_step)
    for step in reversed(range(NS_STEPS)):
        narrow, gram_low, poly = kept[3 * step], kept[3 * step + 1], kept[3 * step + 2]
        grad_low = grad.astype(BF)
        half = nt(grad_low, narrow)
        sym = half + jnp.transpose(half)
        cross = nn(sym.astype(BF), gram_low)
        full = coef_second * sym + coef_third * (cross + jnp.transpose(cross))
        grad = coef_first * grad + nn(poly, grad_low) + nn(full.astype(BF), narrow)
    unit = kept[0].astype(F32)
    along = jnp.sum(grad * unit, keepdims=True)
    cots[...] = ((grad - unit * along) * (1.0 / norm[:1, :1])).astype(BF)


def one_of_three(*dims):
    return pl.BlockSpec((None, *dims), lambda i: (i,) + (0,) * len(dims))


SMEM = pl.BlockSpec(memory_space=pltpu.SMEM)
QUARTERS = [pl.BlockSpec((DH // 4, DH), lambda i: (0, i))] * 4
WHOLE = pl.BlockSpec((DH, DH), lambda i: (0, 0))
PARAMS = pltpu.CompilerParams(vmem_limit_bytes=VMEM_BYTES)


def ortho(blocks, own, w_gate, w_up, w_down):
    return pl.pallas_call(
        ortho_body,
        grid=(3,),
        in_specs=[SMEM, *QUARTERS, WHOLE, WHOLE, WHOLE],
        out_specs=[one_of_three(DH, DH), one_of_three(9, DH, DH), one_of_three(8, 128)],
        out_shape=[shape(3, DH, DH, dtype=BF), shape(3, 9, DH, DH, dtype=BF), shape(3, 8, 128)],
        scratch_shapes=[pltpu.VMEM((DH, DH), F32)],
        compiler_params=PARAMS,
    )(own, *blocks, w_gate, w_up, w_down)


def ortho_back(blocks, own, kept, norm):
    return pl.pallas_call(
        ortho_back_body,
        grid=(3,),
        in_specs=[SMEM, *QUARTERS, one_of_three(9, DH, DH), one_of_three(8, 128)],
        out_specs=[one_of_three(DH, DH), pl.BlockSpec((8, DH), lambda i: (0, i))],
        out_shape=[shape(3, DH, DH, dtype=BF), shape(8, WIDE)],
        scratch_shapes=[pltpu.VMEM((DH, DH), F32)],
        compiler_params=PARAMS,
    )(own, *blocks, kept, norm)


def local(queries, key_rows, value_rows, step_rates, w_gate, w_up, w_down, out_gain, cotangent):
    tokens = queries.shape[1]
    queries, key_rows, value_rows, cotangent = (
        a[0] for a in (queries, key_rows, value_rows, cotangent)
    )
    w_gate, w_up, w_down = w_gate[0], w_up[0], w_down[0]
    own = own_colours()
    inverse = jnp.asarray(
        [[order.index(block) for block in range(64)] for order in ORDERS], jnp.int32
    )
    own = jnp.concatenate([own, jnp.zeros(3, jnp.int32), inverse[own[4]]])

    whole = pltpu.VMEM((DH, WIDE), F32)
    quarters = [shape(DH // 4, WIDE)] * 4
    wide = shape(tokens, DH)
    low = shape(tokens, DH, dtype=BF)
    *blocks, gate, up, mid, mixed, target, dgate, dup = call(
        key_body,
        [*quarters, wide, wide, wide, low, low, low, low],
        w_gate,
        w_up,
        w_down,
        key_rows,
        value_rows,
        step_rates,
        scratch=[whole],
        scalars=own,
    )
    new, kept, norm = ortho(sum_everywhere(blocks, own), own, w_gate, w_up, w_down)
    stats, *query_stored = call(
        query_forward_body,
        [shape(tokens, 128), wide, wide, wide, low],
        new,
        queries,
        cotangent,
        out_gain,
    )
    swap = links(lambda x, y, z, c: (x, y, z))
    swap = [(source, target_at ^ 1) for source, target_at in swap]
    other = lax.ppermute(stats, ALL, swap)
    query_grad, *blocks = call(
        query_backward_body,
        [low, *quarters],
        new,
        queries,
        cotangent,
        out_gain,
        stats,
        other,
        *query_stored,
        scratch=[whole],
        scalars=own,
    )
    cots, share = ortho_back(sum_everywhere(blocks, own), own, kept, norm)
    key_grad, value_grad, *blocks = call(
        key_backward_body,
        [low, low, *quarters],
        cots,
        w_gate,
        w_up,
        w_down,
        key_rows,
        step_rates,
        gate,
        up,
        mid,
        mixed,
        target,
        dgate,
        dup,
        scratch=[whole],
        scalars=own,
    )
    blocks = sum_of_32(blocks, own)
    blocks = call(
        functools.partial(fold_body, 2, 8), [shape(8, WIDE)] * 4, *blocks, scalars=own
    )
    grads = call(share_body, [shape(1, 8, DH)] * 3, share, *received(blocks, 3))
    return (query_grad[None], key_grad[None], value_grad[None], *grads)


def solution(mesh):
    split = Mesh(
        mesh.devices.reshape(4, 4, 4, mesh.shape["head"]), ("tok_0", "tok_1", "tok_2", "head")
    )
    rows = P("head", TOK, None)
    weight = P("head", None, None)
    in_specs = (
        rows,
        rows,
        rows,
        P("head", TOK),
        weight,
        weight,
        weight,
        P("head", None),
        rows,
    )
    return jax.shard_map(
        local, mesh=split, in_specs=in_specs, out_specs=(rows,) * 6, check_vma=False
    )
```

profile of v0, /device:TPU:0, one launch (start us, length us, event | category | flops | bytes accessed | tf_op | source)
XLA Modules:
  0.0 230.3 jit_solution(11187900542897317420)
XLA Ops:
  7.3 3.4 %shard_map.145 = (f32[128,1536]{1,0:T(8,128)S(1)}, f32[128,1536]{1,0:T(8,128)}, f32[128,1536]{1,0:T(8,128)}, f32[128,1536]{1,0:T(8,128)}, f32[256,512]{1,0:T(8,1...) custom-call(s32[72]{0:T(128)S(1)} %concatenate.3.own, ...), custom_call_target="tpu_custom_call" | custom-call | bytes 7865632 | tf_op jit(solution)/shard_map/pallas_call | solution.py:113
  15.7 7.1 %collective-permute-done.b = f32[128,1536]{1,0:T(8,128)S(1)} collective-permute-done((f32[128,1536]{1,0:T(8,128)}, f32[128,1536]{1,0:T(8,128)S(1)}, u32[]{:S(2)}, u32[]{:S(2)}) %collective-permute-start) | collective-permute-done | bytes 786464 | tf_op jit(solution)/shard_map/ppermute | solution.py:57
  31.9 2.8 %collective-permute-start.5 = (f32[32,1536]{1,0:T(8,128)S(1)}, f32[32,1536]{1,0:T(8,128)S(1)}, u32[]{:S(2)}, u32[]{:S(2)}) collective-permute-start(f32[32,1536]{1,0:T(8,128)S(1)} %get-tuple-element.64), channel_id=1, source_target_pairs={{0,96},{1,33},{2,98},{3,35},{4,100},{5,37},{6,102},{7,39},{8,104},... | collective-permute-start | bytes 589832 | tf_op jit(solution)/shard_map/ppermute | solution.py:57
  38.8 2.7 %collective-permute-start.8 = (f32[32,1536]{1,0:T(8,128)S(1)}, f32[32,1536]{1,0:T(8,128)S(1)}, u32[]{:S(2)}, u32[]{:S(2)}) collective-permute-start(f32[32,1536]{1,0:T(8,128)S(1)} %shard_map.147.a), channel_id=1, source_target_pairs={{0,84},{1,85},{2,86},{3,87},{4,80},{5,81},{6,82},{7,83},{8,92},{9,... | collective-permute-start | bytes 589832 | tf_op jit(solution)/shard_map/ppermute | solution.py:57
  43.8 4.1 %collective-permute-start.6 = (f32[32,1536]{1,0:T(8,128)S(1)}, f32[32,1536]{1,0:T(8,128)S(1)}, u32[]{:S(2)}, u32[]{:S(2)}) collective-permute-start(f32[32,1536]{1,0:T(8,128)S(1)} %shard_map.147.a), channel_id=1, source_target_pairs={{0,126},{1,127},{2,124},{3,125},{4,122},{5,123},{6,120},{7,121},{8... | collective-permute-start | bytes 589832 | tf_op jit(solution)/shard_map/ppermute | solution.py:57
  47.8 5.6 %collective-permute-done.8.d = f32[32,1536]{1,0:T(8,128)S(1)} collective-permute-done((f32[32,1536]{1,0:T(8,128)S(1)}, f32[32,1536]{1,0:T(8,128)S(1)}, u32[]{:S(2)}, u32[]{:S(2)}) %collective-permute-start.8) | collective-permute-done | bytes 196640 | tf_op jit(solution)/shard_map/ppermute | solution.py:57
  55.3 2.7 %collective-permute-start.11 = (f32[32,1536]{1,0:T(8,128)S(1)}, f32[32,1536]{1,0:T(8,128)S(1)}, u32[]{:S(2)}, u32[]{:S(2)}) collective-permute-start(f32[32,1536]{1,0:T(8,128)S(1)} %shard_map.148.a), channel_id=1, source_target_pairs={{0,96},{1,33},{2,98},{3,35},{4,100},{5,37},{6,102},{7,39},{8,104},... | collective-permute-start | bytes 589832 | tf_op jit(solution)/shard_map/ppermute | solution.py:57
  66.8 11.8 %collective-permute-done.14.d = f32[128,1536]{1,0:T(8,128)S(1)} collective-permute-done((f32[128,1536]{1,0:T(8,128)S(1)}, f32[128,1536]{1,0:T(8,128)S(1)}, u32[]{:S(2)}, u32[]{:S(2)}) %collective-permute-start.14) | collective-permute-done | bytes 786464 | tf_op jit(solution)/shard_map/ppermute | solution.py:57
  78.8 14.4 %shard_map.150 = (bf16[3,512,512]{2,1,0:T(8,128)(2,1)}, bf16[3,9,512,512]{3,2,1,0:T(8,128)(2,1)}, f32[3,8,128]{2,1,0:T(8,128)S(1)}) custom-call(s32[72]{0:T(128)S(1)} %concatenate.3.own, f32[128,1536]{1,0:T(8,128)S(1)} %shard_map.149.a, f32[128,1536]{1,0:T(8,128)S(1)} %collective-permute-done.12.b, f32[128,1536]{1,0:T(8,128)S(1)} %collective-permute-done.13.c, ...), custom_call_target="tpu_custom_call" | custom-call | tf_op jit(solution)/shard_map/pallas_call | solution.py:364
  96.9 3.5 %shard_map.152 = (bf16[256,512]{1,0:T(8,128)(2,1)}, f32[128,1536]{1,0:T(8,128)S(1)}, f32[128,1536]{1,0:T(8,128)S(1)}, f32[128,1536]{1,0:T(8,128)S(1)}, f32[128,1536]{1,0:T(8,128)S(1)}) custom-call(s32[72]{0:T(128)S(1)} %concatenate.3.own, bf16[3,512,512]{2,1,0:T(8,128)(2,1)} %get-tuple-element.65.new, bf16[256,512]{1,0:T(8,128)(2,1)S(1)} %bitcast.27, ...), custom_call_target="tpu_custom_call" | custom-call | bytes 7604512 | tf_op jit(solution)/shard_map/pallas_call | solution.py:113
  104.3 8.1 %collective-permute-done.16.b = f32[128,1536]{1,0:T(8,128)S(1)} collective-permute-done((f32[128,1536]{1,0:T(8,128)S(1)}, f32[128,1536]{1,0:T(8,128)S(1)}, u32[]{:S(2)}, u32[]{:S(2)}) %collective-permute-start.16) | collective-permute-done | bytes 786464 | tf_op jit(solution)/shard_map/ppermute | solution.py:57
  125.9 4.3 %collective-permute-start.24 = (f32[32,1536]{1,0:T(8,128)S(1)}, f32[32,1536]{1,0:T(8,128)S(1)}, u32[]{:S(2)}, u32[]{:S(2)}) collective-permute-start(f32[32,1536]{1,0:T(8,128)S(1)} %shard_map.154.a), channel_id=1, source_target_pairs={{0,84},{1,85},{2,86},{3,87},{4,80},{5,81},{6,82},{7,83},{8,92},{9,... | collective-permute-start | bytes 589832 | tf_op jit(solution)/shard_map/ppermute | solution.py:57
  131.1 3.7 %collective-permute-start.22 = (f32[32,1536]{1,0:T(8,128)S(1)}, f32[32,1536]{1,0:T(8,128)S(1)}, u32[]{:S(2)}, u32[]{:S(2)}) collective-permute-start(f32[32,1536]{1,0:T(8,128)S(1)} %shard_map.154.a), channel_id=1, source_target_pairs={{0,126},{1,127},{2,124},{3,125},{4,122},{5,123},{6,120},{7,121},{8... | collective-permute-start | bytes 589832 | tf_op jit(solution)/shard_map/ppermute | solution.py:57
  134.9 5.6 %collective-permute-done.24.d = f32[32,1536]{1,0:T(8,128)S(1)} collective-permute-done((f32[32,1536]{1,0:T(8,128)S(1)}, f32[32,1536]{1,0:T(8,128)S(1)}, u32[]{:S(2)}, u32[]{:S(2)}) %collective-permute-start.24) | collective-permute-done | bytes 196640 | tf_op jit(solution)/shard_map/ppermute | solution.py:57
  151.8 2.9 %collective-permute-done.25.b = f32[32,1536]{1,0:T(8,128)S(1)} collective-permute-done((f32[32,1536]{1,0:T(8,128)S(1)}, f32[32,1536]{1,0:T(8,128)S(1)}, u32[]{:S(2)}, u32[]{:S(2)}) %collective-permute-start.25) | collective-permute-done | bytes 196640 | tf_op jit(solution)/shard_map/ppermute | solution.py:57
  155.5 11.8 %collective-permute-done.30.d = f32[128,1536]{1,0:T(8,128)S(1)} collective-permute-done((f32[128,1536]{1,0:T(8,128)S(1)}, f32[128,1536]{1,0:T(8,128)S(1)}, u32[]{:S(2)}, u32[]{:S(2)}) %collective-permute-start.30) | collective-permute-done | bytes 786464 | tf_op jit(solution)/shard_map/ppermute | solution.py:57
  167.5 15.8 %shard_map.157 = (bf16[3,512,512]{2,1,0:T(8,128)(2,1)S(1)}, f32[8,1536]{1,0:T(8,128)S(1)}) custom-call(s32[72]{0:T(128)S(1)} %concatenate.3.own, f32[128,1536]{1,0:T(8,128)S(1)} %shard_map.156.a, f32[128,1536]{1,0:T(8,128)S(1)} %collective-permute-done.28.b, f32[128,1536]{1,0:T(8,128)S(1)} %collective-permute-done.29.c, ...), custom_call_target="tpu_custom_call" | custom-call | tf_op jit(solution)/shard_map/pallas_call | solution.py:376
  184.6 5.0 %shard_map.158 = (bf16[256,512]{1,0:T(8,128)(2,1)}, bf16[256,512]{1,0:T(8,128)(2,1)}, f32[128,1536]{1,0:T(8,128)S(1)}, f32[128,1536]{1,0:T(8,128)S(1)}, f32[128,1536]{1,0:T(8,128)}, /*index=5*/f32[128,1536]{1,0:T(8,128)}) custom-call(s32[72]{0:T(128)S(1)} %concatenate.3.own, bf16[3,512,512]{2,1,0:T(8,128)(2,1)} %copy-done.7, bf16[512,512]{1,0:T(8,128)(2,1)S(1)} %bitcast.19, ...), custom_call_target="tpu_custom_call" | custom-call | bytes 9700640 | tf_op jit(solution)/shard_map/pallas_call | solution.py:113
  193.4 8.1 %collective-permute-done.31.b = f32[128,1536]{1,0:T(8,128)S(1)} collective-permute-done((f32[128,1536]{1,0:T(8,128)S(1)}, f32[128,1536]{1,0:T(8,128)S(1)}, u32[]{:S(2)}, u32[]{:S(2)}) %collective-permute-start.31) | collective-permute-done | bytes 786464 | tf_op jit(solution)/shard_map/ppermute | solution.py:57
  201.8 3.5 %collective-permute-done.33.d = f32[128,1536]{1,0:T(8,128)S(1)} collective-permute-done((f32[128,1536]{1,0:T(8,128)}, f32[128,1536]{1,0:T(8,128)S(1)}, u32[]{:S(2)}, u32[]{:S(2)}) %collective-permute-start.33) | collective-permute-done | bytes 786464 | tf_op jit(solution)/shard_map/ppermute | solution.py:57
  206.7 4.8 %collective-permute-start.36 = (f32[32,1536]{1,0:T(8,128)S(1)}, f32[32,1536]{1,0:T(8,128)S(1)}, u32[]{:S(2)}, u32[]{:S(2)}) collective-permute-start(f32[32,1536]{1,0:T(8,128)S(1)} %get-tuple-element.100), channel_id=1, source_target_pairs={{0,96},{1,33},{2,98},{3,35},{4,100},{5,37},{6,102},{7,39},{8,104},... | collective-permute-start | bytes 589832 | tf_op jit(solution)/shard_map/ppermute | solution.py:57
  215.7 3.3 %collective-permute-start.37 = (f32[8,1536]{1,0:T(8,128)S(1)}, f32[8,1536]{1,0:T(8,128)S(1)}, u32[]{:S(2)}, u32[]{:S(2)}) collective-permute-start(f32[8,1536]{1,0:T(8,128)S(1)} %get-tuple-element.102), channel_id=1, source_target_pairs={{0,126},{1,127},{2,124},{3,125},{4,122},{5,123},{6,120},{7,121},{8... | collective-permute-start | bytes 147464 | tf_op jit(solution)/shard_map/ppermute | solution.py:57
  219.0 7.5 %collective-permute-start.39 = (f32[8,1536]{1,0:T(8,128)S(1)}, f32[8,1536]{1,0:T(8,128)S(1)}, u32[]{:S(2)}, u32[]{:S(2)}) collective-permute-start(f32[8,1536]{1,0:T(8,128)S(1)} %get-tuple-element.104), channel_id=1, source_target_pairs={{0,84},{1,85},{2,86},{3,87},{4,80},{5,81},{6,82},{7,83},{8,92},{9,... | collective-permute-start | bytes 147464 | tf_op jit(solution)/shard_map/ppermute | solution.py:57
  226.5 3.1 %collective-permute-done.39.d = f32[8,1536]{1,0:T(8,128)S(1)} collective-permute-done((f32[8,1536]{1,0:T(8,128)S(1)}, f32[8,1536]{1,0:T(8,128)S(1)}, u32[]{:S(2)}, u32[]{:S(2)}) %collective-permute-start.39) | collective-permute-done | bytes 49184 | tf_op jit(solution)/shard_map/ppermute | solution.py:57
  (108 shorter events, 83.5 us)
Async XLA Ops:
  10.6 12.2 %collective-permute-start = (f32[128,1536]{1,0:T(8,128)}, f32[128,1536]{1,0:T(8,128)S(1)}, u32[]{:S(2)}, u32[]{:S(2)}) collective-permute-start(f32[128,1536]{1,0:T(8,128)} %get-tuple-element.58), channel_id=1, source_target_pairs={{0,2},{1,7},{2,0},{3,5},{4,6},{5,3},{6,4},{7,1},{8,10},{9,15},{10,... | collective-permute-start | bytes 2359304 | tf_op jit(solution)/shard_map/ppermute | solution.py:57
  12.6 12.2 %collective-permute-start.1 = (f32[128,1536]{1,0:T(8,128)}, f32[128,1536]{1,0:T(8,128)S(1)}, u32[]{:S(2)}, u32[]{:S(2)}) collective-permute-start(f32[128,1536]{1,0:T(8,128)} %get-tuple-element.59), channel_id=1, source_target_pairs={{0,8},{1,25},{2,10},{3,27},{4,12},{5,29},{6,14},{7,31},{8,0},{9,17... | collective-permute-start | bytes 2359304 | tf_op jit(solution)/shard_map/ppermute | solution.py:57
  14.2 12.2 %collective-permute-start.2 = (f32[128,1536]{1,0:T(8,128)}, f32[128,1536]{1,0:T(8,128)S(1)}, u32[]{:S(2)}, u32[]{:S(2)}) collective-permute-start(f32[128,1536]{1,0:T(8,128)} %get-tuple-element.60), channel_id=1, source_target_pairs={{0,32},{1,97},{2,34},{3,99},{4,36},{5,101},{6,38},{7,103},{8,40},{... | collective-permute-start | bytes 2359304 | tf_op jit(solution)/shard_map/ppermute | solution.py:57
  38.8 14.6 %collective-permute-start.8 = (f32[32,1536]{1,0:T(8,128)S(1)}, f32[32,1536]{1,0:T(8,128)S(1)}, u32[]{:S(2)}, u32[]{:S(2)}) collective-permute-start(f32[32,1536]{1,0:T(8,128)S(1)} %shard_map.147.a), channel_id=1, source_target_pairs={{0,84},{1,85},{2,86},{3,87},{4,80},{5,81},{6,82},{7,83},{8,92},{9,... | collective-permute-start | bytes 589832 | tf_op jit(solution)/shard_map/ppermute | solution.py:57
  41.6 11.9 %collective-permute-start.7 = (f32[32,1536]{1,0:T(8,128)S(1)}, f32[32,1536]{1,0:T(8,128)S(1)}, u32[]{:S(2)}, u32[]{:S(2)}) collective-permute-start(f32[32,1536]{1,0:T(8,128)S(1)} %shard_map.147.a), channel_id=1, source_target_pairs={{0,42},{1,43},{2,40},{3,41},{4,46},{5,47},{6,44},{7,45},{8,34},{9,... | collective-permute-start | bytes 589832 | tf_op jit(solution)/shard_map/ppermute | solution.py:57
  43.8 11.5 %collective-permute-start.6 = (f32[32,1536]{1,0:T(8,128)S(1)}, f32[32,1536]{1,0:T(8,128)S(1)}, u32[]{:S(2)}, u32[]{:S(2)}) collective-permute-start(f32[32,1536]{1,0:T(8,128)S(1)} %shard_map.147.a), channel_id=1, source_target_pairs={{0,126},{1,127},{2,124},{3,125},{4,122},{5,123},{6,120},{7,121},{8... | collective-permute-start | bytes 589832 | tf_op jit(solution)/shard_map/ppermute | solution.py:57
  66.6 12.1 %collective-permute-start.14 = (f32[128,1536]{1,0:T(8,128)S(1)}, f32[128,1536]{1,0:T(8,128)S(1)}, u32[]{:S(2)}, u32[]{:S(2)}) collective-permute-start(f32[128,1536]{1,0:T(8,128)S(1)} %shard_map.149.a), channel_id=1, source_target_pairs={{0,32},{1,97},{2,34},{3,99},{4,36},{5,101},{6,38},{7,103},{8,40},{... | collective-permute-start | bytes 2359304 | tf_op jit(solution)/shard_map/ppermute | solution.py:57
  66.6 12.1 %collective-permute-start.13 = (f32[128,1536]{1,0:T(8,128)S(1)}, f32[128,1536]{1,0:T(8,128)S(1)}, u32[]{:S(2)}, u32[]{:S(2)}) collective-permute-start(f32[128,1536]{1,0:T(8,128)S(1)} %shard_map.149.a), channel_id=1, source_target_pairs={{0,8},{1,25},{2,10},{3,27},{4,12},{5,29},{6,14},{7,31},{8,0},{9,17... | collective-permute-start | bytes 2359304 | tf_op jit(solution)/shard_map/ppermute | solution.py:57
  66.7 12.1 %collective-permute-start.12 = (f32[128,1536]{1,0:T(8,128)S(1)}, f32[128,1536]{1,0:T(8,128)S(1)}, u32[]{:S(2)}, u32[]{:S(2)}) collective-permute-start(f32[128,1536]{1,0:T(8,128)S(1)} %shard_map.149.a), channel_id=1, source_target_pairs={{0,2},{1,7},{2,0},{3,5},{4,6},{5,3},{6,4},{7,1},{8,10},{9,15},{10,... | collective-permute-start | bytes 2359304 | tf_op jit(solution)/shard_map/ppermute | solution.py:57
  100.4 12.0 %collective-permute-start.16 = (f32[128,1536]{1,0:T(8,128)S(1)}, f32[128,1536]{1,0:T(8,128)S(1)}, u32[]{:S(2)}, u32[]{:S(2)}) collective-permute-start(f32[128,1536]{1,0:T(8,128)S(1)} %get-tuple-element.73), channel_id=1, source_target_pairs={{0,2},{1,7},{2,0},{3,5},{4,6},{5,3},{6,4},{7,1},{8,10},{9,15},{10,... | collective-permute-start | bytes 2359304 | tf_op jit(solution)/shard_map/ppermute | solution.py:57
  100.4 12.0 %collective-permute-start.17 = (f32[128,1536]{1,0:T(8,128)S(1)}, f32[128,1536]{1,0:T(8,128)S(1)}, u32[]{:S(2)}, u32[]{:S(2)}) collective-permute-start(f32[128,1536]{1,0:T(8,128)S(1)} %get-tuple-element.74), channel_id=1, source_target_pairs={{0,8},{1,25},{2,10},{3,27},{4,12},{5,29},{6,14},{7,31},{8,0},{9,17... | collective-permute-start | bytes 2359304 | tf_op jit(solution)/shard_map/ppermute | solution.py:57
  102.3 12.0 %collective-permute-start.18 = (f32[128,1536]{1,0:T(8,128)S(1)}, f32[128,1536]{1,0:T(8,128)S(1)}, u32[]{:S(2)}, u32[]{:S(2)}) collective-permute-start(f32[128,1536]{1,0:T(8,128)S(1)} %get-tuple-element.75), channel_id=1, source_target_pairs={{0,32},{1,97},{2,34},{3,99},{4,36},{5,101},{6,38},{7,103},{8,40},{... | collective-permute-start | bytes 2359304 | tf_op jit(solution)/shard_map/ppermute | solution.py:57
  125.9 14.6 %collective-permute-start.24 = (f32[32,1536]{1,0:T(8,128)S(1)}, f32[32,1536]{1,0:T(8,128)S(1)}, u32[]{:S(2)}, u32[]{:S(2)}) collective-permute-start(f32[32,1536]{1,0:T(8,128)S(1)} %shard_map.154.a), channel_id=1, source_target_pairs={{0,84},{1,85},{2,86},{3,87},{4,80},{5,81},{6,82},{7,83},{8,92},{9,... | collective-permute-start | bytes 589832 | tf_op jit(solution)/shard_map/ppermute | solution.py:57
  130.2 10.3 %collective-permute-start.23 = (f32[32,1536]{1,0:T(8,128)S(1)}, f32[32,1536]{1,0:T(8,128)S(1)}, u32[]{:S(2)}, u32[]{:S(2)}) collective-permute-start(f32[32,1536]{1,0:T(8,128)S(1)} %shard_map.154.a), channel_id=1, source_target_pairs={{0,42},{1,43},{2,40},{3,41},{4,46},{5,47},{6,44},{7,45},{8,34},{9,... | collective-permute-start | bytes 589832 | tf_op jit(solution)/shard_map/ppermute | solution.py:57
  131.1 11.9 %collective-permute-start.22 = (f32[32,1536]{1,0:T(8,128)S(1)}, f32[32,1536]{1,0:T(8,128)S(1)}, u32[]{:S(2)}, u32[]{:S(2)}) collective-permute-start(f32[32,1536]{1,0:T(8,128)S(1)} %shard_map.154.a), channel_id=1, source_target_pairs={{0,126},{1,127},{2,124},{3,125},{4,122},{5,123},{6,120},{7,121},{8... | collective-permute-start | bytes 589832 | tf_op jit(solution)/shard_map/ppermute | solution.py:57
  155.3 12.1 %collective-permute-start.30 = (f32[128,1536]{1,0:T(8,128)S(1)}, f32[128,1536]{1,0:T(8,128)S(1)}, u32[]{:S(2)}, u32[]{:S(2)}) collective-permute-start(f32[128,1536]{1,0:T(8,128)S(1)} %shard_map.156.a), channel_id=1, source_target_pairs={{0,32},{1,97},{2,34},{3,99},{4,36},{5,101},{6,38},{7,103},{8,40},{... | collective-permute-start | bytes 2359304 | tf_op jit(solution)/shard_map/ppermute | solution.py:57
  155.3 12.1 %collective-permute-start.29 = (f32[128,1536]{1,0:T(8,128)S(1)}, f32[128,1536]{1,0:T(8,128)S(1)}, u32[]{:S(2)}, u32[]{:S(2)}) collective-permute-start(f32[128,1536]{1,0:T(8,128)S(1)} %shard_map.156.a), channel_id=1, source_target_pairs={{0,8},{1,25},{2,10},{3,27},{4,12},{5,29},{6,14},{7,31},{8,0},{9,17... | collective-permute-start | bytes 2359304 | tf_op jit(solution)/shard_map/ppermute | solution.py:57
  155.4 12.1 %collective-permute-start.28 = (f32[128,1536]{1,0:T(8,128)S(1)}, f32[128,1536]{1,0:T(8,128)S(1)}, u32[]{:S(2)}, u32[]{:S(2)}) collective-permute-start(f32[128,1536]{1,0:T(8,128)S(1)} %shard_map.156.a), channel_id=1, source_target_pairs={{0,2},{1,7},{2,0},{3,5},{4,6},{5,3},{6,4},{7,1},{8,10},{9,15},{10,... | collective-permute-start | bytes 2359304 | tf_op jit(solution)/shard_map/ppermute | solution.py:57
  189.6 12.0 %collective-permute-start.31 = (f32[128,1536]{1,0:T(8,128)S(1)}, f32[128,1536]{1,0:T(8,128)S(1)}, u32[]{:S(2)}, u32[]{:S(2)}) collective-permute-start(f32[128,1536]{1,0:T(8,128)S(1)} %get-tuple-element.94), channel_id=1, source_target_pairs={{0,2},{1,7},{2,0},{3,5},{4,6},{5,3},{6,4},{7,1},{8,10},{9,15},{10,... | collective-permute-start | bytes 2359304 | tf_op jit(solution)/shard_map/ppermute | solution.py:57
  189.6 12.2 %collective-permute-start.32 = (f32[128,1536]{1,0:T(8,128)}, f32[128,1536]{1,0:T(8,128)S(1)}, u32[]{:S(2)}, u32[]{:S(2)}) collective-permute-start(f32[128,1536]{1,0:T(8,128)} %get-tuple-element.95), channel_id=1, source_target_pairs={{0,8},{1,25},{2,10},{3,27},{4,12},{5,29},{6,14},{7,31},{8,0},{9,17... | collective-permute-start | bytes 2359304 | tf_op jit(solution)/shard_map/ppermute | solution.py:57
  191.5 13.8 %collective-permute-start.33 = (f32[128,1536]{1,0:T(8,128)}, f32[128,1536]{1,0:T(8,128)S(1)}, u32[]{:S(2)}, u32[]{:S(2)}) collective-permute-start(f32[128,1536]{1,0:T(8,128)} %get-tuple-element.96), channel_id=1, source_target_pairs={{0,32},{1,97},{2,34},{3,99},{4,36},{5,101},{6,38},{7,103},{8,40},{... | collective-permute-start | bytes 2359304 | tf_op jit(solution)/shard_map/ppermute | solution.py:57
  206.7 8.4 %collective-permute-start.36 = (f32[32,1536]{1,0:T(8,128)S(1)}, f32[32,1536]{1,0:T(8,128)S(1)}, u32[]{:S(2)}, u32[]{:S(2)}) collective-permute-start(f32[32,1536]{1,0:T(8,128)S(1)} %get-tuple-element.100), channel_id=1, source_target_pairs={{0,96},{1,33},{2,98},{3,35},{4,100},{5,37},{6,102},{7,39},{8,104},... | collective-permute-start | bytes 589832 | tf_op jit(solution)/shard_map/ppermute | solution.py:57
  215.7 10.8 %collective-permute-start.37 = (f32[8,1536]{1,0:T(8,128)S(1)}, f32[8,1536]{1,0:T(8,128)S(1)}, u32[]{:S(2)}, u32[]{:S(2)}) collective-permute-start(f32[8,1536]{1,0:T(8,128)S(1)} %get-tuple-element.102), channel_id=1, source_target_pairs={{0,126},{1,127},{2,124},{3,125},{4,122},{5,123},{6,120},{7,121},{8... | collective-permute-start | bytes 147464 | tf_op jit(solution)/shard_map/ppermute | solution.py:57
  219.0 10.6 %collective-permute-start.39 = (f32[8,1536]{1,0:T(8,128)S(1)}, f32[8,1536]{1,0:T(8,128)S(1)}, u32[]{:S(2)}, u32[]{:S(2)}) collective-permute-start(f32[8,1536]{1,0:T(8,128)S(1)} %get-tuple-element.104), channel_id=1, source_target_pairs={{0,84},{1,85},{2,86},{3,87},{4,80},{5,81},{6,82},{7,83},{8,92},{9,... | collective-permute-start | bytes 147464 | tf_op jit(solution)/shard_map/ppermute | solution.py:57
  (32 other events, 351.4 us)
where the time goes:
time: 232 us; the launch traced here: 230 us
  waiting for transfers between devices  101 us (44%)
  starting transfers between devices  71.6 us (31%)
  Pallas kernels  47.6 us (21%)
  local copies, waits for them, and re-layouts  9.09 us (4%)
    ppermute x39, waiting for transfers between devices, sent(): return lax.ppermute(value, ALL, PARTNERS[level, step])  99.6 us
    ppermute x39, starting transfers between devices, sent(): return lax.ppermute(value, ALL, PARTNERS[level, step])  71.5 us
    pallas_call x15, Pallas kernels, call(): pl.pallas_call(body, out_shape=list(outs), in_specs=specs, out_specs=[pl....  17.4 us
    pallas_call x1, Pallas kernels, ortho_back(): pl.pallas_call(ortho_back_body, grid=(3,), in_specs=[SMEM, *QUARTERS, one...  15.8 us
    pallas_call x1, Pallas kernels, ortho(): pl.pallas_call(ortho_body, grid=(3,), in_specs=[SMEM, *QUARTERS, WHOLE, W...  14.4 us
    unnamed x32, local copies, waits for them, and re-layouts  8.31 us
  transfers between devices with their start and end apart: 40, of which 34 were waited for; matrix products, arithmetic and copies ran while one was open for 0% of the time, Pallas kernels for 0%

commit v1 on v0

v1 whole, which is shorter than its diff:
```python
import jax
import jax.numpy as jnp
from jax import lax
from jax.experimental import pallas as pl
from jax.experimental.pallas import tpu as pltpu
from jax.sharding import Mesh
from jax.sharding import PartitionSpec as P

TOK = ("tok_0", "tok_1", "tok_2")
ALL = TOK + ("head",)
NS_STEPS = 3
DH = 512
WIDE = 3 * DH
BF = jnp.bfloat16
F32 = jnp.float32
coef_first = 3.4445
coef_second = -4.775
coef_third = 2.0315
inner_step = 0.5
VMEM_BYTES = 24 * 1024 * 1024


def flat_at(x, y, z, c):
    return ((x * 4 + y) * 4 + z) * 2 + c


def links(move):
    out = []
    for x in range(4):
        for y in range(4):
            for z in range(4):
                for c in range(2):
                    out.append((flat_at(x, y, z, c), flat_at(*move(x, y, z, c))))
    return out


def pair(i, near):
    return i ^ 1 if near else 3 - i


def partner_links(level, step):
    axis = 3 - step

    def move(x, y, z, c):
        at = [x, y, z]
        at[axis] = pair(at[axis], (level == 1) != (c == 1))
        return (*at, c)

    return links(move)


def antipode_links(level):
    def move(x, y, z, c):
        near = (level == 1) != (c == 1)
        return (pair(x, near), pair(y, near), pair(z, near), c)

    return links(move)


PARTNERS = {(level, step): partner_links(level, step) for level in (1, 2) for step in (1, 2, 3)}
ANTIPODES = {level: antipode_links(level) for level in (1, 2)}
OTHER_CORE = links(lambda x, y, z, c: (x, y, z, 1 - c))


def colour(bit, x, y, z):
    code = bit(x) * 4 + bit(y) * 2 + bit(z)
    return jnp.where(code >= 4, 7 - code, code)


def own_colours():
    x, y, z = (lax.axis_index(a) for a in TOK)
    core = lax.axis_index("head")
    low = colour(lambda i: ((i + 1) // 2) % 2, x, y, z)
    high = colour(lambda i: i // 2, x, y, z)
    first = jnp.where(core == 0, low, high)
    second = jnp.where(core == 0, high, low)
    token = (x * 4 + y) * 4 + z
    return jnp.stack([first, second, token]).astype(jnp.int32)


SMEM = pl.BlockSpec(memory_space=pltpu.SMEM)
VMEM = pl.BlockSpec(memory_space=pltpu.VMEM)
HBM = pl.BlockSpec(memory_space=pl.ANY)


def call(body, outs, *args, scratch=(), scalars=None, flops=0, specs=None, limit=VMEM_BYTES):
    specs = specs or [VMEM] * len(args)
    if scalars is not None:
        specs = [SMEM] + specs
        args = (scalars, *args)
    moved = sum(a.size * a.dtype.itemsize for a in args) + sum(
        o.size * o.dtype.itemsize for o in outs
    )
    return pl.pallas_call(
        body,
        out_shape=list(outs),
        in_specs=specs,
        out_specs=[VMEM] * len(outs),
        scratch_shapes=list(scratch),
        compiler_params=pltpu.CompilerParams(vmem_limit_bytes=limit),
        cost_estimate=pl.CostEstimate(flops=flops, bytes_accessed=moved, transcendentals=0),
    )(*args)


def shape(*dims, dtype=F32):
    return jax.ShapeDtypeStruct(dims, dtype)


def nn(a, b):
    return jnp.dot(a, b, preferred_element_type=F32)


def nt(a, b):
    return lax.dot_general(a, b, (((1,), (1,)), ((), ())), preferred_element_type=F32)


def tn(a, b):
    return lax.dot_general(a, b, (((0,), (0,)), ((), ())), preferred_element_type=F32)


def rows_at(index, rows):
    return pl.ds(pl.multiple_of(index * rows, rows), rows)


def hand_out(own, whole, outs, rows):
    for step in range(4):
        outs[step][...] = whole[rows_at(own ^ step, rows), :]


def fold_body(own, a, b, c, d, *outs):
    rows = outs[0].shape[0]
    for step in range(4):
        at = rows_at(own[1] ^ step, rows)
        outs[step][...] = (a[at, :] + b[at, :]) + (c[at, :] + d[at, :])


def total_body(*refs):
    *parts, out = refs
    values = [part[...] for part in parts]
    while len(values) > 1:
        values = [values[i] + values[i + 1] for i in range(0, len(values), 2)]
    out[...] = values[0]


def join_body(own, a, b, c, d, out):
    rows = a.shape[0]
    for step, piece in enumerate((a, b, c, d)):
        out[rows_at(own[1] ^ step, rows), :] = piece[...]


def received(blocks, level):
    return [blocks[0]] + [
        lax.ppermute(blocks[step], ALL, PARTNERS[level, step]) for step in (1, 2, 3)
    ]


def sum_everywhere(blocks, own):
    piece_shape = [shape(32, WIDE)]
    blocks = received(blocks, 1)
    blocks = call(fold_body, piece_shape * 4, *blocks, scalars=own)
    (piece,) = call(total_body, piece_shape, *received(blocks, 2))
    for level in (1, 2):
        arrived = lax.ppermute(piece, ALL, ANTIPODES[level])
        (piece,) = call(total_body, piece_shape, piece, arrived)
    (piece,) = call(join_body, [shape(128, WIDE)], *received([piece] * 4, 2), scalars=own)
    return received([piece] * 4, 1)


def silu_parts(pre_gate):
    sigma_gate = jax.nn.sigmoid(pre_gate)
    act_gate = pre_gate * sigma_gate
    slope_gate = sigma_gate * (1.0 + pre_gate * (1.0 - sigma_gate))
    return (act_gate, slope_gate, sigma_gate)


def as_column(row):
    return jnp.transpose(jnp.broadcast_to(row, (128, row.shape[1])))[:, :1]


def key_body(own, rates, *refs):
    sources, outs, stored = refs[:5], refs[5:9], refs[9:16]
    whole, copies, sems = refs[16], refs[17:22], refs[22]
    gate, up, mid, mixed, target, dgate, dup = stored
    moves = [
        pltpu.make_async_copy(source, copy, sems.at[i])
        for i, (source, copy) in enumerate(zip(sources, copies))
    ]
    for move in moves:
        move.start()
    keys, w_gate, w_up, values, w_down = copies
    moves[0].wait()
    moves[1].wait()
    k = keys[...]
    g = nn(k, w_gate[...])
    gate[...] = g
    moves[2].wait()
    u = nn(k, w_up[...])
    up[...] = u
    act, slope, _ = silu_parts(g)
    mix = (act * u).astype(BF)
    mixed[...] = mix
    moves[3].wait()
    t = (-as_column(rates[...]) * values[...].astype(F32)).astype(BF)
    target[...] = t
    whole[:, 2 * DH :] = tn(mix, t)
    moves[4].wait()
    m = nt(t, w_down[...])
    mid[...] = m
    dg = (m * u * slope).astype(BF)
    du = (m * act).astype(BF)
    dgate[...] = dg
    dup[...] = du
    whole[:, :DH] = tn(k, dg)
    whole[:, DH : 2 * DH] = tn(k, du)
    hand_out(own[0], whole, outs, DH // 4)


def query_forward(new, queries, cotangent, gain, stats, output, act_out, slope_out, mixed):
    q = queries[...]
    g = nn(q, new[0])
    u = nn(q, new[1])
    act, slope, _ = silu_parts(g)
    mix = (act * u).astype(BF)
    out = nn(mix, new[2])
    squares = jnp.sum(out * out, axis=1, keepdims=True)
    aligned = jnp.sum(cotangent[...].astype(F32) * gain[...] * out, axis=1, keepdims=True)
    lane = lax.broadcasted_iota(jnp.int32, stats.shape, 1)
    stats[...] = jnp.where(lane == 0, squares, aligned)
    output[...] = out
    act_out[...] = act
    slope_out[...] = u * slope
    mixed[...] = mix


def query_terms_body(
    own, w_down, queries, cotangent, gain, stats, other, output, act, slope, mixed, *refs
):
    outs, dgate, dup, whole = refs[:4], refs[4], refs[5], refs[6]
    both = stats[...] + other[...]
    inverse_rms = lax.rsqrt(both[:, :1] / (2 * DH) + 1e-05)
    aligned = both[:, 1:2]
    grad_output = (
        gain[...] * cotangent[...].astype(F32) * inverse_rms
        - output[...] * (aligned * inverse_rms * inverse_rms * inverse_rms / (2 * DH))
    ).astype(BF)
    mid = nt(grad_output, w_down[2])
    dg = (mid * slope[...]).astype(BF)
    du = (mid * act[...]).astype(BF)
    dgate[...] = dg
    dup[...] = du
    q = queries[...]
    whole[:, 2 * DH :] = tn(mixed[...], grad_output)
    whole[:, :DH] = tn(q, dg)
    whole[:, DH : 2 * DH] = tn(q, du)
    hand_out(own[0], whole, outs, DH // 4)


def query_grad_body(new, dgate, dup, query_grad):
    query_grad[...] = (nt(dgate[...], new[0]) + nt(dup[...], new[1])).astype(BF)


def key_terms(cots, keys, gate, up, mid, target, terms, back_mid, gate_back, up_back):
    k = keys[...]
    t = target[...]
    back_gate = nn(k, cots[0])
    back_up = nn(k, cots[1])
    back_mixed = nt(t, cots[2])
    g = gate[...]
    u = up[...]
    m = mid[...]
    act, slope, sigma = silu_parts(g)
    curve = sigma * (1.0 - sigma) * (2.0 + g * (1.0 - 2.0 * sigma))
    bm = (back_gate * u * slope + back_up * act).astype(BF)
    gb = (back_gate * m * u * curve + back_up * m * slope + back_mixed * u * slope).astype(BF)
    ub = (back_gate * m * slope + back_mixed * act).astype(BF)
    back_mid[...] = bm
    gate_back[...] = gb
    up_back[...] = ub
    terms[:, :DH] = tn(k, gb)
    terms[:, DH : 2 * DH] = tn(k, ub)
    terms[:, 2 * DH :] = tn(bm, t)


def key_grads_body(
    cots, w_gate, w_up, w_down, rates, mixed, dgate, dup, back_mid, gate_back, up_back, *outs
):
    key_grad, value_grad = outs
    key_grad[...] = (
        nt(dgate[...], cots[0])
        + nt(dup[...], cots[1])
        + nt(gate_back[...], w_gate[...])
        + nt(up_back[...], w_up[...])
    ).astype(BF)
    value_sum = nn(mixed[...], cots[2]) + nn(back_mid[...], w_down[...])
    value_grad[...] = (-as_column(rates[...]) * value_sum).astype(BF)


SHARE_STEPS = 4


def share_body(share, pieces, out_a, out_b, out_c, total):
    step = pl.program_id(0)

    @pl.when(step == 0)
    def _():
        total[...] = share[...]

    total[...] += jnp.sum(pieces[...], axis=0)

    @pl.when(step == SHARE_STEPS - 1)
    def _():
        out_a[0] = total[:, :DH]
        out_b[0] = total[:, DH : 2 * DH]
        out_c[0] = total[:, 2 * DH :]


def weight_shares(share, pieces):
    out = pl.BlockSpec((1, 8, DH), lambda i: (0, 0, 0))
    return pl.pallas_call(
        share_body,
        grid=(SHARE_STEPS,),
        in_specs=[
            pl.BlockSpec((8, WIDE), lambda i: (0, 0)),
            pl.BlockSpec((pieces.shape[0] // SHARE_STEPS, 8, WIDE), lambda i: (i, 0, 0)),
        ],
        out_specs=[out] * 3,
        out_shape=[shape(1, 8, DH)] * 3,
        scratch_shapes=[pltpu.VMEM((8, WIDE), F32)],
        compiler_params=pltpu.CompilerParams(vmem_limit_bytes=VMEM_BYTES),
    )(share, pieces)


EACH = range(3)


def columns(index):
    return slice(index * DH, (index + 1) * DH)


def ortho_body(own, a, b, c, d, w_gate, w_up, w_down, queries, cotangent, gain, *refs):
    new, kept, norm, query_refs, (current, gram) = refs[0], refs[1], refs[2], refs[3:8], refs[8:]
    for step, block in enumerate((a, b, c, d)):
        for i in EACH:
            current[i, rows_at(own[0] ^ step, DH // 4), :] = block[:, columns(i)]
    for i in EACH:
        matrix = current[i]
        root = jnp.sqrt(jnp.sum(matrix * matrix, keepdims=True) + 1e-06)
        norm[i] = jnp.broadcast_to(root, norm.shape[1:])
        unit = matrix * (1.0 / root)
        current[i] = unit
        kept[i, 0] = unit.astype(BF)
    for step in range(NS_STEPS):
        for i in EACH:
            narrow = kept[i, 3 * step]
            square = nt(narrow, narrow)
            gram[i] = square
            kept[i, 3 * step + 1] = square.astype(BF)
        for i in EACH:
            low = kept[i, 3 * step + 1]
            kept[i, 3 * step + 2] = (coef_second * gram[i] + coef_third * nn(low, low)).astype(BF)
        for i, weight in enumerate((w_gate, w_up, w_down)):
            later = coef_first * current[i] + nn(kept[i, 3 * step + 2], kept[i, 3 * step])
            if step < NS_STEPS - 1:
                current[i] = later
                kept[i, 3 * step + 3] = later.astype(BF)
            else:
                new[i] = (weight[...].astype(F32) - inner_step * later).astype(BF)
    query_forward(new, queries, cotangent, gain, *query_refs)


def ortho_back_body(own, a, b, c, d, kept, norm, keys, gate, up, mid, target, *refs):
    cots, share, terms, key_refs, (grad, grad_low, half, sym) = (
        refs[0],
        refs[1],
        refs[2],
        refs[3:6],
        refs[6:],
    )
    for step, block in enumerate((a, b, c, d)):
        for i in EACH:
            grad[i, rows_at(own[0] ^ step, DH // 4), :] = block[:, columns(i)]
    for i in EACH:
        share[:, columns(i)] = grad[i, rows_at(own[2], 8), :]
        start = grad[i] * (-inner_step)
        grad[i] = start
        grad_low[i] = start.astype(BF)
    for step in reversed(range(NS_STEPS)):
        for i in EACH:
            half[i] = nt(grad_low[i], kept[i, 3 * step])
        for i in EACH:
            both = half[i] + jnp.transpose(half[i])
            sym[i] = both.astype(BF)
        for i in EACH:
            half[i] = coef_third * nn(sym[i], kept[i, 3 * step + 1])
        for i in EACH:
            full = coef_second * sym[i].astype(F32) + (half[i] + jnp.transpose(half[i]))
            sym[i] = full.astype(BF)
        for i in EACH:
            later = (
                coef_first * grad[i]
                + nn(kept[i, 3 * step + 2], grad_low[i])
                + nn(sym[i], kept[i, 3 * step])
            )
            grad[i] = later
            if step > 0:
                grad_low[i] = later.astype(BF)
    for i in EACH:
        unit = kept[i, 0].astype(F32)
        along = jnp.sum(grad[i] * unit, keepdims=True)
        cots[i] = ((grad[i] - unit * along) * (1.0 / norm[i, :1, :1])).astype(BF)
    key_terms(cots, keys, gate, up, mid, target, terms, *key_refs)


def local(queries, key_rows, value_rows, step_rates, w_gate, w_up, w_down, out_gain, cotangent):
    tokens = queries.shape[1]
    queries, key_rows, value_rows, cotangent = (
        a[0] for a in (queries, key_rows, value_rows, cotangent)
    )
    w_gate, w_up, w_down = w_gate[0], w_up[0], w_down[0]
    own = own_colours()

    whole = pltpu.VMEM((DH, WIDE), F32)
    quarters = [shape(DH // 4, WIDE)] * 4
    wide = shape(tokens, DH)
    low = shape(tokens, DH, dtype=BF)
    three = shape(3, DH, DH, dtype=BF)
    three_f32 = pltpu.VMEM((3, DH, DH), F32)
    three_low = pltpu.VMEM((3, DH, DH), BF)
    token_low = pltpu.VMEM((tokens, DH), BF)
    square_low = pltpu.VMEM((DH, DH), BF)
    *blocks, gate, up, mid, mixed, target, dgate, dup = call(
        key_body,
        [*quarters, wide, wide, wide, low, low, low, low],
        step_rates,
        key_rows,
        w_gate,
        w_up,
        value_rows,
        w_down,
        scratch=[
            whole,
            token_low,
            square_low,
            square_low,
            token_low,
            square_low,
            pltpu.SemaphoreType.DMA((5,)),
        ],
        scalars=own,
        specs=[VMEM] + [HBM] * 5,
    )
    new, kept, norm, stats, *query_stored = call(
        ortho_body,
        [
            three,
            shape(3, 9, DH, DH, dtype=BF),
            shape(3, 8, 128),
            shape(tokens, 128),
            wide,
            wide,
            wide,
            low,
        ],
        *sum_everywhere(blocks, own),
        w_gate,
        w_up,
        w_down,
        queries,
        cotangent,
        out_gain,
        scalars=own,
        scratch=[three_f32, three_f32],
    )
    other = lax.ppermute(stats, ALL, OTHER_CORE)
    *blocks, query_dgate, query_dup = call(
        query_terms_body,
        [*quarters, low, low],
        new,
        queries,
        cotangent,
        out_gain,
        stats,
        other,
        *query_stored,
        scratch=[whole],
        scalars=own,
    )
    (query_grad,) = call(
        query_grad_body, [low], new, query_dgate, query_dup, flops=4 * tokens * DH * DH
    )
    cots, share, terms, back_mid, gate_back, up_back = call(
        ortho_back_body,
        [three, shape(8, WIDE), shape(DH, WIDE), low, low, low],
        *sum_everywhere(blocks, own),
        kept,
        norm,
        key_rows,
        gate,
        up,
        mid,
        target,
        scalars=own,
        scratch=[three_f32, three_low, three_f32, three_low],
    )
    devices = lax.axis_size(TOK)
    pieces = lax.all_to_all(
        terms.reshape(devices, DH // devices, WIDE), TOK, 0, 0, tiled=True
    )
    key_grad, value_grad = call(
        key_grads_body,
        [low, low],
        cots,
        w_gate,
        w_up,
        w_down,
        step_rates,
        mixed,
        dgate,
        dup,
        back_mid,
        gate_back,
        up_back,
        flops=12 * tokens * DH * DH,
    )
    grads = weight_shares(share, pieces)
    return (query_grad[None], key_grad[None], value_grad[None], *grads)


def solution(mesh):
    split = Mesh(
        mesh.devices.reshape(4, 4, 4, mesh.shape["head"]), ("tok_0", "tok_1", "tok_2", "head")
    )
    rows = P("head", TOK, None)
    weight = P("head", None, None)
    in_specs = (
        rows,
        rows,
        rows,
        P("head", TOK),
        weight,
        weight,
        weight,
        P("head", None),
        rows,
    )
    return jax.shard_map(
        local, mesh=split, in_specs=in_specs, out_specs=(rows,) * 6, check_vma=False
    )
```

time: 232 us -> 225 us (0.970)
  starting transfers between devices: 71.6 us -> 49.1 us
  waiting for transfers between devices: 101 us -> 116 us
  Pallas kernels: 47.6 us -> 34.3 us
  local copies, waits for them, and re-layouts: 9.09 us -> 22.1 us
    ppermute x40 -> x29, starting transfers between devices: 71.6 us -> 37.5 us  [the longest x24 29.6 us: received(): lax.ppermute(blocks[step], ALL, PARTNERS[level, step])]
    all_to_all x0 -> x1, waiting for transfers between devices: none -> 15.1 us  [local(): lax.all_to_all(terms.reshape(devices, DH // devices, WIDE), TOK, 0, 0, ti...]
    unnamed x32 -> x72, local copies, waits for them, and re-layouts: 8.31 us -> 22.1 us
    pallas_call x17, Pallas kernels: 47.6 us -> 34.3 us  [the longest x16 33.5 us: call(): pl.pallas_call(body, out_shape=list(outs), in_specs=specs, out_specs=[VME...]
    all_to_all x0 -> x1, starting transfers between devices: none -> 11.5 us  [local(): lax.all_to_all(terms.reshape(devices, DH // devices, WIDE), TOK, 0, 0, ti...]
    ppermute x40 -> x29, waiting for transfers between devices: 101 us -> 101 us  [the longest x24 69.9 us: received(): lax.ppermute(blocks[step], ALL, PARTNERS[level, step])]
  transfers between devices with their start and end apart: 40 -> 30, of which waited for: 34 -> 29; matrix products, arithmetic and copies ran while one was open for 0% -> 0% of each run, Pallas kernels for 0% -> 1%
where the time goes in v1:
time: 225 us; the launch traced here: 223 us
  waiting for transfers between devices  116 us (52%)
  starting transfers between devices  49.1 us (22%)
  Pallas kernels  34.3 us (15%)
  local copies, waits for them, and re-layouts  22.1 us (10%)
    ppermute x24, waiting for transfers between devices, received(): lax.ppermute(blocks[step], ALL, PARTNERS[level, step])  69.9 us
    pallas_call x16, Pallas kernels, call(): pl.pallas_call(body, out_shape=list(outs), in_specs=specs, out_specs=[VME...  33.5 us
    ppermute x24, starting transfers between devices, received(): lax.ppermute(blocks[step], ALL, PARTNERS[level, step])  29.6 us
    ppermute x4, waiting for transfers between devices, sum_everywhere(): arrived = lax.ppermute(piece, ALL, ANTIPODES[level])  29.6 us
    unnamed x72, local copies, waits for them, and re-layouts  22.1 us
    all_to_all x1, waiting for transfers between devices, local(): lax.all_to_all(terms.reshape(devices, DH // devices, WIDE), TOK, 0, 0, ti...  15.1 us
    all_to_all x1, starting transfers between devices, local(): lax.all_to_all(terms.reshape(devices, DH // devices, WIDE), TOK, 0, 0, ti...  11.5 us
    ppermute x4, starting transfers between devices, sum_everywhere(): arrived = lax.ppermute(piece, ALL, ANTIPODES[level])  7.83 us
  transfers between devices with their start and end apart: 30, of which 29 were waited for; matrix products, arithmetic and copies ran while one was open for 0% of the time, Pallas kernels for 1%

profile of v1, /device:TPU:0, one launch (start us, length us, event | category | flops | bytes accessed | tf_op | source)
XLA Modules:
  0.0 222.6 jit_solution(16095208397848900511)
XLA Ops:
  6.5 2.9 %shard_map.136 = (f32[128,1536]{1,0:T(8,128)S(1)}, f32[128,1536]{1,0:T(8,128)S(1)}, f32[128,1536]{1,0:T(8,128)S(1)}, f32[128,1536]{1,0:T(8,128)S(1)}, f32[256,51...) custom-call(s32[3]{0:T(128)S(1)} %pad_add_fusion.own, ...), custom_call_target="tpu_custom_call" | custom-call | bytes 7865356 | tf_op jit(solution)/shard_map/pallas_call | solution.py:94
  14.6 6.9 %collective-permute-done.b = f32[128,1536]{1,0:T(8,128)S(1)} collective-permute-done((f32[128,1536]{1,0:T(8,128)S(1)}, f32[128,1536]{1,0:T(8,128)S(1)}, u32[]{:S(2)}, u32[]{:S(2)}) %collective-permute-start) | collective-permute-done | bytes 786464 | tf_op jit(solution)/shard_map/ppermute | solution.py:153
  25.8 2.6 %collective-permute-start.3 = (f32[32,1536]{1,0:T(8,128)S(1)}, f32[32,1536]{1,0:T(8,128)S(1)}, u32[]{:S(2)}, u32[]{:S(2)}) collective-permute-start(f32[32,1536]{1,0:T(8,128)S(1)} %get-tuple-element.55), channel_id=1, source_target_pairs={{0,6},{1,3},{2,4},{3,1},{4,2},{5,7},{6,0},{7,5},{8,14},{9,11},{10,... | collective-permute-start | bytes 589832 | tf_op jit(solution)/shard_map/ppermute | solution.py:153
  30.6 2.8 %collective-permute-start.5 = (f32[32,1536]{1,0:T(8,128)S(1)}, f32[32,1536]{1,0:T(8,128)S(1)}, u32[]{:S(2)}, u32[]{:S(2)}) collective-permute-start(f32[32,1536]{1,0:T(8,128)S(1)} %get-tuple-element.57), channel_id=1, source_target_pairs={{0,96},{1,33},{2,98},{3,35},{4,100},{5,37},{6,102},{7,39},{8,104},... | collective-permute-start | bytes 589832 | tf_op jit(solution)/shard_map/ppermute | solution.py:153
  38.5 6.6 %collective-permute-done.6.refs_1_ = f32[32,1536]{1,0:T(8,128)S(1)} collective-permute-done((f32[32,1536]{1,0:T(8,128)S(1)}, f32[32,1536]{1,0:T(8,128)S(1)}, u32[]{:S(2)}, u32[]{:S(2)}) %collective-permute-start.6) | collective-permute-done | bytes 196640 | tf_op jit(solution)/shard_map/ppermute | solution.py:163
  45.1 3.5 %collective-permute-start.7 = (f32[32,1536]{1,0:T(8,128)S(1)}, f32[32,1536]{1,0:T(8,128)S(1)}, u32[]{:S(2)}, u32[]{:S(2)}) collective-permute-start(f32[32,1536]{1,0:T(8,128)S(1)} %shard_map.139.refs_0_), channel_id=1, source_target_pairs={{0,126},{1,43},{2,124},{3,41},{4,122},{5,47},{6,120},{7,45},{8,118... | collective-permute-start | bytes 589832 | tf_op jit(solution)/shard_map/ppermute | solution.py:163
  48.6 7.7 %collective-permute-done.7.refs_1_ = f32[32,1536]{1,0:T(8,128)S(1)} collective-permute-done((f32[32,1536]{1,0:T(8,128)S(1)}, f32[32,1536]{1,0:T(8,128)S(1)}, u32[]{:S(2)}, u32[]{:S(2)}) %collective-permute-start.7) | collective-permute-done | bytes 196640 | tf_op jit(solution)/shard_map/ppermute | solution.py:163
  56.3 2.8 %collective-permute-start.10 = (f32[32,1536]{1,0:T(8,128)S(1)}, f32[32,1536]{1,0:T(8,128)S(1)}, u32[]{:S(2)}, u32[]{:S(2)}) collective-permute-start(f32[32,1536]{1,0:T(8,128)S(1)} %shard_map.140.a), channel_id=1, source_target_pairs={{0,96},{1,33},{2,98},{3,35},{4,100},{5,37},{6,102},{7,39},{8,104},... | collective-permute-start | bytes 589832 | tf_op jit(solution)/shard_map/ppermute | solution.py:153
  60.9 4.5 %collective-permute-done.10.d = f32[32,1536]{1,0:T(8,128)S(1)} collective-permute-done((f32[32,1536]{1,0:T(8,128)S(1)}, f32[32,1536]{1,0:T(8,128)S(1)}, u32[]{:S(2)}, u32[]{:S(2)}) %collective-permute-start.10) | collective-permute-done | bytes 196640 | tf_op jit(solution)/shard_map/ppermute | solution.py:153
  65.4 2.8 %collective-permute-done.9.c = f32[32,1536]{1,0:T(8,128)S(1)} collective-permute-done((f32[32,1536]{1,0:T(8,128)S(1)}, f32[32,1536]{1,0:T(8,128)S(1)}, u32[]{:S(2)}, u32[]{:S(2)}) %collective-permute-start.9) | collective-permute-done | bytes 196640 | tf_op jit(solution)/shard_map/ppermute | solution.py:153
  70.4 11.6 %collective-permute-done.13.d = f32[128,1536]{1,0:T(8,128)S(1)} collective-permute-done((f32[128,1536]{1,0:T(8,128)S(1)}, f32[128,1536]{1,0:T(8,128)S(1)}, u32[]{:S(2)}, u32[]{:S(2)}) %collective-permute-start.13) | collective-permute-done | bytes 786464 | tf_op jit(solution)/shard_map/ppermute | solution.py:153
  82.4 10.1 %shard_map.142 = (bf16[3,512,512]{2,1,0:T(8,128)(2,1)S(1)}, bf16[3,9,512,512]{3,2,1,0:T(8,128)(2,1)S(1)}, f32[3,8,128]{2,1,0:T(8,128)S(1)}, f32[256,128]{1,0:T(8...) custom-call(s32[3]{0:T(128)S(1)} %pad_add_fusion.own, ...), custom_call_target="tpu_custom_call" | custom-call | bytes 22951948 | tf_op jit(solution)/shard_map/pallas_call | solution.py:94
  99.4 8.2 %collective-permute-done.15.b = f32[128,1536]{1,0:T(8,128)S(1)} collective-permute-done((f32[128,1536]{1,0:T(8,128)S(1)}, f32[128,1536]{1,0:T(8,128)S(1)}, u32[]{:S(2)}, u32[]{:S(2)}) %collective-permute-start.15) | collective-permute-done | bytes 786464 | tf_op jit(solution)/shard_map/ppermute | solution.py:153
  111.0 2.2 collective-permute-start.19
  113.6 3.5 %collective-permute-done.18.refs_1_ = f32[32,1536]{1,0:T(8,128)S(1)} collective-permute-done((f32[32,1536]{1,0:T(8,128)S(1)}, f32[32,1536]{1,0:T(8,128)S(1)}, u32[]{:S(2)}, u32[]{:S(2)}) %collective-permute-start.18) | collective-permute-done | bytes 196640 | tf_op jit(solution)/shard_map/ppermute | solution.py:153
  120.5 7.1 %collective-permute-done.21.refs_1_ = f32[32,1536]{1,0:T(8,128)S(1)} collective-permute-done((f32[32,1536]{1,0:T(8,128)S(1)}, f32[32,1536]{1,0:T(8,128)S(1)}, u32[]{:S(2)}, u32[]{:S(2)}) %collective-permute-start.21) | collective-permute-done | bytes 196640 | tf_op jit(solution)/shard_map/ppermute | solution.py:163
  127.6 3.0 %collective-permute-start.22 = (f32[32,1536]{1,0:T(8,128)S(1)}, f32[32,1536]{1,0:T(8,128)S(1)}, u32[]{:S(2)}, u32[]{:S(2)}) collective-permute-start(f32[32,1536]{1,0:T(8,128)S(1)} %shard_map.147.refs_0_), channel_id=1, source_target_pairs={{0,126},{1,43},{2,124},{3,41},{4,122},{5,47},{6,120},{7,45},{8,118... | collective-permute-start | bytes 589832 | tf_op jit(solution)/shard_map/ppermute | solution.py:163
  130.6 8.2 %collective-permute-done.22.refs_1_ = f32[32,1536]{1,0:T(8,128)S(1)} collective-permute-done((f32[32,1536]{1,0:T(8,128)S(1)}, f32[32,1536]{1,0:T(8,128)S(1)}, u32[]{:S(2)}, u32[]{:S(2)}) %collective-permute-start.22) | collective-permute-done | bytes 196640 | tf_op jit(solution)/shard_map/ppermute | solution.py:163
  140.7 2.5 %collective-permute-start.23 = (f32[32,1536]{1,0:T(8,128)S(1)}, f32[32,1536]{1,0:T(8,128)S(1)}, u32[]{:S(2)}, u32[]{:S(2)}) collective-permute-start(f32[32,1536]{1,0:T(8,128)S(1)} %shard_map.148.a), channel_id=1, source_target_pairs={{0,6},{1,3},{2,4},{3,1},{4,2},{5,7},{6,0},{7,5},{8,14},{9,11},{10,... | collective-permute-start | bytes 589832 | tf_op jit(solution)/shard_map/ppermute | solution.py:153
  143.2 4.9 %collective-permute-done.25.d = f32[32,1536]{1,0:T(8,128)S(1)} collective-permute-done((f32[32,1536]{1,0:T(8,128)S(1)}, f32[32,1536]{1,0:T(8,128)S(1)}, u32[]{:S(2)}, u32[]{:S(2)}) %collective-permute-start.25) | collective-permute-done | bytes 196640 | tf_op jit(solution)/shard_map/ppermute | solution.py:153
  150.6 11.8 %collective-permute-done.28.d = f32[128,1536]{1,0:T(8,128)S(1)} collective-permute-done((f32[128,1536]{1,0:T(8,128)S(1)}, f32[128,1536]{1,0:T(8,128)S(1)}, u32[]{:S(2)}, u32[]{:S(2)}) %collective-permute-start.28) | collective-permute-done | bytes 786464 | tf_op jit(solution)/shard_map/ppermute | solution.py:153
  162.6 13.2 %shard_map.150 = (bf16[3,512,512]{2,1,0:T(8,128)(2,1)S(1)}, f32[8,1536]{1,0:T(8,128)S(1)}, f32[512,1536]{1,0:T(8,128)S(1)}, bf16[256,512]{1,0:T(8,128)(2,1)S(1)}...) custom-call(s32[3]{0:T(128)S(1)} %pad_add_fusion.own, f32[128,1536]{1,0:T(8,128)S(1)} %shard_map.149.a, ...), custom_call_target="tpu_custom_call" | custom-call | bytes 24965132 | tf_op jit(solution)/shard_map/pallas_call | solution.py:94
  180.8 11.5 %all-to-all-start = ((f32[64,8,1536]{2,1,0:T(8,128)}), f32[64,8,1536]{2,1,0:T(8,128)S(1)}, u32[]{:S(2)}, u32[]{:S(2)}) async-start(f32[64,8,1536]{2,1,0:T(8,128)} %bitcast.23), calls=%async_computation | async-start | bytes 6291456 | tf_op jit(solution)/shard_map/all_to_all | solution.py:506
  206.6 15.1 %all-to-all-done.pieces = f32[64,8,1536]{2,1,0:T(8,128)S(1)} async-done(((f32[64,8,1536]{2,1,0:T(8,128)}), f32[64,8,1536]{2,1,0:T(8,128)S(1)}, u32[]{:S(2)}, u32[]{:S(2)}) %all-to-all-start) | async-done | bytes 3145760 | tf_op jit(solution)/shard_map/all_to_all | solution.py:506
  (126 shorter events, 65.5 us)
Async XLA Ops:
  9.5 12.1 %collective-permute-start = (f32[128,1536]{1,0:T(8,128)S(1)}, f32[128,1536]{1,0:T(8,128)S(1)}, u32[]{:S(2)}, u32[]{:S(2)}) collective-permute-start(f32[128,1536]{1,0:T(8,128)S(1)} %get-tuple-element.51), channel_id=1, source_target_pairs={{0,2},{1,7},{2,0},{3,5},{4,6},{5,3},{6,4},{7,1},{8,10},{9,15},{10,... | collective-permute-start | bytes 2359304 | tf_op jit(solution)/shard_map/ppermute | solution.py:153
  11.5 12.0 %collective-permute-start.1 = (f32[128,1536]{1,0:T(8,128)S(1)}, f32[128,1536]{1,0:T(8,128)S(1)}, u32[]{:S(2)}, u32[]{:S(2)}) collective-permute-start(f32[128,1536]{1,0:T(8,128)S(1)} %get-tuple-element.52), channel_id=1, source_target_pairs={{0,8},{1,25},{2,10},{3,27},{4,12},{5,29},{6,14},{7,31},{8,0},{9,17... | collective-permute-start | bytes 2359304 | tf_op jit(solution)/shard_map/ppermute | solution.py:153
  13.1 12.0 %collective-permute-start.2 = (f32[128,1536]{1,0:T(8,128)S(1)}, f32[128,1536]{1,0:T(8,128)S(1)}, u32[]{:S(2)}, u32[]{:S(2)}) collective-permute-start(f32[128,1536]{1,0:T(8,128)S(1)} %get-tuple-element.53), channel_id=1, source_target_pairs={{0,32},{1,97},{2,34},{3,99},{4,36},{5,101},{6,38},{7,103},{8,40},{... | collective-permute-start | bytes 2359304 | tf_op jit(solution)/shard_map/ppermute | solution.py:153
  25.8 7.5 %collective-permute-start.3 = (f32[32,1536]{1,0:T(8,128)S(1)}, f32[32,1536]{1,0:T(8,128)S(1)}, u32[]{:S(2)}, u32[]{:S(2)}) collective-permute-start(f32[32,1536]{1,0:T(8,128)S(1)} %get-tuple-element.55), channel_id=1, source_target_pairs={{0,6},{1,3},{2,4},{3,1},{4,2},{5,7},{6,0},{7,5},{8,14},{9,11},{10,... | collective-permute-start | bytes 589832 | tf_op jit(solution)/shard_map/ppermute | solution.py:153
  37.5 7.5 %collective-permute-start.6 = (f32[32,1536]{1,0:T(8,128)S(1)}, f32[32,1536]{1,0:T(8,128)S(1)}, u32[]{:S(2)}, u32[]{:S(2)}) collective-permute-start(f32[32,1536]{1,0:T(8,128)S(1)} %shard_map.138.refs_0_), channel_id=1, source_target_pairs={{0,42},{1,127},{2,40},{3,125},{4,46},{5,123},{6,44},{7,121},{8,34}... | collective-permute-start | bytes 589832 | tf_op jit(solution)/shard_map/ppermute | solution.py:163
  45.1 11.2 %collective-permute-start.7 = (f32[32,1536]{1,0:T(8,128)S(1)}, f32[32,1536]{1,0:T(8,128)S(1)}, u32[]{:S(2)}, u32[]{:S(2)}) collective-permute-start(f32[32,1536]{1,0:T(8,128)S(1)} %shard_map.139.refs_0_), channel_id=1, source_target_pairs={{0,126},{1,43},{2,124},{3,41},{4,122},{5,47},{6,120},{7,45},{8,118... | collective-permute-start | bytes 589832 | tf_op jit(solution)/shard_map/ppermute | solution.py:163
  56.3 9.1 %collective-permute-start.10 = (f32[32,1536]{1,0:T(8,128)S(1)}, f32[32,1536]{1,0:T(8,128)S(1)}, u32[]{:S(2)}, u32[]{:S(2)}) collective-permute-start(f32[32,1536]{1,0:T(8,128)S(1)} %shard_map.140.a), channel_id=1, source_target_pairs={{0,96},{1,33},{2,98},{3,35},{4,100},{5,37},{6,102},{7,39},{8,104},... | collective-permute-start | bytes 589832 | tf_op jit(solution)/shard_map/ppermute | solution.py:153
  59.2 9.0 %collective-permute-start.9 = (f32[32,1536]{1,0:T(8,128)S(1)}, f32[32,1536]{1,0:T(8,128)S(1)}, u32[]{:S(2)}, u32[]{:S(2)}) collective-permute-start(f32[32,1536]{1,0:T(8,128)S(1)} %shard_map.140.a), channel_id=1, source_target_pairs={{0,24},{1,9},{2,26},{3,11},{4,28},{5,13},{6,30},{7,15},{8,16},{9,1... | collective-permute-start | bytes 589832 | tf_op jit(solution)/shard_map/ppermute | solution.py:153
  60.2 9.1 %collective-permute-start.8 = (f32[32,1536]{1,0:T(8,128)S(1)}, f32[32,1536]{1,0:T(8,128)S(1)}, u32[]{:S(2)}, u32[]{:S(2)}) collective-permute-start(f32[32,1536]{1,0:T(8,128)S(1)} %shard_map.140.a), channel_id=1, source_target_pairs={{0,6},{1,3},{2,4},{3,1},{4,2},{5,7},{6,0},{7,5},{8,14},{9,11},{10,... | collective-permute-start | bytes 589832 | tf_op jit(solution)/shard_map/ppermute | solution.py:153
  69.9 12.1 %collective-permute-start.13 = (f32[128,1536]{1,0:T(8,128)S(1)}, f32[128,1536]{1,0:T(8,128)S(1)}, u32[]{:S(2)}, u32[]{:S(2)}) collective-permute-start(f32[128,1536]{1,0:T(8,128)S(1)} %shard_map.141.a), channel_id=1, source_target_pairs={{0,32},{1,97},{2,34},{3,99},{4,36},{5,101},{6,38},{7,103},{8,40},{... | collective-permute-start | bytes 2359304 | tf_op jit(solution)/shard_map/ppermute | solution.py:153
  70.0 12.1 %collective-permute-start.12 = (f32[128,1536]{1,0:T(8,128)S(1)}, f32[128,1536]{1,0:T(8,128)S(1)}, u32[]{:S(2)}, u32[]{:S(2)}) collective-permute-start(f32[128,1536]{1,0:T(8,128)S(1)} %shard_map.141.a), channel_id=1, source_target_pairs={{0,8},{1,25},{2,10},{3,27},{4,12},{5,29},{6,14},{7,31},{8,0},{9,17... | collective-permute-start | bytes 2359304 | tf_op jit(solution)/shard_map/ppermute | solution.py:153
  70.1 12.3 %collective-permute-start.11 = (f32[128,1536]{1,0:T(8,128)S(1)}, f32[128,1536]{1,0:T(8,128)S(1)}, u32[]{:S(2)}, u32[]{:S(2)}) collective-permute-start(f32[128,1536]{1,0:T(8,128)S(1)} %shard_map.141.a), channel_id=1, source_target_pairs={{0,2},{1,7},{2,0},{3,5},{4,6},{5,3},{6,4},{7,1},{8,10},{9,15},{10,... | collective-permute-start | bytes 2359304 | tf_op jit(solution)/shard_map/ppermute | solution.py:153
  95.5 12.1 %collective-permute-start.15 = (f32[128,1536]{1,0:T(8,128)S(1)}, f32[128,1536]{1,0:T(8,128)S(1)}, u32[]{:S(2)}, u32[]{:S(2)}) collective-permute-start(f32[128,1536]{1,0:T(8,128)S(1)} %get-tuple-element.67), channel_id=1, source_target_pairs={{0,2},{1,7},{2,0},{3,5},{4,6},{5,3},{6,4},{7,1},{8,10},{9,15},{10,... | collective-permute-start | bytes 2359304 | tf_op jit(solution)/shard_map/ppermute | solution.py:153
  95.6 12.1 %collective-permute-start.16 = (f32[128,1536]{1,0:T(8,128)S(1)}, f32[128,1536]{1,0:T(8,128)S(1)}, u32[]{:S(2)}, u32[]{:S(2)}) collective-permute-start(f32[128,1536]{1,0:T(8,128)S(1)} %get-tuple-element.68), channel_id=1, source_target_pairs={{0,8},{1,25},{2,10},{3,27},{4,12},{5,29},{6,14},{7,31},{8,0},{9,17... | collective-permute-start | bytes 2359304 | tf_op jit(solution)/shard_map/ppermute | solution.py:153
  97.5 12.0 %collective-permute-start.17 = (f32[128,1536]{1,0:T(8,128)S(1)}, f32[128,1536]{1,0:T(8,128)S(1)}, u32[]{:S(2)}, u32[]{:S(2)}) collective-permute-start(f32[128,1536]{1,0:T(8,128)S(1)} %get-tuple-element.69), channel_id=1, source_target_pairs={{0,32},{1,97},{2,34},{3,99},{4,36},{5,101},{6,38},{7,103},{8,40},{... | collective-permute-start | bytes 2359304 | tf_op jit(solution)/shard_map/ppermute | solution.py:153
  120.1 7.5 %collective-permute-start.21 = (f32[32,1536]{1,0:T(8,128)S(1)}, f32[32,1536]{1,0:T(8,128)S(1)}, u32[]{:S(2)}, u32[]{:S(2)}) collective-permute-start(f32[32,1536]{1,0:T(8,128)S(1)} %shard_map.146.refs_0_), channel_id=1, source_target_pairs={{0,42},{1,127},{2,40},{3,125},{4,46},{5,123},{6,44},{7,121},{8,34}... | collective-permute-start | bytes 589832 | tf_op jit(solution)/shard_map/ppermute | solution.py:163
  127.6 11.2 %collective-permute-start.22 = (f32[32,1536]{1,0:T(8,128)S(1)}, f32[32,1536]{1,0:T(8,128)S(1)}, u32[]{:S(2)}, u32[]{:S(2)}) collective-permute-start(f32[32,1536]{1,0:T(8,128)S(1)} %shard_map.147.refs_0_), channel_id=1, source_target_pairs={{0,126},{1,43},{2,124},{3,41},{4,122},{5,47},{6,120},{7,45},{8,118... | collective-permute-start | bytes 589832 | tf_op jit(solution)/shard_map/ppermute | solution.py:163
  138.8 9.3 %collective-permute-start.25 = (f32[32,1536]{1,0:T(8,128)S(1)}, f32[32,1536]{1,0:T(8,128)S(1)}, u32[]{:S(2)}, u32[]{:S(2)}) collective-permute-start(f32[32,1536]{1,0:T(8,128)S(1)} %shard_map.148.a), channel_id=1, source_target_pairs={{0,96},{1,33},{2,98},{3,35},{4,100},{5,37},{6,102},{7,39},{8,104},... | collective-permute-start | bytes 589832 | tf_op jit(solution)/shard_map/ppermute | solution.py:153
  139.6 9.0 %collective-permute-start.24 = (f32[32,1536]{1,0:T(8,128)S(1)}, f32[32,1536]{1,0:T(8,128)S(1)}, u32[]{:S(2)}, u32[]{:S(2)}) collective-permute-start(f32[32,1536]{1,0:T(8,128)S(1)} %shard_map.148.a), channel_id=1, source_target_pairs={{0,24},{1,9},{2,26},{3,11},{4,28},{5,13},{6,30},{7,15},{8,16},{9,1... | collective-permute-start | bytes 589832 | tf_op jit(solution)/shard_map/ppermute | solution.py:153
  140.7 9.0 %collective-permute-start.23 = (f32[32,1536]{1,0:T(8,128)S(1)}, f32[32,1536]{1,0:T(8,128)S(1)}, u32[]{:S(2)}, u32[]{:S(2)}) collective-permute-start(f32[32,1536]{1,0:T(8,128)S(1)} %shard_map.148.a), channel_id=1, source_target_pairs={{0,6},{1,3},{2,4},{3,1},{4,2},{5,7},{6,0},{7,5},{8,14},{9,11},{10,... | collective-permute-start | bytes 589832 | tf_op jit(solution)/shard_map/ppermute | solution.py:153
  150.3 12.1 %collective-permute-start.28 = (f32[128,1536]{1,0:T(8,128)S(1)}, f32[128,1536]{1,0:T(8,128)S(1)}, u32[]{:S(2)}, u32[]{:S(2)}) collective-permute-start(f32[128,1536]{1,0:T(8,128)S(1)} %shard_map.149.a), channel_id=1, source_target_pairs={{0,32},{1,97},{2,34},{3,99},{4,36},{5,101},{6,38},{7,103},{8,40},{... | collective-permute-start | bytes 2359304 | tf_op jit(solution)/shard_map/ppermute | solution.py:153
  150.4 12.1 %collective-permute-start.27 = (f32[128,1536]{1,0:T(8,128)S(1)}, f32[128,1536]{1,0:T(8,128)S(1)}, u32[]{:S(2)}, u32[]{:S(2)}) collective-permute-start(f32[128,1536]{1,0:T(8,128)S(1)} %shard_map.149.a), channel_id=1, source_target_pairs={{0,8},{1,25},{2,10},{3,27},{4,12},{5,29},{6,14},{7,31},{8,0},{9,17... | collective-permute-start | bytes 2359304 | tf_op jit(solution)/shard_map/ppermute | solution.py:153
  150.5 12.1 %collective-permute-start.26 = (f32[128,1536]{1,0:T(8,128)S(1)}, f32[128,1536]{1,0:T(8,128)S(1)}, u32[]{:S(2)}, u32[]{:S(2)}) collective-permute-start(f32[128,1536]{1,0:T(8,128)S(1)} %shard_map.149.a), channel_id=1, source_target_pairs={{0,2},{1,7},{2,0},{3,5},{4,6},{5,3},{6,4},{7,1},{8,10},{9,15},{10,... | collective-permute-start | bytes 2359304 | tf_op jit(solution)/shard_map/ppermute | solution.py:153
  180.8 40.9 %all-to-all-start = ((f32[64,8,1536]{2,1,0:T(8,128)}), f32[64,8,1536]{2,1,0:T(8,128)S(1)}, u32[]{:S(2)}, u32[]{:S(2)}) async-start(f32[64,8,1536]{2,1,0:T(8,128)} %bitcast.23), calls=%async_computation | async-start | bytes 6291456 | tf_op jit(solution)/shard_map/all_to_all | solution.py:506
  (42 other events, 720.1 us)

commit v2 on v1

v2 whole, which is shorter than its diff:
```python
import jax
import jax.numpy as jnp
from jax import lax
from jax.experimental import pallas as pl
from jax.experimental.pallas import tpu as pltpu
from jax.sharding import Mesh
from jax.sharding import PartitionSpec as P

TOK = ("tok_0", "tok_1", "tok_2")
ALL = TOK + ("head",)
NS_STEPS = 3
DH = 512
WIDE = 3 * DH
BF = jnp.bfloat16
F32 = jnp.float32
coef_first = 3.4445
coef_second = -4.775
coef_third = 2.0315
inner_step = 0.5
VMEM_BYTES = 24 * 1024 * 1024


def flat_at(x, y, z, c):
    return ((x * 4 + y) * 4 + z) * 2 + c


def links(move):
    out = []
    for x in range(4):
        for y in range(4):
            for z in range(4):
                for c in range(2):
                    out.append((flat_at(x, y, z, c), flat_at(*move(x, y, z, c))))
    return out


def pair(i, near):
    return i ^ 1 if near else 3 - i


def partner_links(step):
    axis = 3 - step

    def move(x, y, z, c):
        at = [x, y, z]
        at[axis] = pair(at[axis], c == 0)
        return (*at, c)

    return links(move)


PARTNERS = {step: partner_links(step) for step in (1, 2, 3)}
OTHER_CORE = links(lambda x, y, z, c: (x, y, z, 1 - c))


def colour(x, y, z, c):
    code = 0
    for at in (x, y, z):
        code = 2 * code + (((at + 1) // 2) % 2 if c == 0 else at // 2)
    return min(code, 7 - code)


def places():
    return [(x, y, z) for x in range(4) for y in range(4) for z in range(4)]


def of_colour(wanted, c):
    return [at for at in places() if colour(*at, c) == wanted]


COLOUR_GROUPS = [[flat_at(*at, c) for at in of_colour(q, c)] for c in range(2) for q in range(4)]
COLOURS = [[colour(*at, c) for at in places()] for c in range(2)]
TOKENS_BY_COLOUR = [
    [places().index(at) for q in range(4) for at in of_colour(q, c)] for c in range(2)
]


def own_table():
    core = lax.axis_index("head")
    own = jnp.asarray(COLOURS, jnp.int32)[core, lax.axis_index(TOK)]
    return jnp.concatenate([own[None], jnp.asarray(TOKENS_BY_COLOUR, jnp.int32)[core]])


SMEM = pl.BlockSpec(memory_space=pltpu.SMEM)
VMEM = pl.BlockSpec(memory_space=pltpu.VMEM)
HBM = pl.BlockSpec(memory_space=pltpu.HBM)


def call(body, outs, *args, scratch=(), scalars=None, flops=0, specs=None, out_specs=None):
    specs = specs or [VMEM] * len(args)
    if scalars is not None:
        specs = [SMEM] + specs
        args = (scalars, *args)
    moved = sum(a.size * a.dtype.itemsize for a in args) + sum(
        o.size * o.dtype.itemsize for o in outs
    )
    return pl.pallas_call(
        body,
        out_shape=list(outs),
        in_specs=specs,
        out_specs=out_specs or [VMEM] * len(outs),
        scratch_shapes=list(scratch),
        compiler_params=pltpu.CompilerParams(vmem_limit_bytes=VMEM_BYTES),
        cost_estimate=pl.CostEstimate(flops=flops, bytes_accessed=moved, transcendentals=0),
    )(*args)


def shape(*dims, dtype=F32):
    return jax.ShapeDtypeStruct(dims, dtype)


def nn(a, b):
    return jnp.dot(a, b, preferred_element_type=F32)


def nt(a, b):
    return lax.dot_general(a, b, (((1,), (1,)), ((), ())), preferred_element_type=F32)


def tn(a, b):
    return lax.dot_general(a, b, (((0,), (0,)), ((), ())), preferred_element_type=F32)


def rows_at(index, rows):
    return pl.ds(pl.multiple_of(index * rows, rows), rows)


def send_part(whole, terms, sems, index):
    at = (slice(None), columns(index))
    copy = pltpu.make_async_copy(whole.at[at], terms.at[at], sems.at[index])
    copy.start()
    return copy


def columns(index):
    return slice(index * DH, (index + 1) * DH)


SUM_STEPS = 4


def sum_body(pieces, copies, total):
    step = pl.program_id(0)
    part = jnp.sum(pieces[...], axis=0)

    @pl.when(step == 0)
    def _():
        total[...] = part

    @pl.when(step > 0)
    def _():
        total[...] += part

    @pl.when(step == SUM_STEPS - 1)
    def _():
        copies[...] = jnp.broadcast_to(total[...], copies.shape)


def pieces_spec(pieces):
    return pl.BlockSpec((pieces.shape[0] // SUM_STEPS, 8, WIDE), lambda i: (i, 0, 0))


def to_owners(terms):
    devices = lax.axis_size(TOK)
    return lax.all_to_all(terms.reshape(devices, DH // devices, WIDE), TOK, 0, 0, tiled=True)


def sum_everywhere(terms):
    pieces = to_owners(terms)
    copies, share = pl.pallas_call(
        sum_body,
        grid=(SUM_STEPS,),
        in_specs=[pieces_spec(pieces)],
        out_specs=[
            pl.BlockSpec((16, 8, WIDE), lambda i: (0, 0, 0)),
            pl.BlockSpec((8, WIDE), lambda i: (0, 0)),
        ],
        out_shape=[shape(16, 8, WIDE), shape(8, WIDE)],
        compiler_params=pltpu.CompilerParams(vmem_limit_bytes=VMEM_BYTES),
    )(pieces)
    mine = lax.all_to_all(copies, ALL, 0, 0, axis_index_groups=COLOUR_GROUPS, tiled=True)
    mine = mine.reshape(DH // 4, WIDE)
    return [mine] + [lax.ppermute(mine, ALL, PARTNERS[step]) for step in (1, 2, 3)], share


def place_rows(own, blocks, matrices):
    for step, block in enumerate(blocks):
        first = 1 + 16 * (own[0] ^ step)
        for j in range(16):
            at = rows_at(own[first + j], 8)
            for i in EACH:
                matrices[i, at, :] = block[8 * j : 8 * j + 8, columns(i)]


EACH = range(3)


def silu_parts(pre_gate):
    sigma_gate = jax.nn.sigmoid(pre_gate)
    act_gate = pre_gate * sigma_gate
    slope_gate = sigma_gate * (1.0 + pre_gate * (1.0 - sigma_gate))
    return (act_gate, slope_gate, sigma_gate)


def as_column(row):
    return jnp.transpose(jnp.broadcast_to(row, (128, row.shape[1])))[:, :1]


def key_body(rates, *refs):
    sources, terms, stored = refs[:5], refs[5], refs[6:13]
    whole, copies, sems, out_sems = refs[13], refs[14:19], refs[19], refs[20]
    gate, up, mid, mixed, target, dgate, dup = stored
    moves = [
        pltpu.make_async_copy(source, copy, sems.at[i])
        for i, (source, copy) in enumerate(zip(sources, copies))
    ]
    for move in moves:
        move.start()
    keys, w_gate, w_up, values, w_down = copies
    moves[0].wait()
    moves[1].wait()
    k = keys[...]
    g = nn(k, w_gate[...])
    gate[...] = g
    moves[2].wait()
    u = nn(k, w_up[...])
    up[...] = u
    act, slope, _ = silu_parts(g)
    mix = (act * u).astype(BF)
    mixed[...] = mix
    moves[3].wait()
    t = (-as_column(rates[...]) * values[...].astype(F32)).astype(BF)
    target[...] = t
    whole[:, 2 * DH :] = tn(mix, t)
    sent = [send_part(whole, terms, out_sems, 2)]
    moves[4].wait()
    m = nt(t, w_down[...])
    mid[...] = m
    dg = (m * u * slope).astype(BF)
    du = (m * act).astype(BF)
    dgate[...] = dg
    dup[...] = du
    whole[:, :DH] = tn(k, dg)
    sent.append(send_part(whole, terms, out_sems, 0))
    whole[:, DH : 2 * DH] = tn(k, du)
    sent.append(send_part(whole, terms, out_sems, 1))
    for copy in sent:
        copy.wait()


def query_forward(new, queries, cotangent, gain, stats, output, act_out, slope_out, mixed):
    q = queries[...]
    g = nn(q, new[0])
    u = nn(q, new[1])
    act, slope, _ = silu_parts(g)
    mix = (act * u).astype(BF)
    out = nn(mix, new[2])
    squares = jnp.sum(out * out, axis=1, keepdims=True)
    aligned = jnp.sum(cotangent[...].astype(F32) * gain[...] * out, axis=1, keepdims=True)
    lane = lax.broadcasted_iota(jnp.int32, stats.shape, 1)
    stats[...] = jnp.where(lane == 0, squares, aligned)
    output[...] = out
    act_out[...] = act
    slope_out[...] = u * slope
    mixed[...] = mix


def query_backward_body(
    new, queries, cotangent, gain, stats, other, output, act, slope, mixed, *refs
):
    terms, query_grad, whole, sems = refs
    both = stats[...] + other[...]
    inverse_rms = lax.rsqrt(both[:, :1] / (2 * DH) + 1e-05)
    aligned = both[:, 1:2]
    grad_output = (
        gain[...] * cotangent[...].astype(F32) * inverse_rms
        - output[...] * (aligned * inverse_rms * inverse_rms * inverse_rms / (2 * DH))
    ).astype(BF)
    whole[:, 2 * DH :] = tn(mixed[...], grad_output)
    sent = [send_part(whole, terms, sems, 2)]
    mid = nt(grad_output, new[2])
    dg = (mid * slope[...]).astype(BF)
    du = (mid * act[...]).astype(BF)
    q = queries[...]
    whole[:, :DH] = tn(q, dg)
    sent.append(send_part(whole, terms, sems, 0))
    whole[:, DH : 2 * DH] = tn(q, du)
    sent.append(send_part(whole, terms, sems, 1))
    query_grad[...] = (nt(dg, new[0]) + nt(du, new[1])).astype(BF)
    for copy in sent:
        copy.wait()


def key_backward(
    cots, w_gate, w_up, w_down, rates, keys, stored, terms, key_grad, value_grad, whole, sems
):
    gate, up, mid, mixed, target, dgate, dup = stored
    k = keys[...]
    t = target[...]
    back_gate = nn(k, cots[0])
    back_up = nn(k, cots[1])
    back_mixed = nt(t, cots[2])
    g = gate[...]
    u = up[...]
    m = mid[...]
    act, slope, sigma = silu_parts(g)
    curve = sigma * (1.0 - sigma) * (2.0 + g * (1.0 - 2.0 * sigma))
    bm = (back_gate * u * slope + back_up * act).astype(BF)
    whole[:, 2 * DH :] = tn(bm, t)
    sent = [send_part(whole, terms, sems, 2)]
    ub = (back_gate * m * slope + back_mixed * act).astype(BF)
    whole[:, DH : 2 * DH] = tn(k, ub)
    sent.append(send_part(whole, terms, sems, 1))
    gb = (back_gate * m * u * curve + back_up * m * slope + back_mixed * u * slope).astype(BF)
    whole[:, :DH] = tn(k, gb)
    sent.append(send_part(whole, terms, sems, 0))
    key_grad[...] = (
        nt(dgate[...], cots[0])
        + nt(dup[...], cots[1])
        + nt(gb, w_gate[...])
        + nt(ub, w_up[...])
    ).astype(BF)
    value_sum = nn(mixed[...], cots[2]) + nn(bm, w_down[...])
    value_grad[...] = (-as_column(rates[...]) * value_sum).astype(BF)
    for copy in sent:
        copy.wait()


def share_body(share, pieces, out_a, out_b, out_c, total):
    step = pl.program_id(0)

    @pl.when(step == 0)
    def _():
        total[...] = share[...]

    total[...] += jnp.sum(pieces[...], axis=0)

    @pl.when(step == SUM_STEPS - 1)
    def _():
        out_a[0] = total[:, :DH]
        out_b[0] = total[:, DH : 2 * DH]
        out_c[0] = total[:, 2 * DH :]


def weight_shares(share, pieces):
    out = pl.BlockSpec((1, 8, DH), lambda i: (0, 0, 0))
    return pl.pallas_call(
        share_body,
        grid=(SUM_STEPS,),
        in_specs=[
            pl.BlockSpec((8, WIDE), lambda i: (0, 0)),
            pieces_spec(pieces),
        ],
        out_specs=[out] * 3,
        out_shape=[shape(1, 8, DH)] * 3,
        scratch_shapes=[pltpu.VMEM((8, WIDE), F32)],
        compiler_params=pltpu.CompilerParams(vmem_limit_bytes=VMEM_BYTES),
    )(share, pieces)


def ortho_body(own, a, b, c, d, w_gate, w_up, w_down, queries, cotangent, gain, *refs):
    new, kept, norm, query_refs, (current, gram) = refs[0], refs[1], refs[2], refs[3:8], refs[8:]
    place_rows(own, (a, b, c, d), current)
    for i in EACH:
        matrix = current[i]
        root = jnp.sqrt(jnp.sum(matrix * matrix, keepdims=True) + 1e-06)
        norm[i] = jnp.broadcast_to(root, norm.shape[1:])
        unit = matrix * (1.0 / root)
        current[i] = unit
        kept[i, 0] = unit.astype(BF)
    for step in range(NS_STEPS):
        for i in EACH:
            narrow = kept[i, 3 * step]
            square = nt(narrow, narrow)
            gram[i] = square
            kept[i, 3 * step + 1] = square.astype(BF)
        for i in EACH:
            low = kept[i, 3 * step + 1]
            kept[i, 3 * step + 2] = (coef_second * gram[i] + coef_third * nn(low, low)).astype(BF)
        for i, weight in enumerate((w_gate, w_up, w_down)):
            later = coef_first * current[i] + nn(kept[i, 3 * step + 2], kept[i, 3 * step])
            if step < NS_STEPS - 1:
                current[i] = later
                kept[i, 3 * step + 3] = later.astype(BF)
            else:
                new[i] = (weight[...].astype(F32) - inner_step * later).astype(BF)
    query_forward(new, queries, cotangent, gain, *query_refs)


def ortho_back_body(
    own, a, b, c, d, kept, norm, w_gate, w_up, w_down, rates, keys, *refs
):
    stored, (terms, key_grad, value_grad) = refs[:7], refs[7:10]
    cots, grad, grad_low, half, sym, whole, sems = refs[10:]
    place_rows(own, (a, b, c, d), grad)
    for i in EACH:
        start = grad[i] * (-inner_step)
        grad[i] = start
        grad_low[i] = start.astype(BF)
    for step in reversed(range(NS_STEPS)):
        for i in EACH:
            half[i] = nt(grad_low[i], kept[i, 3 * step])
        for i in EACH:
            both = half[i] + jnp.transpose(half[i])
            sym[i] = both.astype(BF)
        for i in EACH:
            half[i] = coef_third * nn(sym[i], kept[i, 3 * step + 1])
        for i in EACH:
            full = coef_second * sym[i].astype(F32) + (half[i] + jnp.transpose(half[i]))
            sym[i] = full.astype(BF)
        for i in EACH:
            later = (
                coef_first * grad[i]
                + nn(kept[i, 3 * step + 2], grad_low[i])
                + nn(sym[i], kept[i, 3 * step])
            )
            grad[i] = later
            if step > 0:
                grad_low[i] = later.astype(BF)
    for i in EACH:
        unit = kept[i, 0].astype(F32)
        along = jnp.sum(grad[i] * unit, keepdims=True)
        cots[i] = ((grad[i] - unit * along) * (1.0 / norm[i, :1, :1])).astype(BF)
    key_backward(
        cots, w_gate, w_up, w_down, rates, keys, stored, terms, key_grad, value_grad, whole, sems
    )


def local(queries, key_rows, value_rows, step_rates, w_gate, w_up, w_down, out_gain, cotangent):
    tokens = queries.shape[1]
    queries, key_rows, value_rows, cotangent = (
        a[0] for a in (queries, key_rows, value_rows, cotangent)
    )
    w_gate, w_up, w_down = w_gate[0], w_up[0], w_down[0]
    own = own_table()

    whole = pltpu.VMEM((DH, WIDE), F32)
    out_sems = pltpu.SemaphoreType.DMA((3,))
    wide = shape(tokens, DH)
    low = shape(tokens, DH, dtype=BF)
    three = shape(3, DH, DH, dtype=BF)
    three_f32 = pltpu.VMEM((3, DH, DH), F32)
    three_low = pltpu.VMEM((3, DH, DH), BF)
    token_low = pltpu.VMEM((tokens, DH), BF)
    square_low = pltpu.VMEM((DH, DH), BF)
    terms, *stored = call(
        key_body,
        [shape(DH, WIDE), wide, wide, wide, low, low, low, low],
        step_rates,
        key_rows,
        w_gate,
        w_up,
        value_rows,
        w_down,
        scratch=[
            whole,
            token_low,
            square_low,
            square_low,
            token_low,
            square_low,
            pltpu.SemaphoreType.DMA((5,)),
            out_sems,
        ],
        specs=[VMEM] + [HBM] * 5,
        out_specs=[HBM] + [VMEM] * 7,
    )
    blocks, _ = sum_everywhere(terms)
    new, kept, norm, stats, *query_stored = call(
        ortho_body,
        [
            three,
            shape(3, 9, DH, DH, dtype=BF),
            shape(3, 8, 128),
            shape(tokens, 128),
            wide,
            wide,
            wide,
            low,
        ],
        *blocks,
        w_gate,
        w_up,
        w_down,
        queries,
        cotangent,
        out_gain,
        scalars=own,
        scratch=[three_f32, three_f32],
    )
    other = lax.ppermute(stats, ALL, OTHER_CORE)
    terms, query_grad = call(
        query_backward_body,
        [shape(DH, WIDE), low],
        new,
        queries,
        cotangent,
        out_gain,
        stats,
        other,
        *query_stored,
        scratch=[whole, out_sems],
        out_specs=[HBM, VMEM],
    )
    blocks, share = sum_everywhere(terms)
    terms, key_grad, value_grad = call(
        ortho_back_body,
        [shape(DH, WIDE), low, low],
        *blocks,
        kept,
        norm,
        w_gate,
        w_up,
        w_down,
        step_rates,
        key_rows,
        *stored,
        scalars=own,
        scratch=[three_low, three_f32, three_low, three_f32, three_low, whole, out_sems],
        out_specs=[HBM, VMEM, VMEM],
    )
    grads = weight_shares(share, to_owners(terms))
    return (query_grad[None], key_grad[None], value_grad[None], *grads)


def solution(mesh):
    split = Mesh(
        mesh.devices.reshape(4, 4, 4, mesh.shape["head"]), ("tok_0", "tok_1", "tok_2", "head")
    )
    rows = P("head", TOK, None)
    weight = P("head", None, None)
    in_specs = (
        rows,
        rows,
        rows,
        P("head", TOK),
        weight,
        weight,
        weight,
        P("head", None),
        rows,
    )
    return jax.shard_map(
        local, mesh=split, in_specs=in_specs, out_specs=(rows,) * 6, check_vma=False
    )
```

time: 225 us -> 267 us (1.19)
  blocking collectives: 0 us -> 190 us
  waiting for transfers between devices: 116 us -> 22.9 us
  starting transfers between devices: 49.1 us -> 3.43 us
  local copies, waits for them, and re-layouts: 22.1 us -> 11.1 us
    all_to_all x0 -> x5, blocking collectives: none -> 190 us  [the longest x3 149 us: to_owners(): lax.all_to_all(terms.reshape(devices, DH // devices, WIDE), TOK, 0, 0, ti...]
    ppermute x28 -> x6, waiting for transfers between devices: 99.5 us -> 21.5 us  [sum_everywhere(): lax.ppermute(mine, ALL, PARTNERS[step])]
    ppermute x28 -> x6, starting transfers between devices: 37.5 us -> 3.35 us  [sum_everywhere(): lax.ppermute(mine, ALL, PARTNERS[step])]
    all_to_all x1 -> x0, waiting for transfers between devices: 15.1 us -> none  [local(): lax.all_to_all(terms.reshape(devices, DH // devices, WIDE), TOK, 0, 0, ti...]
    unnamed x72 -> x60, local copies, waits for them, and re-layouts: 22.1 us -> 10.5 us
    all_to_all x1 -> x0, starting transfers between devices: 11.5 us -> none  [local(): lax.all_to_all(terms.reshape(devices, DH // devices, WIDE), TOK, 0, 0, ti...]
    pallas_call x17 -> x7, Pallas kernels: 34.3 us -> 36 us  [the longest x4 33.9 us: call(): pl.pallas_call(body, out_shape=list(outs), in_specs=specs, out_specs=out_...]
  transfers between devices with their start and end apart: 30 -> 7, of which waited for: 29 -> 7; matrix products, arithmetic and copies ran while one was open for 0% -> 0% of each run, Pallas kernels for 1% -> 0%
where the time goes in v2:
time: 267 us; the launch traced here: 265 us
  blocking collectives  190 us (71%)
  Pallas kernels  36 us (13%)
  waiting for transfers between devices  22.9 us (9%)
  local copies, waits for them, and re-layouts  11.1 us (4%)
  starting transfers between devices  3.43 us (1%)
    all_to_all x3, blocking collectives, to_owners(): lax.all_to_all(terms.reshape(devices, DH // devices, WIDE), TOK, 0, 0, ti...  149 us
    all_to_all x2, blocking collectives, sum_everywhere(): lax.all_to_all(copies, ALL, 0, 0, axis_index_groups=COLOUR_GROUPS, tiled=...  40.9 us
    pallas_call x4, Pallas kernels, call(): pl.pallas_call(body, out_shape=list(outs), in_specs=specs, out_specs=out_...  33.9 us
    ppermute x6, waiting for transfers between devices, sum_everywhere(): lax.ppermute(mine, ALL, PARTNERS[step])  21.5 us
    unnamed x60, local copies, waits for them, and re-layouts  10.5 us
  transfers between devices with their start and end apart: 7, of which 7 were waited for; matrix products, arithmetic and copies ran while one was open for 0% of the time, Pallas kernels for 0%

profile of v2, /device:TPU:0, one launch (start us, length us, event | category | flops | bytes accessed | tf_op | source)
XLA Modules:
  0.0 264.9 jit_solution(7868545029631839923)
XLA Ops:
  0.6 1.0 copy-done
  1.7 1.0 copy-done.2
  2.7 1.0 copy-done.4
  3.8 0.9 copy-done.6
  4.7 0.9 copy-done.24
  6.3 2.8 %shard_map.154 = (f32[512,1536]{1,0:T(8,128)S(1)}, f32[256,512]{1,0:T(8,128)S(1)}, f32[256,512]{1,0:T(8,128)S(1)}, f32[256,512]{1,0:T(8,128)S(1)}, bf16[256,512]...) custom-call(f32[1,256]{1,0:T(1,128)S(1)} %copy-done.26, ...), custom_call_target="tpu_custom_call" | custom-call | bytes 7865344 | tf_op jit(solution)/shard_map/pallas_call | solution.py:97
  9.9 0.8 copy-done.12
  10.7 0.8 copy-done.14
  12.9 52.3 %all_to_all.25.pieces = f32[64,8,1536]{2,1,0:T(8,128)S(1)} all-to-all(f32[64,8,1536]{2,1,0:T(8,128)S(1)} %bitcast.37), channel_id=1, replica_groups=mesh['tok_0'=4,'tok_1'=4,'tok_2'=4,'head'=2] {'tok_0','tok_1','tok_2'}, dimensions={0} | all-to-all | bytes 6291456 | tf_op jit(solution)/shard_map/all_to_all | solution.py:165
  65.3 0.9 shard_map.155
  66.2 20.6 %all_to_all.26 = f32[16,8,1536]{2,1,0:T(8,128)S(1)} all-to-all(f32[16,8,1536]{2,1,0:T(8,128)S(1)} %get-tuple-element.34), channel_id=1, replica_groups={{0,6,24,30,42,44,50,52,74,76,82,84,96,102,120,126},{2,4,26,28,40,46,48,..., dimensions={0} | all-to-all | bytes 1572864 | tf_op jit(solution)/shard_map/all_to_all | solution.py:181
  89.7 9.3 %collective-permute-done.2.d = f32[128,1536]{1,0:T(8,128)} collective-permute-done((f32[128,1536]{1,0:T(8,128)S(1)}, f32[128,1536]{1,0:T(8,128)}, u32[]{:S(2)}, u32[]{:S(2)}) %collective-permute-start.2) | collective-permute-done | bytes 786464 | tf_op jit(solution)/shard_map/ppermute | solution.py:183
  99.8 0.9 copy-done.9
  100.8 11.6 %shard_map.156 = (bf16[3,512,512]{2,1,0:T(8,128)(2,1)S(1)}, bf16[3,9,512,512]{3,2,1,0:T(8,128)(2,1)S(1)}, f32[3,8,128]{2,1,0:T(8,128)S(1)}, f32[256,128]{1,0:T(8...) custom-call(s32[65]{0:T(128)S(1)} %pad_add_fusion.own, ...), custom_call_target="tpu_custom_call" | custom-call | bytes 22952196 | tf_op jit(solution)/shard_map/pallas_call | solution.py:97
  112.4 1.3 collective-permute-done.3.other
  113.8 3.0 %shard_map.157 = (f32[512,1536]{1,0:T(8,128)S(1)}, bf16[256,512]{1,0:T(8,128)(2,1)}) custom-call(bf16[3,512,512]{2,1,0:T(8,128)(2,1)S(1)} %get-tuple-element.35.new, bf16[256,512]{1,0:T(8,128)(2,1)S(1)} %bitcast.41, bf16[256,512]{1,0:T(8,128)(2,1)S(1)} %bitcast.43, f32[1,512]{1,0:T(1,128)S(1)} %copy-done.25, f32[256,128]{1,0:T(8,128)S(1)} %get-tuple-element.36.stats, ...), custom_call_target="tpu_custom_call" | custom-call | bytes 7604224 | tf_op jit(solution)/shard_map/pallas_call | solution.py:97
  116.8 48.9 %all_to_all.27.pieces = f32[64,8,1536]{2,1,0:T(8,128)S(1)} all-to-all(f32[64,8,1536]{2,1,0:T(8,128)S(1)} %bitcast.36), channel_id=1, replica_groups=mesh['tok_0'=4,'tok_1'=4,'tok_2'=4,'head'=2] {'tok_0','tok_1','tok_2'}, dimensions={0} | all-to-all | bytes 6291456 | tf_op jit(solution)/shard_map/all_to_all | solution.py:165
  166.1 20.3 %all_to_all.28 = f32[16,8,1536]{2,1,0:T(8,128)S(1)} all-to-all(f32[16,8,1536]{2,1,0:T(8,128)S(1)} %get-tuple-element.43), channel_id=1, replica_groups={{0,6,24,30,42,44,50,52,74,76,82,84,96,102,120,126},{2,4,26,28,40,46,48,..., dimensions={0} | all-to-all | bytes 1572864 | tf_op jit(solution)/shard_map/all_to_all | solution.py:181
  186.7 0.9 collective-permute-start.5
  188.2 10.2 %collective-permute-done.6.d = f32[128,1536]{1,0:T(8,128)S(1)} collective-permute-done((f32[128,1536]{1,0:T(8,128)S(1)}, f32[128,1536]{1,0:T(8,128)S(1)}, u32[]{:S(2)}, u32[]{:S(2)}) %collective-permute-start.6) | collective-permute-done | bytes 786464 | tf_op jit(solution)/shard_map/ppermute | solution.py:183
  198.7 0.9 collective-permute-done.4.b
  199.7 16.5 %shard_map.159 = (f32[512,1536]{1,0:T(8,128)S(1)}, bf16[256,512]{1,0:T(8,128)(2,1)}, bf16[256,512]{1,0:T(8,128)(2,1)}) custom-call(s32[65]{0:T(128)S(1)} %pad_add_fusion.own, f32[128,1536]{1,0:T(8,128)S(1)} %bitcast.30, f32[128,1536]{1,0:T(8,128)S(1)} %collective-permute-done.4.b, f32[128,1536]{1,0:T(8,128)S(1)} %collective-permute-done.5.c, ...), custom_call_target="tpu_custom_call" | custom-call | bytes 25441540 | tf_op jit(solution)/shard_map/pallas_call | solution.py:97
  216.2 47.8 %all_to_all.29.pieces = f32[64,8,1536]{2,1,0:T(8,128)S(1)} all-to-all(f32[64,8,1536]{2,1,0:T(8,128)S(1)} %bitcast.35), channel_id=1, replica_groups=mesh['tok_0'=4,'tok_1'=4,'tok_2'=4,'head'=2] {'tok_0','tok_1','tok_2'}, dimensions={0} | all-to-all | bytes 6291456 | tf_op jit(solution)/shard_map/all_to_all | solution.py:165
  264.0 0.9 shard_map.160
  (65 shorter events, 8.3 us)
Async XLA Ops:
  12.9 52.3 %copy-start.20 = (bf16[256,512]{1,0:T(8,128)(2,1)}, bf16[256,512]{1,0:T(8,128)(2,1)S(1)}, u32[]{:S(2)}) copy-start(bf16[256,512]{1,0:T(8,128)(2,1)S(1)} %get-tuple-element.51.refs_5_) | copy-start | bytes 786436
  12.9 52.3 %copy-start.22 = (bf16[256,512]{1,0:T(8,128)(2,1)}, bf16[256,512]{1,0:T(8,128)(2,1)S(1)}, u32[]{:S(2)}) copy-start(bf16[256,512]{1,0:T(8,128)(2,1)S(1)} %get-tuple-element.52.refs_6_) | copy-start | bytes 786436
  65.2 23.7 %copy-start.29 = (s32[2,64]{1,0:T(2,128)S(1)}, s32[2,64]{1,0:T(2,128)}, u32[]{:S(2)}) copy-start(s32[2,64]{1,0:T(2,128)} %constant.30.clone) | copy-start | bytes 1540
  65.2 34.6 %copy-start.1 = (bf16[1,512,512]{2,1,0:T(8,128)(2,1)S(1)}, bf16[1,512,512]{2,1,0:T(8,128)(2,1)}, u32[]{:S(2)}) copy-start(bf16[1,512,512]{2,1,0:T(8,128)(2,1)} %param.15) | copy-start | bytes 1572868
  65.2 34.6 %copy-start.3 = (bf16[1,512,512]{2,1,0:T(8,128)(2,1)S(1)}, bf16[1,512,512]{2,1,0:T(8,128)(2,1)}, u32[]{:S(2)}) copy-start(bf16[1,512,512]{2,1,0:T(8,128)(2,1)} %param.16) | copy-start | bytes 1572868
  65.2 34.5 %copy-start.5 = (bf16[1,512,512]{2,1,0:T(8,128)(2,1)S(1)}, bf16[1,512,512]{2,1,0:T(8,128)(2,1)}, u32[]{:S(2)}) copy-start(bf16[1,512,512]{2,1,0:T(8,128)(2,1)} %param.17) | copy-start | bytes 1572868
  65.3 34.5 %copy-start.8 = (bf16[1,256,512]{2,1,0:T(8,128)(2,1)S(1)}, bf16[1,256,512]{2,1,0:T(8,128)(2,1)}, u32[]{:S(2)}) copy-start(bf16[1,256,512]{2,1,0:T(8,128)(2,1)} %param.11) | copy-start | bytes 786436
  65.3 34.5 %copy-start.25 = (f32[1,512]{1,0:T(1,128)S(1)}, f32[1,512]{1,0:T(1,128)}, u32[]{:S(2)}) copy-start(f32[1,512]{1,0:T(1,128)} %gain.3) | copy-start | bytes 6148
  86.8 12.1 %collective-permute-start.2 = (f32[128,1536]{1,0:T(8,128)S(1)}, f32[128,1536]{1,0:T(8,128)}, u32[]{:S(2)}, u32[]{:S(2)}) collective-permute-start(f32[128,1536]{1,0:T(8,128)S(1)} %bitcast.31), channel_id=1, source_target_pairs={{0,32},{1,97},{2,34},{3,99},{4,36},{5,101},{6,38},{7,103},{8,40},{... | collective-permute-start | bytes 2359304 | tf_op jit(solution)/shard_map/ppermute | solution.py:183
  87.0 12.1 %collective-permute-start.1 = (f32[128,1536]{1,0:T(8,128)S(1)}, f32[128,1536]{1,0:T(8,128)}, u32[]{:S(2)}, u32[]{:S(2)}) collective-permute-start(f32[128,1536]{1,0:T(8,128)S(1)} %bitcast.32), channel_id=1, source_target_pairs={{0,8},{1,25},{2,10},{3,27},{4,12},{5,29},{6,14},{7,31},{8,0},{9,17... | collective-permute-start | bytes 2359304 | tf_op jit(solution)/shard_map/ppermute | solution.py:183
  87.7 12.1 %collective-permute-start = (f32[128,1536]{1,0:T(8,128)S(1)}, f32[128,1536]{1,0:T(8,128)}, u32[]{:S(2)}, u32[]{:S(2)}) collective-permute-start(f32[128,1536]{1,0:T(8,128)S(1)} %bitcast.33), channel_id=1, source_target_pairs={{0,2},{1,7},{2,0},{3,5},{4,6},{5,3},{6,4},{7,1},{8,10},{9,15},{10,... | collective-permute-start | bytes 2359304 | tf_op jit(solution)/shard_map/ppermute | solution.py:183
  112.3 1.4 collective-permute-start.3
  165.7 33.9 %copy-start.7 = (bf16[1,256,512]{2,1,0:T(8,128)(2,1)S(1)}, bf16[1,256,512]{2,1,0:T(8,128)(2,1)}, u32[]{:S(2)}) copy-start(bf16[1,256,512]{2,1,0:T(8,128)(2,1)} %param.12) | copy-start | bytes 786436
  165.7 33.9 %copy-start.11 = (f32[256,512]{1,0:T(8,128)S(1)}, f32[256,512]{1,0:T(8,128)}, u32[]{:S(2)}) copy-start(f32[256,512]{1,0:T(8,128)} %copy-done.10) | copy-start | bytes 1572868
  165.7 33.9 %copy-start.13 = (f32[256,512]{1,0:T(8,128)S(1)}, f32[256,512]{1,0:T(8,128)}, u32[]{:S(2)}) copy-start(f32[256,512]{1,0:T(8,128)} %copy-done.12) | copy-start | bytes 1572868
  165.7 33.9 %copy-start.15 = (f32[256,512]{1,0:T(8,128)S(1)}, f32[256,512]{1,0:T(8,128)}, u32[]{:S(2)}) copy-start(f32[256,512]{1,0:T(8,128)} %copy-done.14) | copy-start | bytes 1572868
  165.7 33.9 %copy-start.17 = (bf16[256,512]{1,0:T(8,128)(2,1)S(1)}, bf16[256,512]{1,0:T(8,128)(2,1)}, u32[]{:S(2)}) copy-start(bf16[256,512]{1,0:T(8,128)(2,1)} %copy-done.16) | copy-start | bytes 786436
  165.7 33.9 %copy-start.19 = (bf16[256,512]{1,0:T(8,128)(2,1)S(1)}, bf16[256,512]{1,0:T(8,128)(2,1)}, u32[]{:S(2)}) copy-start(bf16[256,512]{1,0:T(8,128)(2,1)} %copy-done.18) | copy-start | bytes 786436
  165.7 33.9 %copy-start.21 = (bf16[256,512]{1,0:T(8,128)(2,1)S(1)}, bf16[256,512]{1,0:T(8,128)(2,1)}, u32[]{:S(2)}) copy-start(bf16[256,512]{1,0:T(8,128)(2,1)} %copy-done.20) | copy-start | bytes 786436
  165.7 33.9 %copy-start.23 = (bf16[256,512]{1,0:T(8,128)(2,1)S(1)}, bf16[256,512]{1,0:T(8,128)(2,1)}, u32[]{:S(2)}) copy-start(bf16[256,512]{1,0:T(8,128)(2,1)} %copy-done.22) | copy-start | bytes 786436
  165.8 33.9 %copy-start.27 = (f32[1,256]{1,0:T(1,128)S(1)}, f32[1,256]{1,0:T(1,128)}, u32[]{:S(2)}) copy-start(f32[1,256]{1,0:T(1,128)} %rates.3) | copy-start | bytes 3076
  186.4 12.0 %collective-permute-start.6 = (f32[128,1536]{1,0:T(8,128)S(1)}, f32[128,1536]{1,0:T(8,128)S(1)}, u32[]{:S(2)}, u32[]{:S(2)}) collective-permute-start(f32[128,1536]{1,0:T(8,128)S(1)} %bitcast.27), channel_id=1, source_target_pairs={{0,32},{1,97},{2,34},{3,99},{4,36},{5,101},{6,38},{7,103},{8,40},{... | collective-permute-start | bytes 2359304 | tf_op jit(solution)/shard_map/ppermute | solution.py:183
  186.7 12.0 %collective-permute-start.5 = (f32[128,1536]{1,0:T(8,128)S(1)}, f32[128,1536]{1,0:T(8,128)S(1)}, u32[]{:S(2)}, u32[]{:S(2)}) collective-permute-start(f32[128,1536]{1,0:T(8,128)S(1)} %bitcast.28), channel_id=1, source_target_pairs={{0,8},{1,25},{2,10},{3,27},{4,12},{5,29},{6,14},{7,31},{8,0},{9,17... | collective-permute-start | bytes 2359304 | tf_op jit(solution)/shard_map/ppermute | solution.py:183
  187.6 12.0 %collective-permute-start.4 = (f32[128,1536]{1,0:T(8,128)S(1)}, f32[128,1536]{1,0:T(8,128)S(1)}, u32[]{:S(2)}, u32[]{:S(2)}) collective-permute-start(f32[128,1536]{1,0:T(8,128)S(1)} %bitcast.29), channel_id=1, source_target_pairs={{0,2},{1,7},{2,0},{3,5},{4,6},{5,3},{6,4},{7,1},{8,10},{9,15},{10,... | collective-permute-start | bytes 2359304 | tf_op jit(solution)/shard_map/ppermute | solution.py:183
  (13 other events, 33.6 us)

commit v3 on v1

--- a/solution.py
+++ b/solution.py
@@ -49,41 +49,52 @@
     return links(move)
 
 
-def antipode_links(level):
-    def move(x, y, z, c):
-        near = (level == 1) != (c == 1)
-        return (pair(x, near), pair(y, near), pair(z, near), c)
-
-    return links(move)
+def antipode_links(step):
+    flip = {1: lambda i: 3 - i, 2: lambda i: i ^ 1, 3: lambda i: i ^ 2}[step]
+    return links(lambda x, y, z, c: (flip(x), flip(y), flip(z), c))
 
 
 PARTNERS = {(level, step): partner_links(level, step) for level in (1, 2) for step in (1, 2, 3)}
-ANTIPODES = {level: antipode_links(level) for level in (1, 2)}
+PARTNERS.update({(3, step): antipode_links(step) for step in (1, 2, 3)})
 OTHER_CORE = links(lambda x, y, z, c: (x, y, z, 1 - c))
 
 
-def colour(bit, x, y, z):
-    code = bit(x) * 4 + bit(y) * 2 + bit(z)
-    return jnp.where(code >= 4, 7 - code, code)
-
-
-def own_colours():
-    x, y, z = (lax.axis_index(a) for a in TOK)
-    core = lax.axis_index("head")
-    low = colour(lambda i: ((i + 1) // 2) % 2, x, y, z)
-    high = colour(lambda i: i // 2, x, y, z)
-    first = jnp.where(core == 0, low, high)
-    second = jnp.where(core == 0, high, low)
-    token = (x * 4 + y) * 4 + z
-    return jnp.stack([first, second, token]).astype(jnp.int32)
+def colour(x, y, z, low):
+    code = 0
+    for at in (x, y, z):
+        code = 2 * code + (((at + 1) // 2) % 2 if low else at // 2)
+    return min(code, 7 - code)
+
+
+PLACES = [(x, y, z) for x in range(4) for y in range(4) for z in range(4)]
+
+
+def of_colour(wanted, c):
+    return [t for t, at in enumerate(PLACES) if colour(*at, c == 0) == wanted]
+
+
+COLOUR_GROUPS = [[2 * t + c for t in of_colour(q, c)] for c in range(2) for q in range(4)]
+TABLE = [
+    [
+        [colour(*at, c == 0), colour(*at, c == 1), t]
+        + [t for q in range(4) for t in of_colour(q, c)]
+        for c in range(2)
+    ]
+    for t, at in enumerate(PLACES)
+]
+
+
+def own_table():
+    table = jnp.asarray(TABLE, jnp.int32)
+    return table[lax.axis_index(TOK), lax.axis_index("head")]
 
 
 SMEM = pl.BlockSpec(memory_space=pltpu.SMEM)
 VMEM = pl.BlockSpec(memory_space=pltpu.VMEM)
-HBM = pl.BlockSpec(memory_space=pl.ANY)
-
-
-def call(body, outs, *args, scratch=(), scalars=None, flops=0, specs=None, limit=VMEM_BYTES):
+HBM = pl.BlockSpec(memory_space=pltpu.HBM)
+
+
+def call(body, outs, *args, scratch=(), scalars=None, flops=0, specs=None, out_specs=None, limit=VMEM_BYTES):
     specs = specs or [VMEM] * len(args)
     if scalars is not None:
         specs = [SMEM] + specs
@@ -95,7 +106,7 @@
         body,
         out_shape=list(outs),
         in_specs=specs,
-        out_specs=[VMEM] * len(outs),
+        out_specs=out_specs or [VMEM] * len(outs),
         scratch_shapes=list(scratch),
         compiler_params=pltpu.CompilerParams(vmem_limit_bytes=limit),
         cost_estimate=pl.CostEstimate(flops=flops, bytes_accessed=moved, transcendentals=0),
@@ -125,6 +136,10 @@
 def hand_out(own, whole, outs, rows):
     for step in range(4):
         outs[step][...] = whole[rows_at(own ^ step, rows), :]
+
+
+def columns(index):
+    return slice(index * DH, (index + 1) * DH)
 
 
 def fold_body(own, a, b, c, d, *outs):
@@ -154,14 +169,15 @@
     ]
 
 
-def sum_everywhere(blocks, own):
+def with_other(blocks, done):
+    return lax.optimization_barrier((tuple(blocks), done))
+
+
+def sum_everywhere(arrived, own):
     piece_shape = [shape(32, WIDE)]
-    blocks = received(blocks, 1)
-    blocks = call(fold_body, piece_shape * 4, *blocks, scalars=own)
+    blocks = call(fold_body, piece_shape * 4, *arrived, scalars=own)
     (piece,) = call(total_body, piece_shape, *received(blocks, 2))
-    for level in (1, 2):
-        arrived = lax.ppermute(piece, ALL, ANTIPODES[level])
-        (piece,) = call(total_body, piece_shape, piece, arrived)
+    (piece,) = call(total_body, piece_shape, *received([piece] * 4, 3))
     (piece,) = call(join_body, [shape(128, WIDE)], *received([piece] * 4, 2), scalars=own)
     return received([piece] * 4, 1)
 
@@ -177,42 +193,62 @@
     return jnp.transpose(jnp.broadcast_to(row, (128, row.shape[1])))[:, :1]
 
 
-def key_body(own, rates, *refs):
-    sources, outs, stored = refs[:5], refs[5:9], refs[9:16]
-    whole, copies, sems = refs[16], refs[17:22], refs[22]
-    gate, up, mid, mixed, target, dgate, dup = stored
+def key_body(own, *refs):
+    sources, outs, finals = refs[:6], refs[6:10], refs[10:17]
+    copies, stored, whole, in_sems, out_sems = refs[17:23], refs[23:30], *refs[30:]
     moves = [
-        pltpu.make_async_copy(source, copy, sems.at[i])
+        pltpu.make_async_copy(source, copy, in_sems.at[i])
         for i, (source, copy) in enumerate(zip(sources, copies))
     ]
     for move in moves:
         move.start()
-    keys, w_gate, w_up, values, w_down = copies
+    keys, w_gate, w_up, rates, values, w_down = copies
+    gate, up, mid, mixed, target, dgate, dup = stored
+    sent = []
+
+    def send(source, goal):
+        sent.append(pltpu.make_async_copy(source, goal, out_sems.at[len(sent)]))
+        sent[-1].start()
+
+    def keep(index, value):
+        stored[index][...] = value
+        send(stored[index], finals[index])
+
+    def send_quarters(index):
+        for step in range(4):
+            at = (rows_at(own[0] ^ step, DH // 4), columns(index))
+            send(whole.at[at], outs[step].at[:, columns(index)])
+
     moves[0].wait()
     moves[1].wait()
     k = keys[...]
     g = nn(k, w_gate[...])
-    gate[...] = g
+    keep(0, g)
     moves[2].wait()
     u = nn(k, w_up[...])
-    up[...] = u
+    keep(1, u)
     act, slope, _ = silu_parts(g)
     mix = (act * u).astype(BF)
-    mixed[...] = mix
+    keep(3, mix)
     moves[3].wait()
+    moves[4].wait()
     t = (-as_column(rates[...]) * values[...].astype(F32)).astype(BF)
-    target[...] = t
-    whole[:, 2 * DH :] = tn(mix, t)
-    moves[4].wait()
+    keep(4, t)
+    whole[:, columns(2)] = tn(mix, t)
+    send_quarters(2)
+    moves[5].wait()
     m = nt(t, w_down[...])
-    mid[...] = m
+    keep(2, m)
+    du = (m * act).astype(BF)
+    keep(6, du)
+    whole[:, columns(1)] = tn(k, du)
+    send_quarters(1)
     dg = (m * u * slope).astype(BF)
-    du = (m * act).astype(BF)
-    dgate[...] = dg
-    dup[...] = du
-    whole[:, :DH] = tn(k, dg)
-    whole[:, DH : 2 * DH] = tn(k, du)
-    hand_out(own[0], whole, outs, DH // 4)
+    keep(5, dg)
+    whole[:, columns(0)] = tn(k, dg)
+    send_quarters(0)
+    for copy in sent:
+        copy.wait()
 
 
 def query_forward(new, queries, cotangent, gain, stats, output, act_out, slope_out, mixed):
@@ -259,7 +295,7 @@
     query_grad[...] = (nt(dgate[...], new[0]) + nt(dup[...], new[1])).astype(BF)
 
 
-def key_terms(cots, keys, gate, up, mid, target, terms, back_mid, gate_back, up_back):
+def key_terms(cots, keys, gate, up, mid, target, back_mid, gate_back, up_back, terms):
     k = keys[...]
     t = target[...]
     back_gate = nn(k, cots[0])
@@ -295,46 +331,13 @@
     value_grad[...] = (-as_column(rates[...]) * value_sum).astype(BF)
 
 
-SHARE_STEPS = 4
-
-
-def share_body(share, pieces, out_a, out_b, out_c, total):
-    step = pl.program_id(0)
-
-    @pl.when(step == 0)
-    def _():
-        total[...] = share[...]
-
-    total[...] += jnp.sum(pieces[...], axis=0)
-
-    @pl.when(step == SHARE_STEPS - 1)
-    def _():
-        out_a[0] = total[:, :DH]
-        out_b[0] = total[:, DH : 2 * DH]
-        out_c[0] = total[:, 2 * DH :]
-
-
-def weight_shares(share, pieces):
-    out = pl.BlockSpec((1, 8, DH), lambda i: (0, 0, 0))
-    return pl.pallas_call(
-        share_body,
-        grid=(SHARE_STEPS,),
-        in_specs=[
-            pl.BlockSpec((8, WIDE), lambda i: (0, 0)),
-            pl.BlockSpec((pieces.shape[0] // SHARE_STEPS, 8, WIDE), lambda i: (i, 0, 0)),
-        ],
-        out_specs=[out] * 3,
-        out_shape=[shape(1, 8, DH)] * 3,
-        scratch_shapes=[pltpu.VMEM((8, WIDE), F32)],
-        compiler_params=pltpu.CompilerParams(vmem_limit_bytes=VMEM_BYTES),
-    )(share, pieces)
+def share_body(share, pieces, out_a, out_b, out_c):
+    value = share[...] + jnp.sum(pieces[...], axis=0)
+    for index, out in enumerate((out_a, out_b, out_c)):
+        out[0] = value[:, columns(index)]
 
 
 EACH = range(3)
-
-
-def columns(index):
-    return slice(index * DH, (index + 1) * DH)
 
 
 def ortho_body(own, a, b, c, d, w_gate, w_up, w_down, queries, cotangent, gain, *refs):
@@ -369,13 +372,8 @@
 
 
 def ortho_back_body(own, a, b, c, d, kept, norm, keys, gate, up, mid, target, *refs):
-    cots, share, terms, key_refs, (grad, grad_low, half, sym) = (
-        refs[0],
-        refs[1],
-        refs[2],
-        refs[3:6],
-        refs[6:],
-    )
+    cots, share, outs, key_refs = refs[0], refs[1], refs[2:6], refs[6:9]
+    grad, grad_low, half, sym, terms = refs[9:]
     for step, block in enumerate((a, b, c, d)):
         for i in EACH:
             grad[i, rows_at(own[0] ^ step, DH // 4), :] = block[:, columns(i)]
@@ -408,7 +406,11 @@
         unit = kept[i, 0].astype(F32)
         along = jnp.sum(grad[i] * unit, keepdims=True)
         cots[i] = ((grad[i] - unit * along) * (1.0 / norm[i, :1, :1])).astype(BF)
-    key_terms(cots, keys, gate, up, mid, target, terms, *key_refs)
+    key_terms(cots, keys, gate, up, mid, target, *key_refs, terms)
+    for step in range(4):
+        first = 3 + 16 * (own[0] ^ step)
+        for j in range(16):
+            outs[step][8 * j : 8 * j + 8, :] = terms[rows_at(own[first + j], 8), :]
 
 
 def local(queries, key_rows, value_rows, step_rates, w_gate, w_up, w_down, out_gain, cotangent):
@@ -417,7 +419,7 @@
         a[0] for a in (queries, key_rows, value_rows, cotangent)
     )
     w_gate, w_up, w_down = w_gate[0], w_up[0], w_down[0]
-    own = own_colours()
+    own = own_table()
 
     whole = pltpu.VMEM((DH, WIDE), F32)
     quarters = [shape(DH // 4, WIDE)] * 4
@@ -426,28 +428,22 @@
     three = shape(3, DH, DH, dtype=BF)
     three_f32 = pltpu.VMEM((3, DH, DH), F32)
     three_low = pltpu.VMEM((3, DH, DH), BF)
-    token_low = pltpu.VMEM((tokens, DH), BF)
-    square_low = pltpu.VMEM((DH, DH), BF)
+    key_inputs = (key_rows, w_gate, w_up, step_rates, value_rows, w_down)
+    stored_shapes = [wide, wide, wide, low, low, low, low]
     *blocks, gate, up, mid, mixed, target, dgate, dup = call(
         key_body,
-        [*quarters, wide, wide, wide, low, low, low, low],
-        step_rates,
-        key_rows,
-        w_gate,
-        w_up,
-        value_rows,
-        w_down,
+        [*quarters, *stored_shapes],
+        *key_inputs,
         scratch=[
+            *(pltpu.VMEM(a.shape, a.dtype) for a in (*key_inputs, *stored_shapes)),
             whole,
-            token_low,
-            square_low,
-            square_low,
-            token_low,
-            square_low,
-            pltpu.SemaphoreType.DMA((5,)),
+            pltpu.SemaphoreType.DMA((6,)),
+            pltpu.SemaphoreType.DMA((19,)),
         ],
         scalars=own,
-        specs=[VMEM] + [HBM] * 5,
+        specs=[HBM] * 6,
+        out_specs=[HBM] * 11,
+        limit=56 * 1024 * 1024,
     )
     new, kept, norm, stats, *query_stored = call(
         ortho_body,
@@ -461,7 +457,7 @@
             wide,
             low,
         ],
-        *sum_everywhere(blocks, own),
+        *sum_everywhere(received(blocks, 1), own),
         w_gate,
         w_up,
         w_down,
@@ -485,12 +481,13 @@
         scratch=[whole],
         scalars=own,
     )
-    (query_grad,) = call(
+    query_grad = call(
         query_grad_body, [low], new, query_dgate, query_dup, flops=4 * tokens * DH * DH
     )
-    cots, share, terms, back_mid, gate_back, up_back = call(
+    blocks, (query_grad,) = with_other(received(blocks, 1), query_grad)
+    cots, share, *blocks, back_mid, gate_back, up_back = call(
         ortho_back_body,
-        [three, shape(8, WIDE), shape(DH, WIDE), low, low, low],
+        [three, shape(8, WIDE), *quarters, low, low, low],
         *sum_everywhere(blocks, own),
         kept,
         norm,
@@ -500,13 +497,9 @@
         mid,
         target,
         scalars=own,
-        scratch=[three_f32, three_low, three_f32, three_low],
-    )
-    devices = lax.axis_size(TOK)
-    pieces = lax.all_to_all(
-        terms.reshape(devices, DH // devices, WIDE), TOK, 0, 0, tiled=True
-    )
-    key_grad, value_grad = call(
+        scratch=[three_f32, three_low, three_f32, three_low, whole],
+    )
+    key_grads = call(
         key_grads_body,
         [low, low],
         cots,
@@ -522,7 +515,12 @@
         up_back,
         flops=12 * tokens * DH * DH,
     )
-    grads = weight_shares(share, pieces)
+    blocks, (key_grad, value_grad) = with_other(received(blocks, 1), key_grads)
+    (quarter,) = call(total_body, quarters[:1], *blocks)
+    pieces = lax.all_to_all(
+        quarter.reshape(16, 8, WIDE), ALL, 0, 0, axis_index_groups=COLOUR_GROUPS, tiled=True
+    )
+    grads = call(share_body, [shape(1, 8, DH)] * 3, share, pieces)
     return (query_grad[None], key_grad[None], value_grad[None], *grads)
 
 

time: 225 us -> 207 us (0.920); the launches traced: 223 us -> 207 us
  waiting for transfers between devices: 116 us -> 89.8 us
  blocking collectives: 0 us -> 21.1 us
  local copies, waits for them, and re-layouts: 22.1 us -> 2.41 us
  starting transfers between devices: 49.1 us -> 55.6 us
  Pallas kernels: 34.3 us -> 37.1 us
    ppermute x4 -> x0, waiting for transfers between devices: 29.6 us -> none  [sum_everywhere(): arrived = lax.ppermute(piece, ALL, ANTIPODES[level])]
    ppermute x24 -> x33, starting transfers between devices: 29.6 us -> 55.5 us  [received(): lax.ppermute(blocks[step], ALL, PARTNERS[level, step])]
    all_to_all x0 -> x1, blocking collectives: none -> 21.1 us  [local(): lax.all_to_all(quarter.reshape(16, 8, WIDE), ALL, 0, 0, axis_index_groups...]
    unnamed x72 -> x34, local copies, waits for them, and re-layouts: 22.1 us -> 1.21 us
    ppermute x24 -> x33, waiting for transfers between devices: 69.9 us -> 88.5 us  [received(): lax.ppermute(blocks[step], ALL, PARTNERS[level, step])]
    all_to_all x1 -> x0, waiting for transfers between devices: 15.1 us -> none  [local(): lax.all_to_all(terms.reshape(devices, DH // devices, WIDE), TOK, 0, 0, ti...]
    all_to_all x1 -> x0, starting transfers between devices: 11.5 us -> none  [local(): lax.all_to_all(terms.reshape(devices, DH // devices, WIDE), TOK, 0, 0, ti...]
    ppermute x4 -> x0, starting transfers between devices: 7.83 us -> none  [sum_everywhere(): arrived = lax.ppermute(piece, ALL, ANTIPODES[level])]
  transfers between devices with their start and end apart: 30 -> 34, of which waited for: 29 -> 31; matrix products, arithmetic and copies ran while one was open for 0% -> 0% of each run, Pallas kernels for 1% -> 1%
where the time goes in v3:
time: 207 us
  waiting for transfers between devices  89.8 us (43%)
  starting transfers between devices  55.6 us (27%)
  Pallas kernels  37.1 us (18%)
  blocking collectives  21.1 us (10%)
  local copies, waits for them, and re-layouts  2.41 us (1%)
    ppermute x33, waiting for transfers between devices, received(): lax.ppermute(blocks[step], ALL, PARTNERS[level, step])  88.5 us
    ppermute x33, starting transfers between devices, received(): lax.ppermute(blocks[step], ALL, PARTNERS[level, step])  55.5 us
    pallas_call x16, Pallas kernels, call(): pl.pallas_call(body, out_shape=list(outs), in_specs=specs, out_specs=out_...  37.1 us
    all_to_all x1, blocking collectives, local(): lax.all_to_all(quarter.reshape(16, 8, WIDE), ALL, 0, 0, axis_index_groups...  21.1 us
  transfers between devices with their start and end apart: 34, of which 31 were waited for; matrix products, arithmetic and copies ran while one was open for 0% of the time, Pallas kernels for 1%

profile of v3, /device:TPU:0, one launch (start us, length us, event | category | flops | bytes accessed | tf_op | source)
XLA Modules:
  0.0 206.9 jit_solution(6851002216491250886)
XLA Ops:
  1.8 5.3 %shard_map.145 = (f32[128,1536]{1,0:T(8,128)}, f32[128,1536]{1,0:T(8,128)}, f32[128,1536]{1,0:T(8,128)}, f32[128,1536]{1,0:T(8,128)}, f32[256,512]{1,0:T(8,128)}...) custom-call(s32[67]{0:T(128)} %dynamic-slice_bitcast_fusion.own, ...), custom_call_target="tpu_custom_call" | custom-call | bytes 7865612 | tf_op jit(solution)/shard_map/pallas_call | solution.py:105
  12.3 7.1 %collective-permute-done.b = f32[128,1536]{1,0:T(8,128)S(1)} collective-permute-done((f32[128,1536]{1,0:T(8,128)}, f32[128,1536]{1,0:T(8,128)S(1)}, u32[]{:S(2)}, u32[]{:S(2)}) %collective-permute-start) | collective-permute-done | bytes 786464 | tf_op jit(solution)/shard_map/ppermute | solution.py:168
  24.9 2.6 %collective-permute-start.3 = (f32[32,1536]{1,0:T(8,128)S(1)}, f32[32,1536]{1,0:T(8,128)S(1)}, u32[]{:S(2)}, u32[]{:S(2)}) collective-permute-start(f32[32,1536]{1,0:T(8,128)S(1)} %get-tuple-element.69), channel_id=1, source_target_pairs={{0,6},{1,3},{2,4},{3,1},{4,2},{5,7},{6,0},{7,5},{8,14},{9,11},{10,... | collective-permute-start | bytes 589832 | tf_op jit(solution)/shard_map/ppermute | solution.py:168
  29.7 2.8 %collective-permute-start.5 = (f32[32,1536]{1,0:T(8,128)S(1)}, f32[32,1536]{1,0:T(8,128)S(1)}, u32[]{:S(2)}, u32[]{:S(2)}) collective-permute-start(f32[32,1536]{1,0:T(8,128)S(1)} %get-tuple-element.71), channel_id=1, source_target_pairs={{0,96},{1,33},{2,98},{3,35},{4,100},{5,37},{6,102},{7,39},{8,104},... | collective-permute-start | bytes 589832 | tf_op jit(solution)/shard_map/ppermute | solution.py:168
  36.6 2.7 %collective-permute-start.8 = (f32[32,1536]{1,0:T(8,128)S(1)}, f32[32,1536]{1,0:T(8,128)S(1)}, u32[]{:S(2)}, u32[]{:S(2)}) collective-permute-start(f32[32,1536]{1,0:T(8,128)S(1)} %shard_map.147.refs_0_), channel_id=1, source_target_pairs={{0,84},{1,85},{2,86},{3,87},{4,80},{5,81},{6,82},{7,83},{8,92},{9,... | collective-permute-start | bytes 589832 | tf_op jit(solution)/shard_map/ppermute | solution.py:168
  41.5 4.1 %collective-permute-start.6 = (f32[32,1536]{1,0:T(8,128)S(1)}, f32[32,1536]{1,0:T(8,128)S(1)}, u32[]{:S(2)}, u32[]{:S(2)}) collective-permute-start(f32[32,1536]{1,0:T(8,128)S(1)} %shard_map.147.refs_0_), channel_id=1, source_target_pairs={{0,126},{1,127},{2,124},{3,125},{4,122},{5,123},{6,120},{7,121},{8... | collective-permute-start | bytes 589832 | tf_op jit(solution)/shard_map/ppermute | solution.py:168
  45.6 5.7 %collective-permute-done.8.refs_3_ = f32[32,1536]{1,0:T(8,128)S(1)} collective-permute-done((f32[32,1536]{1,0:T(8,128)S(1)}, f32[32,1536]{1,0:T(8,128)S(1)}, u32[]{:S(2)}, u32[]{:S(2)}) %collective-permute-start.8) | collective-permute-done | bytes 196640 | tf_op jit(solution)/shard_map/ppermute | solution.py:168
  53.1 2.7 %collective-permute-start.11 = (f32[32,1536]{1,0:T(8,128)S(1)}, f32[32,1536]{1,0:T(8,128)S(1)}, u32[]{:S(2)}, u32[]{:S(2)}) collective-permute-start(f32[32,1536]{1,0:T(8,128)S(1)} %shard_map.148.a), channel_id=1, source_target_pairs={{0,96},{1,33},{2,98},{3,35},{4,100},{5,37},{6,102},{7,39},{8,104},... | collective-permute-start | bytes 589832 | tf_op jit(solution)/shard_map/ppermute | solution.py:168
  61.0 2.6 %collective-permute-done.10.c = f32[32,1536]{1,0:T(8,128)S(1)} collective-permute-done((f32[32,1536]{1,0:T(8,128)S(1)}, f32[32,1536]{1,0:T(8,128)S(1)}, u32[]{:S(2)}, u32[]{:S(2)}) %collective-permute-start.10) | collective-permute-done | bytes 196640 | tf_op jit(solution)/shard_map/ppermute | solution.py:168
  64.8 11.6 %collective-permute-done.14.d = f32[128,1536]{1,0:T(8,128)S(1)} collective-permute-done((f32[128,1536]{1,0:T(8,128)S(1)}, f32[128,1536]{1,0:T(8,128)S(1)}, u32[]{:S(2)}, u32[]{:S(2)}) %collective-permute-start.14) | collective-permute-done | bytes 786464 | tf_op jit(solution)/shard_map/ppermute | solution.py:168
  76.8 10.1 %shard_map.150 = (bf16[3,512,512]{2,1,0:T(8,128)(2,1)S(1)}, bf16[3,9,512,512]{3,2,1,0:T(8,128)(2,1)S(1)}, f32[3,8,128]{2,1,0:T(8,128)S(1)}, f32[256,128]{1,0:T(8...) custom-call(s32[67]{0:T(128)S(1)} %copy-done.14, ...), custom_call_target="tpu_custom_call" | custom-call | bytes 22952204 | tf_op jit(solution)/shard_map/pallas_call | solution.py:105
  95.1 7.0 %collective-permute-done.16.b = f32[128,1536]{1,0:T(8,128)S(1)} collective-permute-done((f32[128,1536]{1,0:T(8,128)S(1)}, f32[128,1536]{1,0:T(8,128)S(1)}, u32[]{:S(2)}, u32[]{:S(2)}) %collective-permute-start.16) | collective-permute-done | bytes 786464 | tf_op jit(solution)/shard_map/ppermute | solution.py:168
  104.6 2.5 %collective-permute-start.19 = (f32[32,1536]{1,0:T(8,128)S(1)}, f32[32,1536]{1,0:T(8,128)S(1)}, u32[]{:S(2)}, u32[]{:S(2)}) collective-permute-start(f32[32,1536]{1,0:T(8,128)S(1)} %get-tuple-element.90), channel_id=1, source_target_pairs={{0,6},{1,3},{2,4},{3,1},{4,2},{5,7},{6,0},{7,5},{8,14},{9,11},{10,... | collective-permute-start | bytes 589832 | tf_op jit(solution)/shard_map/ppermute | solution.py:168
  111.6 2.4 %collective-permute-done.20.refs_2_ = f32[32,1536]{1,0:T(8,128)S(1)} collective-permute-done((f32[32,1536]{1,0:T(8,128)S(1)}, f32[32,1536]{1,0:T(8,128)S(1)}, u32[]{:S(2)}, u32[]{:S(2)}) %collective-permute-start.20) | collective-permute-done | bytes 196640 | tf_op jit(solution)/shard_map/ppermute | solution.py:168
  115.4 4.3 %collective-permute-start.24 = (f32[32,1536]{1,0:T(8,128)S(1)}, f32[32,1536]{1,0:T(8,128)S(1)}, u32[]{:S(2)}, u32[]{:S(2)}) collective-permute-start(f32[32,1536]{1,0:T(8,128)S(1)} %shard_map.154.refs_0_), channel_id=1, source_target_pairs={{0,84},{1,85},{2,86},{3,87},{4,80},{5,81},{6,82},{7,83},{8,92},{9,... | collective-permute-start | bytes 589832 | tf_op jit(solution)/shard_map/ppermute | solution.py:168
  120.8 3.6 %collective-permute-start.22 = (f32[32,1536]{1,0:T(8,128)S(1)}, f32[32,1536]{1,0:T(8,128)S(1)}, u32[]{:S(2)}, u32[]{:S(2)}) collective-permute-start(f32[32,1536]{1,0:T(8,128)S(1)} %shard_map.154.refs_0_), channel_id=1, source_target_pairs={{0,126},{1,127},{2,124},{3,125},{4,122},{5,123},{6,120},{7,121},{8... | collective-permute-start | bytes 589832 | tf_op jit(solution)/shard_map/ppermute | solution.py:168
  124.4 5.6 %collective-permute-done.24.refs_3_ = f32[32,1536]{1,0:T(8,128)S(1)} collective-permute-done((f32[32,1536]{1,0:T(8,128)S(1)}, f32[32,1536]{1,0:T(8,128)S(1)}, u32[]{:S(2)}, u32[]{:S(2)}) %collective-permute-start.24) | collective-permute-done | bytes 196640 | tf_op jit(solution)/shard_map/ppermute | solution.py:168
  130.0 2.6 %collective-permute-done.22.refs_1_ = f32[32,1536]{1,0:T(8,128)S(1)} collective-permute-done((f32[32,1536]{1,0:T(8,128)S(1)}, f32[32,1536]{1,0:T(8,128)S(1)}, u32[]{:S(2)}, u32[]{:S(2)}) %collective-permute-start.22) | collective-permute-done | bytes 196640 | tf_op jit(solution)/shard_map/ppermute | solution.py:168
  134.6 2.4 %collective-permute-start.26 = (f32[32,1536]{1,0:T(8,128)S(1)}, f32[32,1536]{1,0:T(8,128)S(1)}, u32[]{:S(2)}, u32[]{:S(2)}) collective-permute-start(f32[32,1536]{1,0:T(8,128)S(1)} %shard_map.155.a), channel_id=1, source_target_pairs={{0,24},{1,9},{2,26},{3,11},{4,28},{5,13},{6,30},{7,15},{8,16},{9,1... | collective-permute-start | bytes 589832 | tf_op jit(solution)/shard_map/ppermute | solution.py:168
  141.5 3.0 %collective-permute-done.25.b = f32[32,1536]{1,0:T(8,128)S(1)} collective-permute-done((f32[32,1536]{1,0:T(8,128)S(1)}, f32[32,1536]{1,0:T(8,128)S(1)}, u32[]{:S(2)}, u32[]{:S(2)}) %collective-permute-start.25) | collective-permute-done | bytes 196640 | tf_op jit(solution)/shard_map/ppermute | solution.py:168
  145.6 11.6 %collective-permute-done.30.d = f32[128,1536]{1,0:T(8,128)S(1)} collective-permute-done((f32[128,1536]{1,0:T(8,128)S(1)}, f32[128,1536]{1,0:T(8,128)S(1)}, u32[]{:S(2)}, u32[]{:S(2)}) %collective-permute-start.30) | collective-permute-done | bytes 786464 | tf_op jit(solution)/shard_map/ppermute | solution.py:168
  157.6 13.5 %shard_map.157 = (bf16[3,512,512]{2,1,0:T(8,128)(2,1)S(1)}, f32[8,1536]{1,0:T(8,128)S(1)}, f32[128,1536]{1,0:T(8,128)S(1)}, f32[128,1536]{1,0:T(8,128)S(1)}, f32...) custom-call(s32[67]{0:T(128)S(1)} %copy-done.14, ...), custom_call_target="tpu_custom_call" | custom-call | bytes 24965388 | tf_op jit(solution)/shard_map/pallas_call | solution.py:105
  176.7 6.5 %collective-permute-done.31.refs_1_ = f32[128,1536]{1,0:T(8,128)S(1)} collective-permute-done((f32[128,1536]{1,0:T(8,128)S(1)}, f32[128,1536]{1,0:T(8,128)S(1)}, u32[]{:S(2)}, u32[]{:S(2)}) %collective-permute-start.31) | collective-permute-done | bytes 786464 | tf_op jit(solution)/shard_map/ppermute | solution.py:168
  185.2 21.1 %all_to_all.5.pieces = f32[16,8,1536]{2,1,0:T(8,128)S(1)} all-to-all(f32[16,8,1536]{2,1,0:T(8,128)S(1)} %bitcast.22), channel_id=1, replica_groups={{0,6,24,30,42,44,50,52,74,76,82,84,96,102,120,126},{2,4,26,28,40,46,48,..., dimensions={0} | all-to-all | bytes 1572864 | tf_op jit(solution)/shard_map/all_to_all | solution.py:520
  (96 shorter events, 62.7 us)
Async XLA Ops:
  7.2 12.3 %collective-permute-start = (f32[128,1536]{1,0:T(8,128)}, f32[128,1536]{1,0:T(8,128)S(1)}, u32[]{:S(2)}, u32[]{:S(2)}) collective-permute-start(f32[128,1536]{1,0:T(8,128)} %get-tuple-element.65), channel_id=1, source_target_pairs={{0,2},{1,7},{2,0},{3,5},{4,6},{5,3},{6,4},{7,1},{8,10},{9,15},{10,... | collective-permute-start | bytes 2359304 | tf_op jit(solution)/shard_map/ppermute | solution.py:168
  9.3 12.2 %collective-permute-start.1 = (f32[128,1536]{1,0:T(8,128)}, f32[128,1536]{1,0:T(8,128)S(1)}, u32[]{:S(2)}, u32[]{:S(2)}) collective-permute-start(f32[128,1536]{1,0:T(8,128)} %get-tuple-element.66), channel_id=1, source_target_pairs={{0,8},{1,25},{2,10},{3,27},{4,12},{5,29},{6,14},{7,31},{8,0},{9,17... | collective-permute-start | bytes 2359304 | tf_op jit(solution)/shard_map/ppermute | solution.py:168
  10.8 12.2 %collective-permute-start.2 = (f32[128,1536]{1,0:T(8,128)}, f32[128,1536]{1,0:T(8,128)S(1)}, u32[]{:S(2)}, u32[]{:S(2)}) collective-permute-start(f32[128,1536]{1,0:T(8,128)} %get-tuple-element.67), channel_id=1, source_target_pairs={{0,32},{1,97},{2,34},{3,99},{4,36},{5,101},{6,38},{7,103},{8,40},{... | collective-permute-start | bytes 2359304 | tf_op jit(solution)/shard_map/ppermute | solution.py:168
  24.9 7.5 %collective-permute-start.3 = (f32[32,1536]{1,0:T(8,128)S(1)}, f32[32,1536]{1,0:T(8,128)S(1)}, u32[]{:S(2)}, u32[]{:S(2)}) collective-permute-start(f32[32,1536]{1,0:T(8,128)S(1)} %get-tuple-element.69), channel_id=1, source_target_pairs={{0,6},{1,3},{2,4},{3,1},{4,2},{5,7},{6,0},{7,5},{8,14},{9,11},{10,... | collective-permute-start | bytes 589832 | tf_op jit(solution)/shard_map/ppermute | solution.py:168
  36.6 14.7 %collective-permute-start.8 = (f32[32,1536]{1,0:T(8,128)S(1)}, f32[32,1536]{1,0:T(8,128)S(1)}, u32[]{:S(2)}, u32[]{:S(2)}) collective-permute-start(f32[32,1536]{1,0:T(8,128)S(1)} %shard_map.147.refs_0_), channel_id=1, source_target_pairs={{0,84},{1,85},{2,86},{3,87},{4,80},{5,81},{6,82},{7,83},{8,92},{9,... | collective-permute-start | bytes 589832 | tf_op jit(solution)/shard_map/ppermute | solution.py:168
  39.3 11.9 %collective-permute-start.7 = (f32[32,1536]{1,0:T(8,128)S(1)}, f32[32,1536]{1,0:T(8,128)S(1)}, u32[]{:S(2)}, u32[]{:S(2)}) collective-permute-start(f32[32,1536]{1,0:T(8,128)S(1)} %shard_map.147.refs_0_), channel_id=1, source_target_pairs={{0,42},{1,43},{2,40},{3,41},{4,46},{5,47},{6,44},{7,45},{8,34},{9,... | collective-permute-start | bytes 589832 | tf_op jit(solution)/shard_map/ppermute | solution.py:168
  41.5 11.5 %collective-permute-start.6 = (f32[32,1536]{1,0:T(8,128)S(1)}, f32[32,1536]{1,0:T(8,128)S(1)}, u32[]{:S(2)}, u32[]{:S(2)}) collective-permute-start(f32[32,1536]{1,0:T(8,128)S(1)} %shard_map.147.refs_0_), channel_id=1, source_target_pairs={{0,126},{1,127},{2,124},{3,125},{4,122},{5,123},{6,120},{7,121},{8... | collective-permute-start | bytes 589832 | tf_op jit(solution)/shard_map/ppermute | solution.py:168
  53.1 7.9 %collective-permute-start.11 = (f32[32,1536]{1,0:T(8,128)S(1)}, f32[32,1536]{1,0:T(8,128)S(1)}, u32[]{:S(2)}, u32[]{:S(2)}) collective-permute-start(f32[32,1536]{1,0:T(8,128)S(1)} %shard_map.148.a), channel_id=1, source_target_pairs={{0,96},{1,33},{2,98},{3,35},{4,100},{5,37},{6,102},{7,39},{8,104},... | collective-permute-start | bytes 589832 | tf_op jit(solution)/shard_map/ppermute | solution.py:168
  55.8 7.8 %collective-permute-start.10 = (f32[32,1536]{1,0:T(8,128)S(1)}, f32[32,1536]{1,0:T(8,128)S(1)}, u32[]{:S(2)}, u32[]{:S(2)}) collective-permute-start(f32[32,1536]{1,0:T(8,128)S(1)} %shard_map.148.a), channel_id=1, source_target_pairs={{0,24},{1,9},{2,26},{3,11},{4,28},{5,13},{6,30},{7,15},{8,16},{9,1... | collective-permute-start | bytes 589832 | tf_op jit(solution)/shard_map/ppermute | solution.py:168
  64.3 12.1 %collective-permute-start.14 = (f32[128,1536]{1,0:T(8,128)S(1)}, f32[128,1536]{1,0:T(8,128)S(1)}, u32[]{:S(2)}, u32[]{:S(2)}) collective-permute-start(f32[128,1536]{1,0:T(8,128)S(1)} %shard_map.149.a), channel_id=1, source_target_pairs={{0,32},{1,97},{2,34},{3,99},{4,36},{5,101},{6,38},{7,103},{8,40},{... | collective-permute-start | bytes 2359304 | tf_op jit(solution)/shard_map/ppermute | solution.py:168
  64.4 12.1 %collective-permute-start.13 = (f32[128,1536]{1,0:T(8,128)S(1)}, f32[128,1536]{1,0:T(8,128)S(1)}, u32[]{:S(2)}, u32[]{:S(2)}) collective-permute-start(f32[128,1536]{1,0:T(8,128)S(1)} %shard_map.149.a), channel_id=1, source_target_pairs={{0,8},{1,25},{2,10},{3,27},{4,12},{5,29},{6,14},{7,31},{8,0},{9,17... | collective-permute-start | bytes 2359304 | tf_op jit(solution)/shard_map/ppermute | solution.py:168
  64.5 12.3 %collective-permute-start.12 = (f32[128,1536]{1,0:T(8,128)S(1)}, f32[128,1536]{1,0:T(8,128)S(1)}, u32[]{:S(2)}, u32[]{:S(2)}) collective-permute-start(f32[128,1536]{1,0:T(8,128)S(1)} %shard_map.149.a), channel_id=1, source_target_pairs={{0,2},{1,7},{2,0},{3,5},{4,6},{5,3},{6,4},{7,1},{8,10},{9,15},{10,... | collective-permute-start | bytes 2359304 | tf_op jit(solution)/shard_map/ppermute | solution.py:168
  90.0 12.1 %collective-permute-start.16 = (f32[128,1536]{1,0:T(8,128)S(1)}, f32[128,1536]{1,0:T(8,128)S(1)}, u32[]{:S(2)}, u32[]{:S(2)}) collective-permute-start(f32[128,1536]{1,0:T(8,128)S(1)} %get-tuple-element.79), channel_id=1, source_target_pairs={{0,2},{1,7},{2,0},{3,5},{4,6},{5,3},{6,4},{7,1},{8,10},{9,15},{10,... | collective-permute-start | bytes 2359304 | tf_op jit(solution)/shard_map/ppermute | solution.py:168
  90.1 12.1 %collective-permute-start.17 = (f32[128,1536]{1,0:T(8,128)S(1)}, f32[128,1536]{1,0:T(8,128)S(1)}, u32[]{:S(2)}, u32[]{:S(2)}) collective-permute-start(f32[128,1536]{1,0:T(8,128)S(1)} %get-tuple-element.80), channel_id=1, source_target_pairs={{0,8},{1,25},{2,10},{3,27},{4,12},{5,29},{6,14},{7,31},{8,0},{9,17... | collective-permute-start | bytes 2359304 | tf_op jit(solution)/shard_map/ppermute | solution.py:168
  91.9 12.0 %collective-permute-start.18 = (f32[128,1536]{1,0:T(8,128)S(1)}, f32[128,1536]{1,0:T(8,128)S(1)}, u32[]{:S(2)}, u32[]{:S(2)}) collective-permute-start(f32[128,1536]{1,0:T(8,128)S(1)} %get-tuple-element.81), channel_id=1, source_target_pairs={{0,32},{1,97},{2,34},{3,99},{4,36},{5,101},{6,38},{7,103},{8,40},{... | collective-permute-start | bytes 2359304 | tf_op jit(solution)/shard_map/ppermute | solution.py:168
  115.4 14.6 %collective-permute-start.24 = (f32[32,1536]{1,0:T(8,128)S(1)}, f32[32,1536]{1,0:T(8,128)S(1)}, u32[]{:S(2)}, u32[]{:S(2)}) collective-permute-start(f32[32,1536]{1,0:T(8,128)S(1)} %shard_map.154.refs_0_), channel_id=1, source_target_pairs={{0,84},{1,85},{2,86},{3,87},{4,80},{5,81},{6,82},{7,83},{8,92},{9,... | collective-permute-start | bytes 589832 | tf_op jit(solution)/shard_map/ppermute | solution.py:168
  119.7 10.2 %collective-permute-start.23 = (f32[32,1536]{1,0:T(8,128)S(1)}, f32[32,1536]{1,0:T(8,128)S(1)}, u32[]{:S(2)}, u32[]{:S(2)}) collective-permute-start(f32[32,1536]{1,0:T(8,128)S(1)} %shard_map.154.refs_0_), channel_id=1, source_target_pairs={{0,42},{1,43},{2,40},{3,41},{4,46},{5,47},{6,44},{7,45},{8,34},{9,... | collective-permute-start | bytes 589832 | tf_op jit(solution)/shard_map/ppermute | solution.py:168
  120.8 11.7 %collective-permute-start.22 = (f32[32,1536]{1,0:T(8,128)S(1)}, f32[32,1536]{1,0:T(8,128)S(1)}, u32[]{:S(2)}, u32[]{:S(2)}) collective-permute-start(f32[32,1536]{1,0:T(8,128)S(1)} %shard_map.154.refs_0_), channel_id=1, source_target_pairs={{0,126},{1,127},{2,124},{3,125},{4,122},{5,123},{6,120},{7,121},{8... | collective-permute-start | bytes 589832 | tf_op jit(solution)/shard_map/ppermute | solution.py:168
  145.1 12.1 %collective-permute-start.30 = (f32[128,1536]{1,0:T(8,128)S(1)}, f32[128,1536]{1,0:T(8,128)S(1)}, u32[]{:S(2)}, u32[]{:S(2)}) collective-permute-start(f32[128,1536]{1,0:T(8,128)S(1)} %shard_map.156.a), channel_id=1, source_target_pairs={{0,32},{1,97},{2,34},{3,99},{4,36},{5,101},{6,38},{7,103},{8,40},{... | collective-permute-start | bytes 2359304 | tf_op jit(solution)/shard_map/ppermute | solution.py:168
  145.2 12.1 %collective-permute-start.29 = (f32[128,1536]{1,0:T(8,128)S(1)}, f32[128,1536]{1,0:T(8,128)S(1)}, u32[]{:S(2)}, u32[]{:S(2)}) collective-permute-start(f32[128,1536]{1,0:T(8,128)S(1)} %shard_map.156.a), channel_id=1, source_target_pairs={{0,8},{1,25},{2,10},{3,27},{4,12},{5,29},{6,14},{7,31},{8,0},{9,17... | collective-permute-start | bytes 2359304 | tf_op jit(solution)/shard_map/ppermute | solution.py:168
  145.3 12.3 %collective-permute-start.28 = (f32[128,1536]{1,0:T(8,128)S(1)}, f32[128,1536]{1,0:T(8,128)S(1)}, u32[]{:S(2)}, u32[]{:S(2)}) collective-permute-start(f32[128,1536]{1,0:T(8,128)S(1)} %shard_map.156.a), channel_id=1, source_target_pairs={{0,2},{1,7},{2,0},{3,5},{4,6},{5,3},{6,4},{7,1},{8,10},{9,15},{10,... | collective-permute-start | bytes 2359304 | tf_op jit(solution)/shard_map/ppermute | solution.py:168
  171.1 12.1 %collective-permute-start.31 = (f32[128,1536]{1,0:T(8,128)S(1)}, f32[128,1536]{1,0:T(8,128)S(1)}, u32[]{:S(2)}, u32[]{:S(2)}) collective-permute-start(f32[128,1536]{1,0:T(8,128)S(1)} %get-tuple-element.100), channel_id=1, source_target_pairs={{0,2},{1,7},{2,0},{3,5},{4,6},{5,3},{6,4},{7,1},{8,10},{9,15},{10,... | collective-permute-start | bytes 2359304 | tf_op jit(solution)/shard_map/ppermute | solution.py:168
  171.2 12.1 %collective-permute-start.32 = (f32[128,1536]{1,0:T(8,128)S(1)}, f32[128,1536]{1,0:T(8,128)S(1)}, u32[]{:S(2)}, u32[]{:S(2)}) collective-permute-start(f32[128,1536]{1,0:T(8,128)S(1)} %get-tuple-element.101), channel_id=1, source_target_pairs={{0,8},{1,25},{2,10},{3,27},{4,12},{5,29},{6,14},{7,31},{8,0},{9,17... | collective-permute-start | bytes 2359304 | tf_op jit(solution)/shard_map/ppermute | solution.py:168
  173.0 12.0 %collective-permute-start.33 = (f32[128,1536]{1,0:T(8,128)S(1)}, f32[128,1536]{1,0:T(8,128)S(1)}, u32[]{:S(2)}, u32[]{:S(2)}) collective-permute-start(f32[128,1536]{1,0:T(8,128)S(1)} %get-tuple-element.102), channel_id=1, source_target_pairs={{0,32},{1,97},{2,34},{3,99},{4,36},{5,101},{6,38},{7,103},{8,40},{... | collective-permute-start | bytes 2359304 | tf_op jit(solution)/shard_map/ppermute | solution.py:168
  (27 other events, 608.7 us)

commit v4 on v3

--- a/solution.py
+++ b/solution.py
@@ -74,19 +74,26 @@
 
 
 COLOUR_GROUPS = [[2 * t + c for t in of_colour(q, c)] for c in range(2) for q in range(4)]
-TABLE = [
-    [
-        [colour(*at, c == 0), colour(*at, c == 1), t]
-        + [t for q in range(4) for t in of_colour(q, c)]
-        for c in range(2)
-    ]
-    for t, at in enumerate(PLACES)
-]
-
-
-def own_table():
-    table = jnp.asarray(TABLE, jnp.int32)
-    return table[lax.axis_index(TOK), lax.axis_index("head")]
+TOKENS_BY_COLOUR = [[t for q in range(4) for t in of_colour(q, c)] for c in range(2)]
+
+
+def position():
+    return [lax.axis_index(a) for a in TOK], lax.axis_index("head")
+
+
+def own_colour(near):
+    at, core = position()
+    low, high = 0, 0
+    for i in at:
+        low = 2 * low + (((i + 1) >> 1) & 1)
+        high = 2 * high + (i >> 1)
+    code = jnp.where((core == 0) == near, low, high)
+    return jnp.where(code >= 4, 7 - code, code)
+
+
+def own_index():
+    (x, y, z), _ = position()
+    return (x * 4 + y) * 4 + z
 
 
 SMEM = pl.BlockSpec(memory_space=pltpu.SMEM)
@@ -142,10 +149,11 @@
     return slice(index * DH, (index + 1) * DH)
 
 
-def fold_body(own, a, b, c, d, *outs):
+def fold_body(a, b, c, d, *outs):
     rows = outs[0].shape[0]
+    own = own_colour(False)
     for step in range(4):
-        at = rows_at(own[1] ^ step, rows)
+        at = rows_at(own ^ step, rows)
         outs[step][...] = (a[at, :] + b[at, :]) + (c[at, :] + d[at, :])
 
 
@@ -157,10 +165,11 @@
     out[...] = values[0]
 
 
-def join_body(own, a, b, c, d, out):
+def join_body(a, b, c, d, out):
     rows = a.shape[0]
+    own = own_colour(False)
     for step, piece in enumerate((a, b, c, d)):
-        out[rows_at(own[1] ^ step, rows), :] = piece[...]
+        out[rows_at(own ^ step, rows), :] = piece[...]
 
 
 def received(blocks, level):
@@ -173,12 +182,12 @@
     return lax.optimization_barrier((tuple(blocks), done))
 
 
-def sum_everywhere(arrived, own):
+def sum_everywhere(arrived):
     piece_shape = [shape(32, WIDE)]
-    blocks = call(fold_body, piece_shape * 4, *arrived, scalars=own)
+    blocks = call(fold_body, piece_shape * 4, *arrived)
     (piece,) = call(total_body, piece_shape, *received(blocks, 2))
     (piece,) = call(total_body, piece_shape, *received([piece] * 4, 3))
-    (piece,) = call(join_body, [shape(128, WIDE)], *received([piece] * 4, 2), scalars=own)
+    (piece,) = call(join_body, [shape(128, WIDE)], *received([piece] * 4, 2))
     return received([piece] * 4, 1)
 
 
@@ -193,7 +202,7 @@
     return jnp.transpose(jnp.broadcast_to(row, (128, row.shape[1])))[:, :1]
 
 
-def key_body(own, *refs):
+def key_body(*refs):
     sources, outs, finals = refs[:6], refs[6:10], refs[10:17]
     copies, stored, whole, in_sems, out_sems = refs[17:23], refs[23:30], *refs[30:]
     moves = [
@@ -205,6 +214,7 @@
     keys, w_gate, w_up, rates, values, w_down = copies
     gate, up, mid, mixed, target, dgate, dup = stored
     sent = []
+    own = own_colour(True)
 
     def send(source, goal):
         sent.append(pltpu.make_async_copy(source, goal, out_sems.at[len(sent)]))
@@ -216,7 +226,7 @@
 
     def send_quarters(index):
         for step in range(4):
-            at = (rows_at(own[0] ^ step, DH // 4), columns(index))
+            at = (rows_at(own ^ step, DH // 4), columns(index))
             send(whole.at[at], outs[step].at[:, columns(index)])
 
     moves[0].wait()
@@ -269,7 +279,7 @@
 
 
 def query_terms_body(
-    own, w_down, queries, cotangent, gain, stats, other, output, act, slope, mixed, *refs
+    w_down, queries, cotangent, gain, stats, other, output, act, slope, mixed, *refs
 ):
     outs, dgate, dup, whole = refs[:4], refs[4], refs[5], refs[6]
     both = stats[...] + other[...]
@@ -288,7 +298,7 @@
     whole[:, 2 * DH :] = tn(mixed[...], grad_output)
     whole[:, :DH] = tn(q, dg)
     whole[:, DH : 2 * DH] = tn(q, du)
-    hand_out(own[0], whole, outs, DH // 4)
+    hand_out(own_colour(True), whole, outs, DH // 4)
 
 
 def query_grad_body(new, dgate, dup, query_grad):
@@ -340,11 +350,28 @@
 EACH = range(3)
 
 
-def ortho_body(own, a, b, c, d, w_gate, w_up, w_down, queries, cotangent, gain, *refs):
+HALF = DH // 2
+
+
+def symmetric_product(ref, product, full, added, low):
+    value = ref[...]
+    for rows, cols in ((slice(0, HALF), slice(0, DH)), (slice(HALF, DH), slice(HALF, DH))):
+        other = value[cols] if product is nt else value[:, cols]
+        block = product(value[rows], other)
+        if added is not None:
+            block = coef_second * added[rows, cols] + coef_third * block
+        if full is not None:
+            full[rows, cols] = block
+        low[rows, cols] = block.astype(BF)
+    low[HALF:, :HALF] = jnp.transpose(low[:HALF, HALF:])
+
+
+def ortho_body(a, b, c, d, w_gate, w_up, w_down, queries, cotangent, gain, *refs):
     new, kept, norm, query_refs, (current, gram) = refs[0], refs[1], refs[2], refs[3:8], refs[8:]
+    own = own_colour(True)
     for step, block in enumerate((a, b, c, d)):
         for i in EACH:
-            current[i, rows_at(own[0] ^ step, DH // 4), :] = block[:, columns(i)]
+            current[i, rows_at(own ^ step, DH // 4), :] = block[:, columns(i)]
     for i in EACH:
         matrix = current[i]
         root = jnp.sqrt(jnp.sum(matrix * matrix, keepdims=True) + 1e-06)
@@ -354,13 +381,9 @@
         kept[i, 0] = unit.astype(BF)
     for step in range(NS_STEPS):
         for i in EACH:
-            narrow = kept[i, 3 * step]
-            square = nt(narrow, narrow)
-            gram[i] = square
-            kept[i, 3 * step + 1] = square.astype(BF)
-        for i in EACH:
-            low = kept[i, 3 * step + 1]
-            kept[i, 3 * step + 2] = (coef_second * gram[i] + coef_third * nn(low, low)).astype(BF)
+            symmetric_product(kept.at[i, 3 * step], nt, gram.at[i], None, kept.at[i, 3 * step + 1])
+        for i in EACH:
+            symmetric_product(kept.at[i, 3 * step + 1], nn, None, gram.at[i], kept.at[i, 3 * step + 2])
         for i, weight in enumerate((w_gate, w_up, w_down)):
             later = coef_first * current[i] + nn(kept[i, 3 * step + 2], kept[i, 3 * step])
             if step < NS_STEPS - 1:
@@ -371,14 +394,15 @@
     query_forward(new, queries, cotangent, gain, *query_refs)
 
 
-def ortho_back_body(own, a, b, c, d, kept, norm, keys, gate, up, mid, target, *refs):
+def ortho_back_body(by_colour, a, b, c, d, kept, norm, keys, gate, up, mid, target, *refs):
     cots, share, outs, key_refs = refs[0], refs[1], refs[2:6], refs[6:9]
     grad, grad_low, half, sym, terms = refs[9:]
+    near = own_colour(True)
     for step, block in enumerate((a, b, c, d)):
         for i in EACH:
-            grad[i, rows_at(own[0] ^ step, DH // 4), :] = block[:, columns(i)]
+            grad[i, rows_at(near ^ step, DH // 4), :] = block[:, columns(i)]
     for i in EACH:
-        share[:, columns(i)] = grad[i, rows_at(own[2], 8), :]
+        share[:, columns(i)] = grad[i, rows_at(own_index(), 8), :]
         start = grad[i] * (-inner_step)
         grad[i] = start
         grad_low[i] = start.astype(BF)
@@ -408,9 +432,9 @@
         cots[i] = ((grad[i] - unit * along) * (1.0 / norm[i, :1, :1])).astype(BF)
     key_terms(cots, keys, gate, up, mid, target, *key_refs, terms)
     for step in range(4):
-        first = 3 + 16 * (own[0] ^ step)
+        first = 16 * (near ^ step)
         for j in range(16):
-            outs[step][8 * j : 8 * j + 8, :] = terms[rows_at(own[first + j], 8), :]
+            outs[step][8 * j : 8 * j + 8, :] = terms[rows_at(by_colour[first + j], 8), :]
 
 
 def local(queries, key_rows, value_rows, step_rates, w_gate, w_up, w_down, out_gain, cotangent):
@@ -419,8 +443,6 @@
         a[0] for a in (queries, key_rows, value_rows, cotangent)
     )
     w_gate, w_up, w_down = w_gate[0], w_up[0], w_down[0]
-    own = own_table()
-
     whole = pltpu.VMEM((DH, WIDE), F32)
     quarters = [shape(DH // 4, WIDE)] * 4
     wide = shape(tokens, DH)
@@ -440,11 +462,12 @@
             pltpu.SemaphoreType.DMA((6,)),
             pltpu.SemaphoreType.DMA((19,)),
         ],
-        scalars=own,
         specs=[HBM] * 6,
         out_specs=[HBM] * 11,
         limit=56 * 1024 * 1024,
     )
+    arrived, (mine,) = with_other(received(blocks, 1), call(total_body, quarters[:1], blocks[0]))
+    arrived = (mine, *arrived[1:])
     new, kept, norm, stats, *query_stored = call(
         ortho_body,
         [
@@ -457,14 +480,13 @@
             wide,
             low,
         ],
-        *sum_everywhere(received(blocks, 1), own),
+        *sum_everywhere(arrived),
         w_gate,
         w_up,
         w_down,
         queries,
         cotangent,
         out_gain,
-        scalars=own,
         scratch=[three_f32, three_f32],
     )
     other = lax.ppermute(stats, ALL, OTHER_CORE)
@@ -479,8 +501,11 @@
         other,
         *query_stored,
         scratch=[whole],
-        scalars=own,
-    )
+    )
+    by_colour, query_dup = lax.optimization_barrier(
+        (jnp.asarray(TOKENS_BY_COLOUR, jnp.int32), query_dup)
+    )
+    by_colour = by_colour[lax.axis_index("head")]
     query_grad = call(
         query_grad_body, [low], new, query_dgate, query_dup, flops=4 * tokens * DH * DH
     )
@@ -488,7 +513,7 @@
     cots, share, *blocks, back_mid, gate_back, up_back = call(
         ortho_back_body,
         [three, shape(8, WIDE), *quarters, low, low, low],
-        *sum_everywhere(blocks, own),
+        *sum_everywhere(blocks),
         kept,
         norm,
         key_rows,
@@ -496,7 +521,7 @@
         up,
         mid,
         target,
-        scalars=own,
+        scalars=by_colour,
         scratch=[three_f32, three_low, three_f32, three_low, whole],
     )
     key_grads = call(

time: 207 us -> 216 us (1.043)
  local copies, waits for them, and re-layouts: 2.41 us -> 15.3 us
  Pallas kernels: 37.1 us -> 32.9 us
    unnamed x34 -> x38, local copies, waits for them, and re-layouts: 1.21 us -> 15.3 us
    pallas_call x16 -> x17, Pallas kernels: 37.1 us -> 32.9 us  [call(): pl.pallas_call(body, out_shape=list(outs), in_specs=specs, out_specs=out_...]
where the time goes in v4:
time: 216 us; the launch traced here: 215 us
  waiting for transfers between devices  89.7 us (42%)
  starting transfers between devices  55.3 us (26%)
  Pallas kernels  32.9 us (15%)
  blocking collectives  21.1 us (10%)
  local copies, waits for them, and re-layouts  15.3 us (7%)
    ppermute x33, waiting for transfers between devices, received(): lax.ppermute(blocks[step], ALL, PARTNERS[level, step])  88.3 us
    ppermute x33, starting transfers between devices, received(): lax.ppermute(blocks[step], ALL, PARTNERS[level, step])  55.3 us
    pallas_call x17, Pallas kernels, call(): pl.pallas_call(body, out_shape=list(outs), in_specs=specs, out_specs=out_...  32.9 us
    all_to_all x1, blocking collectives, local(): lax.all_to_all(quarter.reshape(16, 8, WIDE), ALL, 0, 0, axis_index_groups...  21.1 us
    unnamed x38, local copies, waits for them, and re-layouts  15.3 us
  transfers between devices with their start and end apart: 34, of which 31 were waited for; matrix products, arithmetic and copies ran while one was open for 0% of the time, Pallas kernels for 1%

profile of v4, /device:TPU:0, one launch (start us, length us, event | category | flops | bytes accessed | tf_op | source)
XLA Modules:
  0.0 215.3 jit_solution(1484194571074085915)
XLA Ops:
  0.6 4.5 %shard_map.145 = (f32[128,1536]{1,0:T(8,128)}, f32[128,1536]{1,0:T(8,128)}, f32[128,1536]{1,0:T(8,128)}, f32[128,1536]{1,0:T(8,128)}, f32[256,512]{1,0:T(8,128)}...) custom-call(bf16[256,512]{1,0:T(8,128)(2,1)} %bitcast.23, ...), custom_call_target="tpu_custom_call" | custom-call | bytes 7865344 | tf_op jit(solution)/shard_map/pallas_call | solution.py:112
  11.5 5.9 %collective-permute-done.b = f32[128,1536]{1,0:T(8,128)S(1)} collective-permute-done((f32[128,1536]{1,0:T(8,128)}, f32[128,1536]{1,0:T(8,128)S(1)}, u32[]{:S(2)}, u32[]{:S(2)}) %collective-permute-start) | collective-permute-done | bytes 786464 | tf_op jit(solution)/shard_map/ppermute | solution.py:177
  21.2 2.6 %collective-permute-start.3 = (f32[32,1536]{1,0:T(8,128)S(1)}, f32[32,1536]{1,0:T(8,128)S(1)}, u32[]{:S(2)}, u32[]{:S(2)}) collective-permute-start(f32[32,1536]{1,0:T(8,128)S(1)} %get-tuple-element.79), channel_id=1, source_target_pairs={{0,6},{1,3},{2,4},{3,1},{4,2},{5,7},{6,0},{7,5},{8,14},{9,11},{10,... | collective-permute-start | bytes 589832 | tf_op jit(solution)/shard_map/ppermute | solution.py:177
  26.0 2.8 %collective-permute-start.5 = (f32[32,1536]{1,0:T(8,128)S(1)}, f32[32,1536]{1,0:T(8,128)S(1)}, u32[]{:S(2)}, u32[]{:S(2)}) collective-permute-start(f32[32,1536]{1,0:T(8,128)S(1)} %get-tuple-element.81), channel_id=1, source_target_pairs={{0,96},{1,33},{2,98},{3,35},{4,100},{5,37},{6,102},{7,39},{8,104},... | collective-permute-start | bytes 589832 | tf_op jit(solution)/shard_map/ppermute | solution.py:177
  33.0 2.7 %collective-permute-start.8 = (f32[32,1536]{1,0:T(8,128)S(1)}, f32[32,1536]{1,0:T(8,128)S(1)}, u32[]{:S(2)}, u32[]{:S(2)}) collective-permute-start(f32[32,1536]{1,0:T(8,128)S(1)} %shard_map.148.refs_0_), channel_id=1, source_target_pairs={{0,84},{1,85},{2,86},{3,87},{4,80},{5,81},{6,82},{7,83},{8,92},{9,... | collective-permute-start | bytes 589832 | tf_op jit(solution)/shard_map/ppermute | solution.py:177
  37.9 4.1 %collective-permute-start.6 = (f32[32,1536]{1,0:T(8,128)S(1)}, f32[32,1536]{1,0:T(8,128)S(1)}, u32[]{:S(2)}, u32[]{:S(2)}) collective-permute-start(f32[32,1536]{1,0:T(8,128)S(1)} %shard_map.148.refs_0_), channel_id=1, source_target_pairs={{0,126},{1,127},{2,124},{3,125},{4,122},{5,123},{6,120},{7,121},{8... | collective-permute-start | bytes 589832 | tf_op jit(solution)/shard_map/ppermute | solution.py:177
  41.9 5.7 %collective-permute-done.8.refs_3_ = f32[32,1536]{1,0:T(8,128)S(1)} collective-permute-done((f32[32,1536]{1,0:T(8,128)S(1)}, f32[32,1536]{1,0:T(8,128)S(1)}, u32[]{:S(2)}, u32[]{:S(2)}) %collective-permute-start.8) | collective-permute-done | bytes 196640 | tf_op jit(solution)/shard_map/ppermute | solution.py:177
  49.4 2.7 %collective-permute-start.11 = (f32[32,1536]{1,0:T(8,128)S(1)}, f32[32,1536]{1,0:T(8,128)S(1)}, u32[]{:S(2)}, u32[]{:S(2)}) collective-permute-start(f32[32,1536]{1,0:T(8,128)S(1)} %shard_map.149.a), channel_id=1, source_target_pairs={{0,96},{1,33},{2,98},{3,35},{4,100},{5,37},{6,102},{7,39},{8,104},... | collective-permute-start | bytes 589832 | tf_op jit(solution)/shard_map/ppermute | solution.py:177
  55.1 2.8 %collective-permute-done.11.d = f32[32,1536]{1,0:T(8,128)S(1)} collective-permute-done((f32[32,1536]{1,0:T(8,128)S(1)}, f32[32,1536]{1,0:T(8,128)S(1)}, u32[]{:S(2)}, u32[]{:S(2)}) %collective-permute-start.11) | collective-permute-done | bytes 196640 | tf_op jit(solution)/shard_map/ppermute | solution.py:177
  57.9 2.6 %collective-permute-done.10.c = f32[32,1536]{1,0:T(8,128)S(1)} collective-permute-done((f32[32,1536]{1,0:T(8,128)S(1)}, f32[32,1536]{1,0:T(8,128)S(1)}, u32[]{:S(2)}, u32[]{:S(2)}) %collective-permute-start.10) | collective-permute-done | bytes 196640 | tf_op jit(solution)/shard_map/ppermute | solution.py:177
  61.2 11.6 %collective-permute-done.14.d = f32[128,1536]{1,0:T(8,128)S(1)} collective-permute-done((f32[128,1536]{1,0:T(8,128)S(1)}, f32[128,1536]{1,0:T(8,128)S(1)}, u32[]{:S(2)}, u32[]{:S(2)}) %collective-permute-start.14) | collective-permute-done | bytes 786464 | tf_op jit(solution)/shard_map/ppermute | solution.py:177
  73.2 8.6 %shard_map.151 = (bf16[3,512,512]{2,1,0:T(8,128)(2,1)S(1)}, bf16[3,9,512,512]{3,2,1,0:T(8,128)(2,1)S(1)}, f32[3,8,128]{2,1,0:T(8,128)S(1)}, f32[256,128]{1,0:T(8...) custom-call(f32[128,1536]{1,0:T(8,128)S(1)} %shard_map.150.a, ...), custom_call_target="tpu_custom_call" | custom-call | bytes 22951936 | tf_op jit(solution)/shard_map/pallas_call | solution.py:112
  81.8 5.0 %copy-done = bf16[3,9,512,512]{3,2,1,0:T(8,128)(2,1)} copy-done((bf16[3,9,512,512]{3,2,1,0:T(8,128)(2,1)}, bf16[3,9,512,512]{3,2,1,0:T(8,128)(2,1)S(1)}, u32[]{:S(2)}) %copy-start) | copy-done | bytes 14155800
  94.3 7.0 %collective-permute-done.16.b = f32[128,1536]{1,0:T(8,128)S(1)} collective-permute-done((f32[128,1536]{1,0:T(8,128)S(1)}, f32[128,1536]{1,0:T(8,128)S(1)}, u32[]{:S(2)}, u32[]{:S(2)}) %collective-permute-start.16) | collective-permute-done | bytes 786464 | tf_op jit(solution)/shard_map/ppermute | solution.py:177
  114.1 4.3 %collective-permute-start.24 = (f32[32,1536]{1,0:T(8,128)S(1)}, f32[32,1536]{1,0:T(8,128)S(1)}, u32[]{:S(2)}, u32[]{:S(2)}) collective-permute-start(f32[32,1536]{1,0:T(8,128)S(1)} %shard_map.155.refs_0_), channel_id=1, source_target_pairs={{0,84},{1,85},{2,86},{3,87},{4,80},{5,81},{6,82},{7,83},{8,92},{9,... | collective-permute-start | bytes 589832 | tf_op jit(solution)/shard_map/ppermute | solution.py:177
  119.4 3.6 %collective-permute-start.22 = (f32[32,1536]{1,0:T(8,128)S(1)}, f32[32,1536]{1,0:T(8,128)S(1)}, u32[]{:S(2)}, u32[]{:S(2)}) collective-permute-start(f32[32,1536]{1,0:T(8,128)S(1)} %shard_map.155.refs_0_), channel_id=1, source_target_pairs={{0,126},{1,127},{2,124},{3,125},{4,122},{5,123},{6,120},{7,121},{8... | collective-permute-start | bytes 589832 | tf_op jit(solution)/shard_map/ppermute | solution.py:177
  123.0 5.6 %collective-permute-done.24.refs_3_ = f32[32,1536]{1,0:T(8,128)S(1)} collective-permute-done((f32[32,1536]{1,0:T(8,128)S(1)}, f32[32,1536]{1,0:T(8,128)S(1)}, u32[]{:S(2)}, u32[]{:S(2)}) %collective-permute-start.24) | collective-permute-done | bytes 196640 | tf_op jit(solution)/shard_map/ppermute | solution.py:177
  128.6 2.7 %collective-permute-done.22.refs_1_ = f32[32,1536]{1,0:T(8,128)S(1)} collective-permute-done((f32[32,1536]{1,0:T(8,128)S(1)}, f32[32,1536]{1,0:T(8,128)S(1)}, u32[]{:S(2)}, u32[]{:S(2)}) %collective-permute-start.22) | collective-permute-done | bytes 196640 | tf_op jit(solution)/shard_map/ppermute | solution.py:177
  140.0 3.3 %collective-permute-done.25.b = f32[32,1536]{1,0:T(8,128)S(1)} collective-permute-done((f32[32,1536]{1,0:T(8,128)S(1)}, f32[32,1536]{1,0:T(8,128)S(1)}, u32[]{:S(2)}, u32[]{:S(2)}) %collective-permute-start.25) | collective-permute-done | bytes 196640 | tf_op jit(solution)/shard_map/ppermute | solution.py:177
  143.8 11.8 %collective-permute-done.30.d = f32[128,1536]{1,0:T(8,128)S(1)} collective-permute-done((f32[128,1536]{1,0:T(8,128)S(1)}, f32[128,1536]{1,0:T(8,128)S(1)}, u32[]{:S(2)}, u32[]{:S(2)}) %collective-permute-start.30) | collective-permute-done | bytes 786464 | tf_op jit(solution)/shard_map/ppermute | solution.py:177
  155.8 5.0 %copy-done.1 = bf16[3,9,512,512]{3,2,1,0:T(8,128)(2,1)S(1)} copy-done((bf16[3,9,512,512]{3,2,1,0:T(8,128)(2,1)S(1)}, bf16[3,9,512,512]{3,2,1,0:T(8,128)(2,1)}, u32[]{:S(2)}) %copy-start.1) | copy-done | bytes 14155800
  164.9 14.3 %shard_map.158 = (bf16[3,512,512]{2,1,0:T(8,128)(2,1)S(1)}, f32[8,1536]{1,0:T(8,128)S(1)}, f32[128,1536]{1,0:T(8,128)S(1)}, f32[128,1536]{1,0:T(8,128)S(1)}, f32...) custom-call(s32[64]{0:T(128)S(1)} %dynamic-slice_bitcast_fusion.by_c, ...), custom_call_target="tpu_custom_call" | custom-call | bytes 24965376 | tf_op jit(solution)/shard_map/pallas_call | solution.py:112
  185.0 6.3 %collective-permute-done.31.refs_1_ = f32[128,1536]{1,0:T(8,128)S(1)} collective-permute-done((f32[128,1536]{1,0:T(8,128)S(1)}, f32[128,1536]{1,0:T(8,128)S(1)}, u32[]{:S(2)}, u32[]{:S(2)}) %collective-permute-start.31) | collective-permute-done | bytes 786464 | tf_op jit(solution)/shard_map/ppermute | solution.py:177
  193.5 21.1 %all_to_all.5.pieces = f32[16,8,1536]{2,1,0:T(8,128)S(1)} all-to-all(f32[16,8,1536]{2,1,0:T(8,128)S(1)} %bitcast.22), channel_id=1, replica_groups={{0,6,24,30,42,44,50,52,74,76,82,84,96,102,120,126},{2,4,26,28,40,46,48,..., dimensions={0} | all-to-all | bytes 1572864 | tf_op jit(solution)/shard_map/all_to_all | solution.py:545
  (101 shorter events, 67.6 us)
Async XLA Ops:
  5.2 12.3 %collective-permute-start = (f32[128,1536]{1,0:T(8,128)}, f32[128,1536]{1,0:T(8,128)S(1)}, u32[]{:S(2)}, u32[]{:S(2)}) collective-permute-start(f32[128,1536]{1,0:T(8,128)} %get-tuple-element.71), channel_id=1, source_target_pairs={{0,2},{1,7},{2,0},{3,5},{4,6},{5,3},{6,4},{7,1},{8,10},{9,15},{10,... | collective-permute-start | bytes 2359304 | tf_op jit(solution)/shard_map/ppermute | solution.py:177
  7.3 12.2 %collective-permute-start.1 = (f32[128,1536]{1,0:T(8,128)}, f32[128,1536]{1,0:T(8,128)S(1)}, u32[]{:S(2)}, u32[]{:S(2)}) collective-permute-start(f32[128,1536]{1,0:T(8,128)} %get-tuple-element.72), channel_id=1, source_target_pairs={{0,8},{1,25},{2,10},{3,27},{4,12},{5,29},{6,14},{7,31},{8,0},{9,17... | collective-permute-start | bytes 2359304 | tf_op jit(solution)/shard_map/ppermute | solution.py:177
  8.8 12.2 %collective-permute-start.2 = (f32[128,1536]{1,0:T(8,128)}, f32[128,1536]{1,0:T(8,128)S(1)}, u32[]{:S(2)}, u32[]{:S(2)}) collective-permute-start(f32[128,1536]{1,0:T(8,128)} %get-tuple-element.73), channel_id=1, source_target_pairs={{0,32},{1,97},{2,34},{3,99},{4,36},{5,101},{6,38},{7,103},{8,40},{... | collective-permute-start | bytes 2359304 | tf_op jit(solution)/shard_map/ppermute | solution.py:177
  33.0 14.7 %collective-permute-start.8 = (f32[32,1536]{1,0:T(8,128)S(1)}, f32[32,1536]{1,0:T(8,128)S(1)}, u32[]{:S(2)}, u32[]{:S(2)}) collective-permute-start(f32[32,1536]{1,0:T(8,128)S(1)} %shard_map.148.refs_0_), channel_id=1, source_target_pairs={{0,84},{1,85},{2,86},{3,87},{4,80},{5,81},{6,82},{7,83},{8,92},{9,... | collective-permute-start | bytes 589832 | tf_op jit(solution)/shard_map/ppermute | solution.py:177
  35.7 11.9 %collective-permute-start.7 = (f32[32,1536]{1,0:T(8,128)S(1)}, f32[32,1536]{1,0:T(8,128)S(1)}, u32[]{:S(2)}, u32[]{:S(2)}) collective-permute-start(f32[32,1536]{1,0:T(8,128)S(1)} %shard_map.148.refs_0_), channel_id=1, source_target_pairs={{0,42},{1,43},{2,40},{3,41},{4,46},{5,47},{6,44},{7,45},{8,34},{9,... | collective-permute-start | bytes 589832 | tf_op jit(solution)/shard_map/ppermute | solution.py:177
  37.9 11.5 %collective-permute-start.6 = (f32[32,1536]{1,0:T(8,128)S(1)}, f32[32,1536]{1,0:T(8,128)S(1)}, u32[]{:S(2)}, u32[]{:S(2)}) collective-permute-start(f32[32,1536]{1,0:T(8,128)S(1)} %shard_map.148.refs_0_), channel_id=1, source_target_pairs={{0,126},{1,127},{2,124},{3,125},{4,122},{5,123},{6,120},{7,121},{8... | collective-permute-start | bytes 589832 | tf_op jit(solution)/shard_map/ppermute | solution.py:177
  49.4 8.5 %collective-permute-start.11 = (f32[32,1536]{1,0:T(8,128)S(1)}, f32[32,1536]{1,0:T(8,128)S(1)}, u32[]{:S(2)}, u32[]{:S(2)}) collective-permute-start(f32[32,1536]{1,0:T(8,128)S(1)} %shard_map.149.a), channel_id=1, source_target_pairs={{0,96},{1,33},{2,98},{3,35},{4,100},{5,37},{6,102},{7,39},{8,104},... | collective-permute-start | bytes 589832 | tf_op jit(solution)/shard_map/ppermute | solution.py:177
  52.1 8.4 %collective-permute-start.10 = (f32[32,1536]{1,0:T(8,128)S(1)}, f32[32,1536]{1,0:T(8,128)S(1)}, u32[]{:S(2)}, u32[]{:S(2)}) collective-permute-start(f32[32,1536]{1,0:T(8,128)S(1)} %shard_map.149.a), channel_id=1, source_target_pairs={{0,24},{1,9},{2,26},{3,11},{4,28},{5,13},{6,30},{7,15},{8,16},{9,1... | collective-permute-start | bytes 589832 | tf_op jit(solution)/shard_map/ppermute | solution.py:177
  52.8 7.8 %collective-permute-start.9 = (f32[32,1536]{1,0:T(8,128)S(1)}, f32[32,1536]{1,0:T(8,128)S(1)}, u32[]{:S(2)}, u32[]{:S(2)}) collective-permute-start(f32[32,1536]{1,0:T(8,128)S(1)} %shard_map.149.a), channel_id=1, source_target_pairs={{0,6},{1,3},{2,4},{3,1},{4,2},{5,7},{6,0},{7,5},{8,14},{9,11},{10,... | collective-permute-start | bytes 589832 | tf_op jit(solution)/shard_map/ppermute | solution.py:177
  60.7 12.1 %collective-permute-start.14 = (f32[128,1536]{1,0:T(8,128)S(1)}, f32[128,1536]{1,0:T(8,128)S(1)}, u32[]{:S(2)}, u32[]{:S(2)}) collective-permute-start(f32[128,1536]{1,0:T(8,128)S(1)} %shard_map.150.a), channel_id=1, source_target_pairs={{0,32},{1,97},{2,34},{3,99},{4,36},{5,101},{6,38},{7,103},{8,40},{... | collective-permute-start | bytes 2359304 | tf_op jit(solution)/shard_map/ppermute | solution.py:177
  60.8 12.1 %collective-permute-start.13 = (f32[128,1536]{1,0:T(8,128)S(1)}, f32[128,1536]{1,0:T(8,128)S(1)}, u32[]{:S(2)}, u32[]{:S(2)}) collective-permute-start(f32[128,1536]{1,0:T(8,128)S(1)} %shard_map.150.a), channel_id=1, source_target_pairs={{0,8},{1,25},{2,10},{3,27},{4,12},{5,29},{6,14},{7,31},{8,0},{9,17... | collective-permute-start | bytes 2359304 | tf_op jit(solution)/shard_map/ppermute | solution.py:177
  60.9 12.3 %collective-permute-start.12 = (f32[128,1536]{1,0:T(8,128)S(1)}, f32[128,1536]{1,0:T(8,128)S(1)}, u32[]{:S(2)}, u32[]{:S(2)}) collective-permute-start(f32[128,1536]{1,0:T(8,128)S(1)} %shard_map.150.a), channel_id=1, source_target_pairs={{0,2},{1,7},{2,0},{3,5},{4,6},{5,3},{6,4},{7,1},{8,10},{9,15},{10,... | collective-permute-start | bytes 2359304 | tf_op jit(solution)/shard_map/ppermute | solution.py:177
  89.3 12.1 %collective-permute-start.16 = (f32[128,1536]{1,0:T(8,128)S(1)}, f32[128,1536]{1,0:T(8,128)S(1)}, u32[]{:S(2)}, u32[]{:S(2)}) collective-permute-start(f32[128,1536]{1,0:T(8,128)S(1)} %get-tuple-element.89), channel_id=1, source_target_pairs={{0,2},{1,7},{2,0},{3,5},{4,6},{5,3},{6,4},{7,1},{8,10},{9,15},{10,... | collective-permute-start | bytes 2359304 | tf_op jit(solution)/shard_map/ppermute | solution.py:177
  89.4 12.1 %collective-permute-start.17 = (f32[128,1536]{1,0:T(8,128)S(1)}, f32[128,1536]{1,0:T(8,128)S(1)}, u32[]{:S(2)}, u32[]{:S(2)}) collective-permute-start(f32[128,1536]{1,0:T(8,128)S(1)} %get-tuple-element.90), channel_id=1, source_target_pairs={{0,8},{1,25},{2,10},{3,27},{4,12},{5,29},{6,14},{7,31},{8,0},{9,17... | collective-permute-start | bytes 2359304 | tf_op jit(solution)/shard_map/ppermute | solution.py:177
  91.2 12.0 %collective-permute-start.18 = (f32[128,1536]{1,0:T(8,128)S(1)}, f32[128,1536]{1,0:T(8,128)S(1)}, u32[]{:S(2)}, u32[]{:S(2)}) collective-permute-start(f32[128,1536]{1,0:T(8,128)S(1)} %get-tuple-element.91), channel_id=1, source_target_pairs={{0,32},{1,97},{2,34},{3,99},{4,36},{5,101},{6,38},{7,103},{8,40},{... | collective-permute-start | bytes 2359304 | tf_op jit(solution)/shard_map/ppermute | solution.py:177
  114.1 14.6 %collective-permute-start.24 = (f32[32,1536]{1,0:T(8,128)S(1)}, f32[32,1536]{1,0:T(8,128)S(1)}, u32[]{:S(2)}, u32[]{:S(2)}) collective-permute-start(f32[32,1536]{1,0:T(8,128)S(1)} %shard_map.155.refs_0_), channel_id=1, source_target_pairs={{0,84},{1,85},{2,86},{3,87},{4,80},{5,81},{6,82},{7,83},{8,92},{9,... | collective-permute-start | bytes 589832 | tf_op jit(solution)/shard_map/ppermute | solution.py:177
  118.3 10.3 %collective-permute-start.23 = (f32[32,1536]{1,0:T(8,128)S(1)}, f32[32,1536]{1,0:T(8,128)S(1)}, u32[]{:S(2)}, u32[]{:S(2)}) collective-permute-start(f32[32,1536]{1,0:T(8,128)S(1)} %shard_map.155.refs_0_), channel_id=1, source_target_pairs={{0,42},{1,43},{2,40},{3,41},{4,46},{5,47},{6,44},{7,45},{8,34},{9,... | collective-permute-start | bytes 589832 | tf_op jit(solution)/shard_map/ppermute | solution.py:177
  119.4 11.9 %collective-permute-start.22 = (f32[32,1536]{1,0:T(8,128)S(1)}, f32[32,1536]{1,0:T(8,128)S(1)}, u32[]{:S(2)}, u32[]{:S(2)}) collective-permute-start(f32[32,1536]{1,0:T(8,128)S(1)} %shard_map.155.refs_0_), channel_id=1, source_target_pairs={{0,126},{1,127},{2,124},{3,125},{4,122},{5,123},{6,120},{7,121},{8... | collective-permute-start | bytes 589832 | tf_op jit(solution)/shard_map/ppermute | solution.py:177
  143.5 12.1 %collective-permute-start.30 = (f32[128,1536]{1,0:T(8,128)S(1)}, f32[128,1536]{1,0:T(8,128)S(1)}, u32[]{:S(2)}, u32[]{:S(2)}) collective-permute-start(f32[128,1536]{1,0:T(8,128)S(1)} %shard_map.157.a), channel_id=1, source_target_pairs={{0,32},{1,97},{2,34},{3,99},{4,36},{5,101},{6,38},{7,103},{8,40},{... | collective-permute-start | bytes 2359304 | tf_op jit(solution)/shard_map/ppermute | solution.py:177
  143.6 12.2 %collective-permute-start.29 = (f32[128,1536]{1,0:T(8,128)S(1)}, f32[128,1536]{1,0:T(8,128)}, u32[]{:S(2)}, u32[]{:S(2)}) collective-permute-start(f32[128,1536]{1,0:T(8,128)S(1)} %shard_map.157.a), channel_id=1, source_target_pairs={{0,8},{1,25},{2,10},{3,27},{4,12},{5,29},{6,14},{7,31},{8,0},{9,17... | collective-permute-start | bytes 2359304 | tf_op jit(solution)/shard_map/ppermute | solution.py:177
  143.7 12.2 %collective-permute-start.28 = (f32[128,1536]{1,0:T(8,128)S(1)}, f32[128,1536]{1,0:T(8,128)}, u32[]{:S(2)}, u32[]{:S(2)}) collective-permute-start(f32[128,1536]{1,0:T(8,128)S(1)} %shard_map.157.a), channel_id=1, source_target_pairs={{0,2},{1,7},{2,0},{3,5},{4,6},{5,3},{6,4},{7,1},{8,10},{9,15},{10,... | collective-permute-start | bytes 2359304 | tf_op jit(solution)/shard_map/ppermute | solution.py:177
  179.2 12.1 %collective-permute-start.31 = (f32[128,1536]{1,0:T(8,128)S(1)}, f32[128,1536]{1,0:T(8,128)S(1)}, u32[]{:S(2)}, u32[]{:S(2)}) collective-permute-start(f32[128,1536]{1,0:T(8,128)S(1)} %get-tuple-element.112), channel_id=1, source_target_pairs={{0,2},{1,7},{2,0},{3,5},{4,6},{5,3},{6,4},{7,1},{8,10},{9,15},{10,... | collective-permute-start | bytes 2359304 | tf_op jit(solution)/shard_map/ppermute | solution.py:177
  179.3 12.1 %collective-permute-start.32 = (f32[128,1536]{1,0:T(8,128)S(1)}, f32[128,1536]{1,0:T(8,128)S(1)}, u32[]{:S(2)}, u32[]{:S(2)}) collective-permute-start(f32[128,1536]{1,0:T(8,128)S(1)} %get-tuple-element.113), channel_id=1, source_target_pairs={{0,8},{1,25},{2,10},{3,27},{4,12},{5,29},{6,14},{7,31},{8,0},{9,17... | collective-permute-start | bytes 2359304 | tf_op jit(solution)/shard_map/ppermute | solution.py:177
  181.3 12.0 %collective-permute-start.33 = (f32[128,1536]{1,0:T(8,128)S(1)}, f32[128,1536]{1,0:T(8,128)S(1)}, u32[]{:S(2)}, u32[]{:S(2)}) collective-permute-start(f32[128,1536]{1,0:T(8,128)S(1)} %get-tuple-element.114), channel_id=1, source_target_pairs={{0,32},{1,97},{2,34},{3,99},{4,36},{5,101},{6,38},{7,103},{8,40},{... | collective-permute-start | bytes 2359304 | tf_op jit(solution)/shard_map/ppermute | solution.py:177
  (29 other events, 466.8 us)

commit v5 on v4

--- a/solution.py
+++ b/solution.py
@@ -17,7 +17,7 @@
 coef_second = -4.775
 coef_third = 2.0315
 inner_step = 0.5
-VMEM_BYTES = 24 * 1024 * 1024
+MIB = 1024 * 1024
 
 
 def flat_at(x, y, z, c):
@@ -101,7 +101,7 @@
 HBM = pl.BlockSpec(memory_space=pltpu.HBM)
 
 
-def call(body, outs, *args, scratch=(), scalars=None, flops=0, specs=None, out_specs=None, limit=VMEM_BYTES):
+def call(body, outs, *args, scratch=(), scalars=None, flops=0, specs=None, out_specs=None, limit=3):
     specs = specs or [VMEM] * len(args)
     if scalars is not None:
         specs = [SMEM] + specs
@@ -115,7 +115,7 @@
         in_specs=specs,
         out_specs=out_specs or [VMEM] * len(outs),
         scratch_shapes=list(scratch),
-        compiler_params=pltpu.CompilerParams(vmem_limit_bytes=limit),
+        compiler_params=pltpu.CompilerParams(vmem_limit_bytes=limit * MIB),
         cost_estimate=pl.CostEstimate(flops=flops, bytes_accessed=moved, transcendentals=0),
     )(*args)
 
@@ -464,7 +464,7 @@
         ],
         specs=[HBM] * 6,
         out_specs=[HBM] * 11,
-        limit=56 * 1024 * 1024,
+        limit=56,
     )
     arrived, (mine,) = with_other(received(blocks, 1), call(total_body, quarters[:1], blocks[0]))
     arrived = (mine, *arrived[1:])
@@ -488,6 +488,7 @@
         cotangent,
         out_gain,
         scratch=[three_f32, three_f32],
+        limit=14,
     )
     other = lax.ppermute(stats, ALL, OTHER_CORE)
     *blocks, query_dgate, query_dup = call(
@@ -501,13 +502,14 @@
         other,
         *query_stored,
         scratch=[whole],
+        limit=8,
     )
     by_colour, query_dup = lax.optimization_barrier(
         (jnp.asarray(TOKENS_BY_COLOUR, jnp.int32), query_dup)
     )
     by_colour = by_colour[lax.axis_index("head")]
     query_grad = call(
-        query_grad_body, [low], new, query_dgate, query_dup, flops=4 * tokens * DH * DH
+        query_grad_body, [low], new, query_dgate, query_dup, flops=4 * tokens * DH * DH, limit=4
     )
     blocks, (query_grad,) = with_other(received(blocks, 1), query_grad)
     cots, share, *blocks, back_mid, gate_back, up_back = call(
@@ -523,6 +525,7 @@
         target,
         scalars=by_colour,
         scratch=[three_f32, three_low, three_f32, three_low, whole],
+        limit=20,
     )
     key_grads = call(
         key_grads_body,
@@ -539,6 +542,7 @@
         gate_back,
         up_back,
         flops=12 * tokens * DH * DH,
+        limit=6,
     )
     blocks, (key_grad, value_grad) = with_other(received(blocks, 1), key_grads)
     (quarter,) = call(total_body, quarters[:1], *blocks)

time: 216 us -> 216 us (level)
  no operation moved by 1% of the time
where the time goes in v5:
time: 216 us; the launch traced here: 215 us
  waiting for transfers between devices  89.7 us (42%)
  starting transfers between devices  55.3 us (26%)
  Pallas kernels  33 us (15%)
  blocking collectives  21.1 us (10%)
  local copies, waits for them, and re-layouts  15.3 us (7%)
    ppermute x33, waiting for transfers between devices, received(): lax.ppermute(blocks[step], ALL, PARTNERS[level, step])  88.3 us
    ppermute x33, starting transfers between devices, received(): lax.ppermute(blocks[step], ALL, PARTNERS[level, step])  55.3 us
    pallas_call x17, Pallas kernels, call(): pl.pallas_call(body, out_shape=list(outs), in_specs=specs, out_specs=out_...  33 us
    all_to_all x1, blocking collectives, local(): lax.all_to_all(quarter.reshape(16, 8, WIDE), ALL, 0, 0, axis_index_groups...  21.1 us
    unnamed x38, local copies, waits for them, and re-layouts  15.3 us
  transfers between devices with their start and end apart: 34, of which 31 were waited for; matrix products, arithmetic and copies ran while one was open for 0% of the time, Pallas kernels for 1%

profile of v5, /device:TPU:0, one launch (start us, length us, event | category | flops | bytes accessed | tf_op | source)
XLA Modules:
  0.0 215.3 jit_solution(12848120645852762848)
XLA Ops:
  0.6 4.5 %shard_map.145 = (f32[128,1536]{1,0:T(8,128)}, f32[128,1536]{1,0:T(8,128)}, f32[128,1536]{1,0:T(8,128)}, f32[128,1536]{1,0:T(8,128)}, f32[256,512]{1,0:T(8,128)}...) custom-call(bf16[256,512]{1,0:T(8,128)(2,1)} %bitcast.23, ...), custom_call_target="tpu_custom_call" | custom-call | bytes 7865344 | tf_op jit(solution)/shard_map/pallas_call | solution.py:112
  11.5 5.9 %collective-permute-done.b = f32[128,1536]{1,0:T(8,128)S(1)} collective-permute-done((f32[128,1536]{1,0:T(8,128)}, f32[128,1536]{1,0:T(8,128)S(1)}, u32[]{:S(2)}, u32[]{:S(2)}) %collective-permute-start) | collective-permute-done | bytes 786464 | tf_op jit(solution)/shard_map/ppermute | solution.py:177
  21.2 2.6 %collective-permute-start.3 = (f32[32,1536]{1,0:T(8,128)S(1)}, f32[32,1536]{1,0:T(8,128)S(1)}, u32[]{:S(2)}, u32[]{:S(2)}) collective-permute-start(f32[32,1536]{1,0:T(8,128)S(1)} %get-tuple-element.79), channel_id=1, source_target_pairs={{0,6},{1,3},{2,4},{3,1},{4,2},{5,7},{6,0},{7,5},{8,14},{9,11},{10,... | collective-permute-start | bytes 589832 | tf_op jit(solution)/shard_map/ppermute | solution.py:177
  26.0 2.8 %collective-permute-start.5 = (f32[32,1536]{1,0:T(8,128)S(1)}, f32[32,1536]{1,0:T(8,128)S(1)}, u32[]{:S(2)}, u32[]{:S(2)}) collective-permute-start(f32[32,1536]{1,0:T(8,128)S(1)} %get-tuple-element.81), channel_id=1, source_target_pairs={{0,96},{1,33},{2,98},{3,35},{4,100},{5,37},{6,102},{7,39},{8,104},... | collective-permute-start | bytes 589832 | tf_op jit(solution)/shard_map/ppermute | solution.py:177
  33.0 2.7 %collective-permute-start.8 = (f32[32,1536]{1,0:T(8,128)S(1)}, f32[32,1536]{1,0:T(8,128)S(1)}, u32[]{:S(2)}, u32[]{:S(2)}) collective-permute-start(f32[32,1536]{1,0:T(8,128)S(1)} %shard_map.148.refs_0_), channel_id=1, source_target_pairs={{0,84},{1,85},{2,86},{3,87},{4,80},{5,81},{6,82},{7,83},{8,92},{9,... | collective-permute-start | bytes 589832 | tf_op jit(solution)/shard_map/ppermute | solution.py:177
  37.9 4.1 %collective-permute-start.6 = (f32[32,1536]{1,0:T(8,128)S(1)}, f32[32,1536]{1,0:T(8,128)S(1)}, u32[]{:S(2)}, u32[]{:S(2)}) collective-permute-start(f32[32,1536]{1,0:T(8,128)S(1)} %shard_map.148.refs_0_), channel_id=1, source_target_pairs={{0,126},{1,127},{2,124},{3,125},{4,122},{5,123},{6,120},{7,121},{8... | collective-permute-start | bytes 589832 | tf_op jit(solution)/shard_map/ppermute | solution.py:177
  41.9 5.7 %collective-permute-done.8.refs_3_ = f32[32,1536]{1,0:T(8,128)S(1)} collective-permute-done((f32[32,1536]{1,0:T(8,128)S(1)}, f32[32,1536]{1,0:T(8,128)S(1)}, u32[]{:S(2)}, u32[]{:S(2)}) %collective-permute-start.8) | collective-permute-done | bytes 196640 | tf_op jit(solution)/shard_map/ppermute | solution.py:177
  49.4 2.7 %collective-permute-start.11 = (f32[32,1536]{1,0:T(8,128)S(1)}, f32[32,1536]{1,0:T(8,128)S(1)}, u32[]{:S(2)}, u32[]{:S(2)}) collective-permute-start(f32[32,1536]{1,0:T(8,128)S(1)} %shard_map.149.a), channel_id=1, source_target_pairs={{0,96},{1,33},{2,98},{3,35},{4,100},{5,37},{6,102},{7,39},{8,104},... | collective-permute-start | bytes 589832 | tf_op jit(solution)/shard_map/ppermute | solution.py:177
  55.1 2.8 %collective-permute-done.11.d = f32[32,1536]{1,0:T(8,128)S(1)} collective-permute-done((f32[32,1536]{1,0:T(8,128)S(1)}, f32[32,1536]{1,0:T(8,128)S(1)}, u32[]{:S(2)}, u32[]{:S(2)}) %collective-permute-start.11) | collective-permute-done | bytes 196640 | tf_op jit(solution)/shard_map/ppermute | solution.py:177
  57.9 2.6 %collective-permute-done.10.c = f32[32,1536]{1,0:T(8,128)S(1)} collective-permute-done((f32[32,1536]{1,0:T(8,128)S(1)}, f32[32,1536]{1,0:T(8,128)S(1)}, u32[]{:S(2)}, u32[]{:S(2)}) %collective-permute-start.10) | collective-permute-done | bytes 196640 | tf_op jit(solution)/shard_map/ppermute | solution.py:177
  61.2 11.6 %collective-permute-done.14.d = f32[128,1536]{1,0:T(8,128)S(1)} collective-permute-done((f32[128,1536]{1,0:T(8,128)S(1)}, f32[128,1536]{1,0:T(8,128)S(1)}, u32[]{:S(2)}, u32[]{:S(2)}) %collective-permute-start.14) | collective-permute-done | bytes 786464 | tf_op jit(solution)/shard_map/ppermute | solution.py:177
  73.2 8.7 %shard_map.151 = (bf16[3,512,512]{2,1,0:T(8,128)(2,1)S(1)}, bf16[3,9,512,512]{3,2,1,0:T(8,128)(2,1)S(1)}, f32[3,8,128]{2,1,0:T(8,128)S(1)}, f32[256,128]{1,0:T(8...) custom-call(f32[128,1536]{1,0:T(8,128)S(1)} %shard_map.150.a, ...), custom_call_target="tpu_custom_call" | custom-call | bytes 22951936 | tf_op jit(solution)/shard_map/pallas_call | solution.py:112
  81.9 5.0 %copy-done = bf16[3,9,512,512]{3,2,1,0:T(8,128)(2,1)} copy-done((bf16[3,9,512,512]{3,2,1,0:T(8,128)(2,1)}, bf16[3,9,512,512]{3,2,1,0:T(8,128)(2,1)S(1)}, u32[]{:S(2)}) %copy-start) | copy-done | bytes 14155800
  94.4 7.0 %collective-permute-done.16.b = f32[128,1536]{1,0:T(8,128)S(1)} collective-permute-done((f32[128,1536]{1,0:T(8,128)S(1)}, f32[128,1536]{1,0:T(8,128)S(1)}, u32[]{:S(2)}, u32[]{:S(2)}) %collective-permute-start.16) | collective-permute-done | bytes 786464 | tf_op jit(solution)/shard_map/ppermute | solution.py:177
  114.1 4.3 %collective-permute-start.24 = (f32[32,1536]{1,0:T(8,128)S(1)}, f32[32,1536]{1,0:T(8,128)S(1)}, u32[]{:S(2)}, u32[]{:S(2)}) collective-permute-start(f32[32,1536]{1,0:T(8,128)S(1)} %shard_map.155.refs_0_), channel_id=1, source_target_pairs={{0,84},{1,85},{2,86},{3,87},{4,80},{5,81},{6,82},{7,83},{8,92},{9,... | collective-permute-start | bytes 589832 | tf_op jit(solution)/shard_map/ppermute | solution.py:177
  119.5 3.6 %collective-permute-start.22 = (f32[32,1536]{1,0:T(8,128)S(1)}, f32[32,1536]{1,0:T(8,128)S(1)}, u32[]{:S(2)}, u32[]{:S(2)}) collective-permute-start(f32[32,1536]{1,0:T(8,128)S(1)} %shard_map.155.refs_0_), channel_id=1, source_target_pairs={{0,126},{1,127},{2,124},{3,125},{4,122},{5,123},{6,120},{7,121},{8... | collective-permute-start | bytes 589832 | tf_op jit(solution)/shard_map/ppermute | solution.py:177
  123.1 5.6 %collective-permute-done.24.refs_3_ = f32[32,1536]{1,0:T(8,128)S(1)} collective-permute-done((f32[32,1536]{1,0:T(8,128)S(1)}, f32[32,1536]{1,0:T(8,128)S(1)}, u32[]{:S(2)}, u32[]{:S(2)}) %collective-permute-start.24) | collective-permute-done | bytes 196640 | tf_op jit(solution)/shard_map/ppermute | solution.py:177
  128.7 2.7 %collective-permute-done.22.refs_1_ = f32[32,1536]{1,0:T(8,128)S(1)} collective-permute-done((f32[32,1536]{1,0:T(8,128)S(1)}, f32[32,1536]{1,0:T(8,128)S(1)}, u32[]{:S(2)}, u32[]{:S(2)}) %collective-permute-start.22) | collective-permute-done | bytes 196640 | tf_op jit(solution)/shard_map/ppermute | solution.py:177
  140.1 3.3 %collective-permute-done.25.b = f32[32,1536]{1,0:T(8,128)S(1)} collective-permute-done((f32[32,1536]{1,0:T(8,128)S(1)}, f32[32,1536]{1,0:T(8,128)S(1)}, u32[]{:S(2)}, u32[]{:S(2)}) %collective-permute-start.25) | collective-permute-done | bytes 196640 | tf_op jit(solution)/shard_map/ppermute | solution.py:177
  143.8 11.8 %collective-permute-done.30.d = f32[128,1536]{1,0:T(8,128)S(1)} collective-permute-done((f32[128,1536]{1,0:T(8,128)S(1)}, f32[128,1536]{1,0:T(8,128)S(1)}, u32[]{:S(2)}, u32[]{:S(2)}) %collective-permute-start.30) | collective-permute-done | bytes 786464 | tf_op jit(solution)/shard_map/ppermute | solution.py:177
  155.9 5.0 %copy-done.1 = bf16[3,9,512,512]{3,2,1,0:T(8,128)(2,1)S(1)} copy-done((bf16[3,9,512,512]{3,2,1,0:T(8,128)(2,1)S(1)}, bf16[3,9,512,512]{3,2,1,0:T(8,128)(2,1)}, u32[]{:S(2)}) %copy-start.1) | copy-done | bytes 14155800
  165.0 14.3 %shard_map.158 = (bf16[3,512,512]{2,1,0:T(8,128)(2,1)S(1)}, f32[8,1536]{1,0:T(8,128)S(1)}, f32[128,1536]{1,0:T(8,128)S(1)}, f32[128,1536]{1,0:T(8,128)S(1)}, f32...) custom-call(s32[64]{0:T(128)S(1)} %dynamic-slice_bitcast_fusion.by_c, ...), custom_call_target="tpu_custom_call" | custom-call | bytes 24965376 | tf_op jit(solution)/shard_map/pallas_call | solution.py:112
  185.1 6.3 %collective-permute-done.31.refs_1_ = f32[128,1536]{1,0:T(8,128)S(1)} collective-permute-done((f32[128,1536]{1,0:T(8,128)S(1)}, f32[128,1536]{1,0:T(8,128)S(1)}, u32[]{:S(2)}, u32[]{:S(2)}) %collective-permute-start.31) | collective-permute-done | bytes 786464 | tf_op jit(solution)/shard_map/ppermute | solution.py:177
  193.6 21.1 %all_to_all.5.pieces = f32[16,8,1536]{2,1,0:T(8,128)S(1)} all-to-all(f32[16,8,1536]{2,1,0:T(8,128)S(1)} %bitcast.22), channel_id=1, replica_groups={{0,6,24,30,42,44,50,52,74,76,82,84,96,102,120,126},{2,4,26,28,40,46,48,..., dimensions={0} | all-to-all | bytes 1572864 | tf_op jit(solution)/shard_map/all_to_all | solution.py:549
  (101 shorter events, 67.7 us)
Async XLA Ops:
  5.2 12.3 %collective-permute-start = (f32[128,1536]{1,0:T(8,128)}, f32[128,1536]{1,0:T(8,128)S(1)}, u32[]{:S(2)}, u32[]{:S(2)}) collective-permute-start(f32[128,1536]{1,0:T(8,128)} %get-tuple-element.71), channel_id=1, source_target_pairs={{0,2},{1,7},{2,0},{3,5},{4,6},{5,3},{6,4},{7,1},{8,10},{9,15},{10,... | collective-permute-start | bytes 2359304 | tf_op jit(solution)/shard_map/ppermute | solution.py:177
  7.3 12.2 %collective-permute-start.1 = (f32[128,1536]{1,0:T(8,128)}, f32[128,1536]{1,0:T(8,128)S(1)}, u32[]{:S(2)}, u32[]{:S(2)}) collective-permute-start(f32[128,1536]{1,0:T(8,128)} %get-tuple-element.72), channel_id=1, source_target_pairs={{0,8},{1,25},{2,10},{3,27},{4,12},{5,29},{6,14},{7,31},{8,0},{9,17... | collective-permute-start | bytes 2359304 | tf_op jit(solution)/shard_map/ppermute | solution.py:177
  8.8 12.2 %collective-permute-start.2 = (f32[128,1536]{1,0:T(8,128)}, f32[128,1536]{1,0:T(8,128)S(1)}, u32[]{:S(2)}, u32[]{:S(2)}) collective-permute-start(f32[128,1536]{1,0:T(8,128)} %get-tuple-element.73), channel_id=1, source_target_pairs={{0,32},{1,97},{2,34},{3,99},{4,36},{5,101},{6,38},{7,103},{8,40},{... | collective-permute-start | bytes 2359304 | tf_op jit(solution)/shard_map/ppermute | solution.py:177
  33.0 14.7 %collective-permute-start.8 = (f32[32,1536]{1,0:T(8,128)S(1)}, f32[32,1536]{1,0:T(8,128)S(1)}, u32[]{:S(2)}, u32[]{:S(2)}) collective-permute-start(f32[32,1536]{1,0:T(8,128)S(1)} %shard_map.148.refs_0_), channel_id=1, source_target_pairs={{0,84},{1,85},{2,86},{3,87},{4,80},{5,81},{6,82},{7,83},{8,92},{9,... | collective-permute-start | bytes 589832 | tf_op jit(solution)/shard_map/ppermute | solution.py:177
  35.7 11.9 %collective-permute-start.7 = (f32[32,1536]{1,0:T(8,128)S(1)}, f32[32,1536]{1,0:T(8,128)S(1)}, u32[]{:S(2)}, u32[]{:S(2)}) collective-permute-start(f32[32,1536]{1,0:T(8,128)S(1)} %shard_map.148.refs_0_), channel_id=1, source_target_pairs={{0,42},{1,43},{2,40},{3,41},{4,46},{5,47},{6,44},{7,45},{8,34},{9,... | collective-permute-start | bytes 589832 | tf_op jit(solution)/shard_map/ppermute | solution.py:177
  37.9 11.5 %collective-permute-start.6 = (f32[32,1536]{1,0:T(8,128)S(1)}, f32[32,1536]{1,0:T(8,128)S(1)}, u32[]{:S(2)}, u32[]{:S(2)}) collective-permute-start(f32[32,1536]{1,0:T(8,128)S(1)} %shard_map.148.refs_0_), channel_id=1, source_target_pairs={{0,126},{1,127},{2,124},{3,125},{4,122},{5,123},{6,120},{7,121},{8... | collective-permute-start | bytes 589832 | tf_op jit(solution)/shard_map/ppermute | solution.py:177
  49.4 8.5 %collective-permute-start.11 = (f32[32,1536]{1,0:T(8,128)S(1)}, f32[32,1536]{1,0:T(8,128)S(1)}, u32[]{:S(2)}, u32[]{:S(2)}) collective-permute-start(f32[32,1536]{1,0:T(8,128)S(1)} %shard_map.149.a), channel_id=1, source_target_pairs={{0,96},{1,33},{2,98},{3,35},{4,100},{5,37},{6,102},{7,39},{8,104},... | collective-permute-start | bytes 589832 | tf_op jit(solution)/shard_map/ppermute | solution.py:177
  52.1 8.4 %collective-permute-start.10 = (f32[32,1536]{1,0:T(8,128)S(1)}, f32[32,1536]{1,0:T(8,128)S(1)}, u32[]{:S(2)}, u32[]{:S(2)}) collective-permute-start(f32[32,1536]{1,0:T(8,128)S(1)} %shard_map.149.a), channel_id=1, source_target_pairs={{0,24},{1,9},{2,26},{3,11},{4,28},{5,13},{6,30},{7,15},{8,16},{9,1... | collective-permute-start | bytes 589832 | tf_op jit(solution)/shard_map/ppermute | solution.py:177
  52.8 7.8 %collective-permute-start.9 = (f32[32,1536]{1,0:T(8,128)S(1)}, f32[32,1536]{1,0:T(8,128)S(1)}, u32[]{:S(2)}, u32[]{:S(2)}) collective-permute-start(f32[32,1536]{1,0:T(8,128)S(1)} %shard_map.149.a), channel_id=1, source_target_pairs={{0,6},{1,3},{2,4},{3,1},{4,2},{5,7},{6,0},{7,5},{8,14},{9,11},{10,... | collective-permute-start | bytes 589832 | tf_op jit(solution)/shard_map/ppermute | solution.py:177
  60.7 12.1 %collective-permute-start.14 = (f32[128,1536]{1,0:T(8,128)S(1)}, f32[128,1536]{1,0:T(8,128)S(1)}, u32[]{:S(2)}, u32[]{:S(2)}) collective-permute-start(f32[128,1536]{1,0:T(8,128)S(1)} %shard_map.150.a), channel_id=1, source_target_pairs={{0,32},{1,97},{2,34},{3,99},{4,36},{5,101},{6,38},{7,103},{8,40},{... | collective-permute-start | bytes 2359304 | tf_op jit(solution)/shard_map/ppermute | solution.py:177
  60.8 12.1 %collective-permute-start.13 = (f32[128,1536]{1,0:T(8,128)S(1)}, f32[128,1536]{1,0:T(8,128)S(1)}, u32[]{:S(2)}, u32[]{:S(2)}) collective-permute-start(f32[128,1536]{1,0:T(8,128)S(1)} %shard_map.150.a), channel_id=1, source_target_pairs={{0,8},{1,25},{2,10},{3,27},{4,12},{5,29},{6,14},{7,31},{8,0},{9,17... | collective-permute-start | bytes 2359304 | tf_op jit(solution)/shard_map/ppermute | solution.py:177
  60.9 12.3 %collective-permute-start.12 = (f32[128,1536]{1,0:T(8,128)S(1)}, f32[128,1536]{1,0:T(8,128)S(1)}, u32[]{:S(2)}, u32[]{:S(2)}) collective-permute-start(f32[128,1536]{1,0:T(8,128)S(1)} %shard_map.150.a), channel_id=1, source_target_pairs={{0,2},{1,7},{2,0},{3,5},{4,6},{5,3},{6,4},{7,1},{8,10},{9,15},{10,... | collective-permute-start | bytes 2359304 | tf_op jit(solution)/shard_map/ppermute | solution.py:177
  89.4 12.1 %collective-permute-start.16 = (f32[128,1536]{1,0:T(8,128)S(1)}, f32[128,1536]{1,0:T(8,128)S(1)}, u32[]{:S(2)}, u32[]{:S(2)}) collective-permute-start(f32[128,1536]{1,0:T(8,128)S(1)} %get-tuple-element.89), channel_id=1, source_target_pairs={{0,2},{1,7},{2,0},{3,5},{4,6},{5,3},{6,4},{7,1},{8,10},{9,15},{10,... | collective-permute-start | bytes 2359304 | tf_op jit(solution)/shard_map/ppermute | solution.py:177
  89.5 12.1 %collective-permute-start.17 = (f32[128,1536]{1,0:T(8,128)S(1)}, f32[128,1536]{1,0:T(8,128)S(1)}, u32[]{:S(2)}, u32[]{:S(2)}) collective-permute-start(f32[128,1536]{1,0:T(8,128)S(1)} %get-tuple-element.90), channel_id=1, source_target_pairs={{0,8},{1,25},{2,10},{3,27},{4,12},{5,29},{6,14},{7,31},{8,0},{9,17... | collective-permute-start | bytes 2359304 | tf_op jit(solution)/shard_map/ppermute | solution.py:177
  91.3 12.0 %collective-permute-start.18 = (f32[128,1536]{1,0:T(8,128)S(1)}, f32[128,1536]{1,0:T(8,128)S(1)}, u32[]{:S(2)}, u32[]{:S(2)}) collective-permute-start(f32[128,1536]{1,0:T(8,128)S(1)} %get-tuple-element.91), channel_id=1, source_target_pairs={{0,32},{1,97},{2,34},{3,99},{4,36},{5,101},{6,38},{7,103},{8,40},{... | collective-permute-start | bytes 2359304 | tf_op jit(solution)/shard_map/ppermute | solution.py:177
  114.1 14.6 %collective-permute-start.24 = (f32[32,1536]{1,0:T(8,128)S(1)}, f32[32,1536]{1,0:T(8,128)S(1)}, u32[]{:S(2)}, u32[]{:S(2)}) collective-permute-start(f32[32,1536]{1,0:T(8,128)S(1)} %shard_map.155.refs_0_), channel_id=1, source_target_pairs={{0,84},{1,85},{2,86},{3,87},{4,80},{5,81},{6,82},{7,83},{8,92},{9,... | collective-permute-start | bytes 589832 | tf_op jit(solution)/shard_map/ppermute | solution.py:177
  118.4 10.3 %collective-permute-start.23 = (f32[32,1536]{1,0:T(8,128)S(1)}, f32[32,1536]{1,0:T(8,128)S(1)}, u32[]{:S(2)}, u32[]{:S(2)}) collective-permute-start(f32[32,1536]{1,0:T(8,128)S(1)} %shard_map.155.refs_0_), channel_id=1, source_target_pairs={{0,42},{1,43},{2,40},{3,41},{4,46},{5,47},{6,44},{7,45},{8,34},{9,... | collective-permute-start | bytes 589832 | tf_op jit(solution)/shard_map/ppermute | solution.py:177
  119.5 11.9 %collective-permute-start.22 = (f32[32,1536]{1,0:T(8,128)S(1)}, f32[32,1536]{1,0:T(8,128)S(1)}, u32[]{:S(2)}, u32[]{:S(2)}) collective-permute-start(f32[32,1536]{1,0:T(8,128)S(1)} %shard_map.155.refs_0_), channel_id=1, source_target_pairs={{0,126},{1,127},{2,124},{3,125},{4,122},{5,123},{6,120},{7,121},{8... | collective-permute-start | bytes 589832 | tf_op jit(solution)/shard_map/ppermute | solution.py:177
  143.5 12.1 %collective-permute-start.30 = (f32[128,1536]{1,0:T(8,128)S(1)}, f32[128,1536]{1,0:T(8,128)S(1)}, u32[]{:S(2)}, u32[]{:S(2)}) collective-permute-start(f32[128,1536]{1,0:T(8,128)S(1)} %shard_map.157.a), channel_id=1, source_target_pairs={{0,32},{1,97},{2,34},{3,99},{4,36},{5,101},{6,38},{7,103},{8,40},{... | collective-permute-start | bytes 2359304 | tf_op jit(solution)/shard_map/ppermute | solution.py:177
  143.6 12.2 %collective-permute-start.29 = (f32[128,1536]{1,0:T(8,128)S(1)}, f32[128,1536]{1,0:T(8,128)}, u32[]{:S(2)}, u32[]{:S(2)}) collective-permute-start(f32[128,1536]{1,0:T(8,128)S(1)} %shard_map.157.a), channel_id=1, source_target_pairs={{0,8},{1,25},{2,10},{3,27},{4,12},{5,29},{6,14},{7,31},{8,0},{9,17... | collective-permute-start | bytes 2359304 | tf_op jit(solution)/shard_map/ppermute | solution.py:177
  143.7 12.2 %collective-permute-start.28 = (f32[128,1536]{1,0:T(8,128)S(1)}, f32[128,1536]{1,0:T(8,128)}, u32[]{:S(2)}, u32[]{:S(2)}) collective-permute-start(f32[128,1536]{1,0:T(8,128)S(1)} %shard_map.157.a), channel_id=1, source_target_pairs={{0,2},{1,7},{2,0},{3,5},{4,6},{5,3},{6,4},{7,1},{8,10},{9,15},{10,... | collective-permute-start | bytes 2359304 | tf_op jit(solution)/shard_map/ppermute | solution.py:177
  179.3 12.1 %collective-permute-start.31 = (f32[128,1536]{1,0:T(8,128)S(1)}, f32[128,1536]{1,0:T(8,128)S(1)}, u32[]{:S(2)}, u32[]{:S(2)}) collective-permute-start(f32[128,1536]{1,0:T(8,128)S(1)} %get-tuple-element.112), channel_id=1, source_target_pairs={{0,2},{1,7},{2,0},{3,5},{4,6},{5,3},{6,4},{7,1},{8,10},{9,15},{10,... | collective-permute-start | bytes 2359304 | tf_op jit(solution)/shard_map/ppermute | solution.py:177
  179.4 12.1 %collective-permute-start.32 = (f32[128,1536]{1,0:T(8,128)S(1)}, f32[128,1536]{1,0:T(8,128)S(1)}, u32[]{:S(2)}, u32[]{:S(2)}) collective-permute-start(f32[128,1536]{1,0:T(8,128)S(1)} %get-tuple-element.113), channel_id=1, source_target_pairs={{0,8},{1,25},{2,10},{3,27},{4,12},{5,29},{6,14},{7,31},{8,0},{9,17... | collective-permute-start | bytes 2359304 | tf_op jit(solution)/shard_map/ppermute | solution.py:177
  181.4 12.0 %collective-permute-start.33 = (f32[128,1536]{1,0:T(8,128)S(1)}, f32[128,1536]{1,0:T(8,128)S(1)}, u32[]{:S(2)}, u32[]{:S(2)}) collective-permute-start(f32[128,1536]{1,0:T(8,128)S(1)} %get-tuple-element.114), channel_id=1, source_target_pairs={{0,32},{1,97},{2,34},{3,99},{4,36},{5,101},{6,38},{7,103},{8,40},{... | collective-permute-start | bytes 2359304 | tf_op jit(solution)/shard_map/ppermute | solution.py:177
  (29 other events, 466.8 us)

commit v6 on v5

--- a/solution.py
+++ b/solution.py
@@ -433,8 +433,9 @@
     key_terms(cots, keys, gate, up, mid, target, *key_refs, terms)
     for step in range(4):
         first = 16 * (near ^ step)
+        core = lax.axis_index("head")
         for j in range(16):
-            outs[step][8 * j : 8 * j + 8, :] = terms[rows_at(by_colour[first + j], 8), :]
+            outs[step][8 * j : 8 * j + 8, :] = terms[rows_at(by_colour[core, first + j], 8), :]
 
 
 def local(queries, key_rows, value_rows, step_rates, w_gate, w_up, w_down, out_gain, cotangent):
@@ -504,10 +505,6 @@
         scratch=[whole],
         limit=8,
     )
-    by_colour, query_dup = lax.optimization_barrier(
-        (jnp.asarray(TOKENS_BY_COLOUR, jnp.int32), query_dup)
-    )
-    by_colour = by_colour[lax.axis_index("head")]
     query_grad = call(
         query_grad_body, [low], new, query_dgate, query_dup, flops=4 * tokens * DH * DH, limit=4
     )
@@ -523,7 +520,7 @@
         up,
         mid,
         target,
-        scalars=by_colour,
+        scalars=jnp.asarray(TOKENS_BY_COLOUR, jnp.int32),
         scratch=[three_f32, three_low, three_f32, three_low, whole],
         limit=20,
     )

time: 216 us -> 200 us (0.926)
  local copies, waits for them, and re-layouts: 15.3 us -> 1.21 us
    unnamed x38 -> x34, local copies, waits for them, and re-layouts: 15.3 us -> 1.21 us
where the time goes in v6:
time: 200 us
  waiting for transfers between devices  89.6 us (45%)
  starting transfers between devices  55.4 us (28%)
  Pallas kernels  31.5 us (16%)
  blocking collectives  21.1 us (11%)
    ppermute x33, waiting for transfers between devices, received(): lax.ppermute(blocks[step], ALL, PARTNERS[level, step])  88.3 us
    ppermute x33, starting transfers between devices, received(): lax.ppermute(blocks[step], ALL, PARTNERS[level, step])  55.3 us
    pallas_call x17, Pallas kernels, call(): pl.pallas_call(body, out_shape=list(outs), in_specs=specs, out_specs=out_...  31.5 us
    all_to_all x1, blocking collectives, local(): lax.all_to_all(quarter.reshape(16, 8, WIDE), ALL, 0, 0, axis_index_groups...  21.1 us
  transfers between devices with their start and end apart: 34, of which 31 were waited for; matrix products, arithmetic and copies ran while one was open for 0% of the time, Pallas kernels for 1%

profile of v6, /device:TPU:0, one launch (start us, length us, event | category | flops | bytes accessed | tf_op | source)
XLA Modules:
  0.0 199.8 jit_solution(2107819460194774607)
XLA Ops:
  0.6 4.5 %shard_map.145 = (f32[128,1536]{1,0:T(8,128)}, f32[128,1536]{1,0:T(8,128)}, f32[128,1536]{1,0:T(8,128)}, f32[128,1536]{1,0:T(8,128)}, f32[256,512]{1,0:T(8,128)}...) custom-call(bf16[256,512]{1,0:T(8,128)(2,1)} %bitcast.21, ...), custom_call_target="tpu_custom_call" | custom-call | bytes 7865344 | tf_op jit(solution)/shard_map/pallas_call | solution.py:112
  11.5 5.9 %collective-permute-done.b = f32[128,1536]{1,0:T(8,128)S(1)} collective-permute-done((f32[128,1536]{1,0:T(8,128)}, f32[128,1536]{1,0:T(8,128)S(1)}, u32[]{:S(2)}, u32[]{:S(2)}) %collective-permute-start) | collective-permute-done | bytes 786464 | tf_op jit(solution)/shard_map/ppermute | solution.py:177
  21.2 2.6 %collective-permute-start.3 = (f32[32,1536]{1,0:T(8,128)S(1)}, f32[32,1536]{1,0:T(8,128)S(1)}, u32[]{:S(2)}, u32[]{:S(2)}) collective-permute-start(f32[32,1536]{1,0:T(8,128)S(1)} %get-tuple-element.77), channel_id=1, source_target_pairs={{0,6},{1,3},{2,4},{3,1},{4,2},{5,7},{6,0},{7,5},{8,14},{9,11},{10,... | collective-permute-start | bytes 589832 | tf_op jit(solution)/shard_map/ppermute | solution.py:177
  26.0 2.8 %collective-permute-start.5 = (f32[32,1536]{1,0:T(8,128)S(1)}, f32[32,1536]{1,0:T(8,128)S(1)}, u32[]{:S(2)}, u32[]{:S(2)}) collective-permute-start(f32[32,1536]{1,0:T(8,128)S(1)} %get-tuple-element.79), channel_id=1, source_target_pairs={{0,96},{1,33},{2,98},{3,35},{4,100},{5,37},{6,102},{7,39},{8,104},... | collective-permute-start | bytes 589832 | tf_op jit(solution)/shard_map/ppermute | solution.py:177
  32.9 2.7 %collective-permute-start.8 = (f32[32,1536]{1,0:T(8,128)S(1)}, f32[32,1536]{1,0:T(8,128)S(1)}, u32[]{:S(2)}, u32[]{:S(2)}) collective-permute-start(f32[32,1536]{1,0:T(8,128)S(1)} %shard_map.148.refs_0_), channel_id=1, source_target_pairs={{0,84},{1,85},{2,86},{3,87},{4,80},{5,81},{6,82},{7,83},{8,92},{9,... | collective-permute-start | bytes 589832 | tf_op jit(solution)/shard_map/ppermute | solution.py:177
  37.9 4.1 %collective-permute-start.6 = (f32[32,1536]{1,0:T(8,128)S(1)}, f32[32,1536]{1,0:T(8,128)S(1)}, u32[]{:S(2)}, u32[]{:S(2)}) collective-permute-start(f32[32,1536]{1,0:T(8,128)S(1)} %shard_map.148.refs_0_), channel_id=1, source_target_pairs={{0,126},{1,127},{2,124},{3,125},{4,122},{5,123},{6,120},{7,121},{8... | collective-permute-start | bytes 589832 | tf_op jit(solution)/shard_map/ppermute | solution.py:177
  41.9 5.7 %collective-permute-done.8.refs_3_ = f32[32,1536]{1,0:T(8,128)S(1)} collective-permute-done((f32[32,1536]{1,0:T(8,128)S(1)}, f32[32,1536]{1,0:T(8,128)S(1)}, u32[]{:S(2)}, u32[]{:S(2)}) %collective-permute-start.8) | collective-permute-done | bytes 196640 | tf_op jit(solution)/shard_map/ppermute | solution.py:177
  49.4 2.7 %collective-permute-start.11 = (f32[32,1536]{1,0:T(8,128)S(1)}, f32[32,1536]{1,0:T(8,128)S(1)}, u32[]{:S(2)}, u32[]{:S(2)}) collective-permute-start(f32[32,1536]{1,0:T(8,128)S(1)} %shard_map.149.a), channel_id=1, source_target_pairs={{0,96},{1,33},{2,98},{3,35},{4,100},{5,37},{6,102},{7,39},{8,104},... | collective-permute-start | bytes 589832 | tf_op jit(solution)/shard_map/ppermute | solution.py:177
  55.1 2.8 %collective-permute-done.11.d = f32[32,1536]{1,0:T(8,128)S(1)} collective-permute-done((f32[32,1536]{1,0:T(8,128)S(1)}, f32[32,1536]{1,0:T(8,128)S(1)}, u32[]{:S(2)}, u32[]{:S(2)}) %collective-permute-start.11) | collective-permute-done | bytes 196640 | tf_op jit(solution)/shard_map/ppermute | solution.py:177
  57.9 2.6 %collective-permute-done.10.c = f32[32,1536]{1,0:T(8,128)S(1)} collective-permute-done((f32[32,1536]{1,0:T(8,128)S(1)}, f32[32,1536]{1,0:T(8,128)S(1)}, u32[]{:S(2)}, u32[]{:S(2)}) %collective-permute-start.10) | collective-permute-done | bytes 196640 | tf_op jit(solution)/shard_map/ppermute | solution.py:177
  61.2 11.6 %collective-permute-done.14.d = f32[128,1536]{1,0:T(8,128)S(1)} collective-permute-done((f32[128,1536]{1,0:T(8,128)S(1)}, f32[128,1536]{1,0:T(8,128)S(1)}, u32[]{:S(2)}, u32[]{:S(2)}) %collective-permute-start.14) | collective-permute-done | bytes 786464 | tf_op jit(solution)/shard_map/ppermute | solution.py:177
  73.2 8.2 %shard_map.151 = (bf16[3,512,512]{2,1,0:T(8,128)(2,1)S(1)}, bf16[3,9,512,512]{3,2,1,0:T(8,128)(2,1)S(1)}, f32[3,8,128]{2,1,0:T(8,128)S(1)}, f32[256,128]{1,0:T(8...) custom-call(f32[128,1536]{1,0:T(8,128)S(1)} %shard_map.150.a, ...), custom_call_target="tpu_custom_call" | custom-call | bytes 22951936 | tf_op jit(solution)/shard_map/pallas_call | solution.py:112
  88.9 7.0 %collective-permute-done.16.b = f32[128,1536]{1,0:T(8,128)S(1)} collective-permute-done((f32[128,1536]{1,0:T(8,128)S(1)}, f32[128,1536]{1,0:T(8,128)S(1)}, u32[]{:S(2)}, u32[]{:S(2)}) %collective-permute-start.16) | collective-permute-done | bytes 786464 | tf_op jit(solution)/shard_map/ppermute | solution.py:177
  97.9 2.5 %collective-permute-start.19 = (f32[32,1536]{1,0:T(8,128)S(1)}, f32[32,1536]{1,0:T(8,128)S(1)}, u32[]{:S(2)}, u32[]{:S(2)}) collective-permute-start(f32[32,1536]{1,0:T(8,128)S(1)} %get-tuple-element.98), channel_id=1, source_target_pairs={{0,6},{1,3},{2,4},{3,1},{4,2},{5,7},{6,0},{7,5},{8,14},{9,11},{10,... | collective-permute-start | bytes 589832 | tf_op jit(solution)/shard_map/ppermute | solution.py:177
  108.7 4.3 %collective-permute-start.24 = (f32[32,1536]{1,0:T(8,128)S(1)}, f32[32,1536]{1,0:T(8,128)S(1)}, u32[]{:S(2)}, u32[]{:S(2)}) collective-permute-start(f32[32,1536]{1,0:T(8,128)S(1)} %shard_map.155.refs_0_), channel_id=1, source_target_pairs={{0,84},{1,85},{2,86},{3,87},{4,80},{5,81},{6,82},{7,83},{8,92},{9,... | collective-permute-start | bytes 589832 | tf_op jit(solution)/shard_map/ppermute | solution.py:177
  114.0 3.6 %collective-permute-start.22 = (f32[32,1536]{1,0:T(8,128)S(1)}, f32[32,1536]{1,0:T(8,128)S(1)}, u32[]{:S(2)}, u32[]{:S(2)}) collective-permute-start(f32[32,1536]{1,0:T(8,128)S(1)} %shard_map.155.refs_0_), channel_id=1, source_target_pairs={{0,126},{1,127},{2,124},{3,125},{4,122},{5,123},{6,120},{7,121},{8... | collective-permute-start | bytes 589832 | tf_op jit(solution)/shard_map/ppermute | solution.py:177
  117.6 5.6 %collective-permute-done.24.refs_3_ = f32[32,1536]{1,0:T(8,128)S(1)} collective-permute-done((f32[32,1536]{1,0:T(8,128)S(1)}, f32[32,1536]{1,0:T(8,128)S(1)}, u32[]{:S(2)}, u32[]{:S(2)}) %collective-permute-start.24) | collective-permute-done | bytes 196640 | tf_op jit(solution)/shard_map/ppermute | solution.py:177
  123.2 2.7 %collective-permute-done.22.refs_1_ = f32[32,1536]{1,0:T(8,128)S(1)} collective-permute-done((f32[32,1536]{1,0:T(8,128)S(1)}, f32[32,1536]{1,0:T(8,128)S(1)}, u32[]{:S(2)}, u32[]{:S(2)}) %collective-permute-start.22) | collective-permute-done | bytes 196640 | tf_op jit(solution)/shard_map/ppermute | solution.py:177
  127.8 2.5 %collective-permute-start.26 = (f32[32,1536]{1,0:T(8,128)S(1)}, f32[32,1536]{1,0:T(8,128)S(1)}, u32[]{:S(2)}, u32[]{:S(2)}) collective-permute-start(f32[32,1536]{1,0:T(8,128)S(1)} %shard_map.156.a), channel_id=1, source_target_pairs={{0,24},{1,9},{2,26},{3,11},{4,28},{5,13},{6,30},{7,15},{8,16},{9,1... | collective-permute-start | bytes 589832 | tf_op jit(solution)/shard_map/ppermute | solution.py:177
  134.7 3.3 %collective-permute-done.25.b = f32[32,1536]{1,0:T(8,128)S(1)} collective-permute-done((f32[32,1536]{1,0:T(8,128)S(1)}, f32[32,1536]{1,0:T(8,128)S(1)}, u32[]{:S(2)}, u32[]{:S(2)}) %collective-permute-start.25) | collective-permute-done | bytes 196640 | tf_op jit(solution)/shard_map/ppermute | solution.py:177
  138.4 11.8 %collective-permute-done.30.d = f32[128,1536]{1,0:T(8,128)S(1)} collective-permute-done((f32[128,1536]{1,0:T(8,128)S(1)}, f32[128,1536]{1,0:T(8,128)S(1)}, u32[]{:S(2)}, u32[]{:S(2)}) %collective-permute-start.30) | collective-permute-done | bytes 786464 | tf_op jit(solution)/shard_map/ppermute | solution.py:177
  150.4 13.4 %shard_map.158 = (bf16[3,512,512]{2,1,0:T(8,128)(2,1)S(1)}, f32[8,1536]{1,0:T(8,128)S(1)}, f32[128,1536]{1,0:T(8,128)S(1)}, f32[128,1536]{1,0:T(8,128)S(1)}, f32...) custom-call(s32[2,64]{1,0:T(2,128)S(1)} %copy-done.16, ...), custom_call_target="tpu_custom_call" | custom-call | bytes 24965632 | tf_op jit(solution)/shard_map/pallas_call | solution.py:112
  169.6 6.3 %collective-permute-done.31.refs_1_ = f32[128,1536]{1,0:T(8,128)S(1)} collective-permute-done((f32[128,1536]{1,0:T(8,128)S(1)}, f32[128,1536]{1,0:T(8,128)S(1)}, u32[]{:S(2)}, u32[]{:S(2)}) %collective-permute-start.31) | collective-permute-done | bytes 786464 | tf_op jit(solution)/shard_map/ppermute | solution.py:177
  178.1 21.1 %all_to_all.5.pieces = f32[16,8,1536]{2,1,0:T(8,128)S(1)} all-to-all(f32[16,8,1536]{2,1,0:T(8,128)S(1)} %bitcast.20), channel_id=1, replica_groups={{0,6,24,30,42,44,50,52,74,76,82,84,96,102,120,126},{2,4,26,28,40,46,48,..., dimensions={0} | all-to-all | bytes 1572864 | tf_op jit(solution)/shard_map/all_to_all | solution.py:546
  (96 shorter events, 58.5 us)
Async XLA Ops:
  5.2 12.3 %collective-permute-start = (f32[128,1536]{1,0:T(8,128)}, f32[128,1536]{1,0:T(8,128)S(1)}, u32[]{:S(2)}, u32[]{:S(2)}) collective-permute-start(f32[128,1536]{1,0:T(8,128)} %get-tuple-element.69), channel_id=1, source_target_pairs={{0,2},{1,7},{2,0},{3,5},{4,6},{5,3},{6,4},{7,1},{8,10},{9,15},{10,... | collective-permute-start | bytes 2359304 | tf_op jit(solution)/shard_map/ppermute | solution.py:177
  7.3 12.2 %collective-permute-start.1 = (f32[128,1536]{1,0:T(8,128)}, f32[128,1536]{1,0:T(8,128)S(1)}, u32[]{:S(2)}, u32[]{:S(2)}) collective-permute-start(f32[128,1536]{1,0:T(8,128)} %get-tuple-element.70), channel_id=1, source_target_pairs={{0,8},{1,25},{2,10},{3,27},{4,12},{5,29},{6,14},{7,31},{8,0},{9,17... | collective-permute-start | bytes 2359304 | tf_op jit(solution)/shard_map/ppermute | solution.py:177
  8.8 12.2 %collective-permute-start.2 = (f32[128,1536]{1,0:T(8,128)}, f32[128,1536]{1,0:T(8,128)S(1)}, u32[]{:S(2)}, u32[]{:S(2)}) collective-permute-start(f32[128,1536]{1,0:T(8,128)} %get-tuple-element.71), channel_id=1, source_target_pairs={{0,32},{1,97},{2,34},{3,99},{4,36},{5,101},{6,38},{7,103},{8,40},{... | collective-permute-start | bytes 2359304 | tf_op jit(solution)/shard_map/ppermute | solution.py:177
  32.9 14.7 %collective-permute-start.8 = (f32[32,1536]{1,0:T(8,128)S(1)}, f32[32,1536]{1,0:T(8,128)S(1)}, u32[]{:S(2)}, u32[]{:S(2)}) collective-permute-start(f32[32,1536]{1,0:T(8,128)S(1)} %shard_map.148.refs_0_), channel_id=1, source_target_pairs={{0,84},{1,85},{2,86},{3,87},{4,80},{5,81},{6,82},{7,83},{8,92},{9,... | collective-permute-start | bytes 589832 | tf_op jit(solution)/shard_map/ppermute | solution.py:177
  35.7 11.9 %collective-permute-start.7 = (f32[32,1536]{1,0:T(8,128)S(1)}, f32[32,1536]{1,0:T(8,128)S(1)}, u32[]{:S(2)}, u32[]{:S(2)}) collective-permute-start(f32[32,1536]{1,0:T(8,128)S(1)} %shard_map.148.refs_0_), channel_id=1, source_target_pairs={{0,42},{1,43},{2,40},{3,41},{4,46},{5,47},{6,44},{7,45},{8,34},{9,... | collective-permute-start | bytes 589832 | tf_op jit(solution)/shard_map/ppermute | solution.py:177
  37.9 11.5 %collective-permute-start.6 = (f32[32,1536]{1,0:T(8,128)S(1)}, f32[32,1536]{1,0:T(8,128)S(1)}, u32[]{:S(2)}, u32[]{:S(2)}) collective-permute-start(f32[32,1536]{1,0:T(8,128)S(1)} %shard_map.148.refs_0_), channel_id=1, source_target_pairs={{0,126},{1,127},{2,124},{3,125},{4,122},{5,123},{6,120},{7,121},{8... | collective-permute-start | bytes 589832 | tf_op jit(solution)/shard_map/ppermute | solution.py:177
  49.4 8.5 %collective-permute-start.11 = (f32[32,1536]{1,0:T(8,128)S(1)}, f32[32,1536]{1,0:T(8,128)S(1)}, u32[]{:S(2)}, u32[]{:S(2)}) collective-permute-start(f32[32,1536]{1,0:T(8,128)S(1)} %shard_map.149.a), channel_id=1, source_target_pairs={{0,96},{1,33},{2,98},{3,35},{4,100},{5,37},{6,102},{7,39},{8,104},... | collective-permute-start | bytes 589832 | tf_op jit(solution)/shard_map/ppermute | solution.py:177
  52.1 8.4 %collective-permute-start.10 = (f32[32,1536]{1,0:T(8,128)S(1)}, f32[32,1536]{1,0:T(8,128)S(1)}, u32[]{:S(2)}, u32[]{:S(2)}) collective-permute-start(f32[32,1536]{1,0:T(8,128)S(1)} %shard_map.149.a), channel_id=1, source_target_pairs={{0,24},{1,9},{2,26},{3,11},{4,28},{5,13},{6,30},{7,15},{8,16},{9,1... | collective-permute-start | bytes 589832 | tf_op jit(solution)/shard_map/ppermute | solution.py:177
  52.8 7.8 %collective-permute-start.9 = (f32[32,1536]{1,0:T(8,128)S(1)}, f32[32,1536]{1,0:T(8,128)S(1)}, u32[]{:S(2)}, u32[]{:S(2)}) collective-permute-start(f32[32,1536]{1,0:T(8,128)S(1)} %shard_map.149.a), channel_id=1, source_target_pairs={{0,6},{1,3},{2,4},{3,1},{4,2},{5,7},{6,0},{7,5},{8,14},{9,11},{10,... | collective-permute-start | bytes 589832 | tf_op jit(solution)/shard_map/ppermute | solution.py:177
  60.7 12.1 %collective-permute-start.14 = (f32[128,1536]{1,0:T(8,128)S(1)}, f32[128,1536]{1,0:T(8,128)S(1)}, u32[]{:S(2)}, u32[]{:S(2)}) collective-permute-start(f32[128,1536]{1,0:T(8,128)S(1)} %shard_map.150.a), channel_id=1, source_target_pairs={{0,32},{1,97},{2,34},{3,99},{4,36},{5,101},{6,38},{7,103},{8,40},{... | collective-permute-start | bytes 2359304 | tf_op jit(solution)/shard_map/ppermute | solution.py:177
  60.8 12.1 %collective-permute-start.13 = (f32[128,1536]{1,0:T(8,128)S(1)}, f32[128,1536]{1,0:T(8,128)S(1)}, u32[]{:S(2)}, u32[]{:S(2)}) collective-permute-start(f32[128,1536]{1,0:T(8,128)S(1)} %shard_map.150.a), channel_id=1, source_target_pairs={{0,8},{1,25},{2,10},{3,27},{4,12},{5,29},{6,14},{7,31},{8,0},{9,17... | collective-permute-start | bytes 2359304 | tf_op jit(solution)/shard_map/ppermute | solution.py:177
  60.9 12.3 %collective-permute-start.12 = (f32[128,1536]{1,0:T(8,128)S(1)}, f32[128,1536]{1,0:T(8,128)S(1)}, u32[]{:S(2)}, u32[]{:S(2)}) collective-permute-start(f32[128,1536]{1,0:T(8,128)S(1)} %shard_map.150.a), channel_id=1, source_target_pairs={{0,2},{1,7},{2,0},{3,5},{4,6},{5,3},{6,4},{7,1},{8,10},{9,15},{10,... | collective-permute-start | bytes 2359304 | tf_op jit(solution)/shard_map/ppermute | solution.py:177
  83.9 12.1 %collective-permute-start.16 = (f32[128,1536]{1,0:T(8,128)S(1)}, f32[128,1536]{1,0:T(8,128)S(1)}, u32[]{:S(2)}, u32[]{:S(2)}) collective-permute-start(f32[128,1536]{1,0:T(8,128)S(1)} %get-tuple-element.87), channel_id=1, source_target_pairs={{0,2},{1,7},{2,0},{3,5},{4,6},{5,3},{6,4},{7,1},{8,10},{9,15},{10,... | collective-permute-start | bytes 2359304 | tf_op jit(solution)/shard_map/ppermute | solution.py:177
  84.0 12.1 %collective-permute-start.17 = (f32[128,1536]{1,0:T(8,128)S(1)}, f32[128,1536]{1,0:T(8,128)S(1)}, u32[]{:S(2)}, u32[]{:S(2)}) collective-permute-start(f32[128,1536]{1,0:T(8,128)S(1)} %get-tuple-element.88), channel_id=1, source_target_pairs={{0,8},{1,25},{2,10},{3,27},{4,12},{5,29},{6,14},{7,31},{8,0},{9,17... | collective-permute-start | bytes 2359304 | tf_op jit(solution)/shard_map/ppermute | solution.py:177
  85.8 12.0 %collective-permute-start.18 = (f32[128,1536]{1,0:T(8,128)S(1)}, f32[128,1536]{1,0:T(8,128)S(1)}, u32[]{:S(2)}, u32[]{:S(2)}) collective-permute-start(f32[128,1536]{1,0:T(8,128)S(1)} %get-tuple-element.89), channel_id=1, source_target_pairs={{0,32},{1,97},{2,34},{3,99},{4,36},{5,101},{6,38},{7,103},{8,40},{... | collective-permute-start | bytes 2359304 | tf_op jit(solution)/shard_map/ppermute | solution.py:177
  108.7 14.6 %collective-permute-start.24 = (f32[32,1536]{1,0:T(8,128)S(1)}, f32[32,1536]{1,0:T(8,128)S(1)}, u32[]{:S(2)}, u32[]{:S(2)}) collective-permute-start(f32[32,1536]{1,0:T(8,128)S(1)} %shard_map.155.refs_0_), channel_id=1, source_target_pairs={{0,84},{1,85},{2,86},{3,87},{4,80},{5,81},{6,82},{7,83},{8,92},{9,... | collective-permute-start | bytes 589832 | tf_op jit(solution)/shard_map/ppermute | solution.py:177
  112.9 10.3 %collective-permute-start.23 = (f32[32,1536]{1,0:T(8,128)S(1)}, f32[32,1536]{1,0:T(8,128)S(1)}, u32[]{:S(2)}, u32[]{:S(2)}) collective-permute-start(f32[32,1536]{1,0:T(8,128)S(1)} %shard_map.155.refs_0_), channel_id=1, source_target_pairs={{0,42},{1,43},{2,40},{3,41},{4,46},{5,47},{6,44},{7,45},{8,34},{9,... | collective-permute-start | bytes 589832 | tf_op jit(solution)/shard_map/ppermute | solution.py:177
  114.0 11.9 %collective-permute-start.22 = (f32[32,1536]{1,0:T(8,128)S(1)}, f32[32,1536]{1,0:T(8,128)S(1)}, u32[]{:S(2)}, u32[]{:S(2)}) collective-permute-start(f32[32,1536]{1,0:T(8,128)S(1)} %shard_map.155.refs_0_), channel_id=1, source_target_pairs={{0,126},{1,127},{2,124},{3,125},{4,122},{5,123},{6,120},{7,121},{8... | collective-permute-start | bytes 589832 | tf_op jit(solution)/shard_map/ppermute | solution.py:177
  138.1 12.1 %collective-permute-start.30 = (f32[128,1536]{1,0:T(8,128)S(1)}, f32[128,1536]{1,0:T(8,128)S(1)}, u32[]{:S(2)}, u32[]{:S(2)}) collective-permute-start(f32[128,1536]{1,0:T(8,128)S(1)} %shard_map.157.a), channel_id=1, source_target_pairs={{0,32},{1,97},{2,34},{3,99},{4,36},{5,101},{6,38},{7,103},{8,40},{... | collective-permute-start | bytes 2359304 | tf_op jit(solution)/shard_map/ppermute | solution.py:177
  138.2 12.1 %collective-permute-start.29 = (f32[128,1536]{1,0:T(8,128)S(1)}, f32[128,1536]{1,0:T(8,128)S(1)}, u32[]{:S(2)}, u32[]{:S(2)}) collective-permute-start(f32[128,1536]{1,0:T(8,128)S(1)} %shard_map.157.a), channel_id=1, source_target_pairs={{0,8},{1,25},{2,10},{3,27},{4,12},{5,29},{6,14},{7,31},{8,0},{9,17... | collective-permute-start | bytes 2359304 | tf_op jit(solution)/shard_map/ppermute | solution.py:177
  138.3 12.1 %collective-permute-start.28 = (f32[128,1536]{1,0:T(8,128)S(1)}, f32[128,1536]{1,0:T(8,128)S(1)}, u32[]{:S(2)}, u32[]{:S(2)}) collective-permute-start(f32[128,1536]{1,0:T(8,128)S(1)} %shard_map.157.a), channel_id=1, source_target_pairs={{0,2},{1,7},{2,0},{3,5},{4,6},{5,3},{6,4},{7,1},{8,10},{9,15},{10,... | collective-permute-start | bytes 2359304 | tf_op jit(solution)/shard_map/ppermute | solution.py:177
  163.8 12.1 %collective-permute-start.31 = (f32[128,1536]{1,0:T(8,128)S(1)}, f32[128,1536]{1,0:T(8,128)S(1)}, u32[]{:S(2)}, u32[]{:S(2)}) collective-permute-start(f32[128,1536]{1,0:T(8,128)S(1)} %get-tuple-element.108), channel_id=1, source_target_pairs={{0,2},{1,7},{2,0},{3,5},{4,6},{5,3},{6,4},{7,1},{8,10},{9,15},{10,... | collective-permute-start | bytes 2359304 | tf_op jit(solution)/shard_map/ppermute | solution.py:177
  163.9 12.1 %collective-permute-start.32 = (f32[128,1536]{1,0:T(8,128)S(1)}, f32[128,1536]{1,0:T(8,128)S(1)}, u32[]{:S(2)}, u32[]{:S(2)}) collective-permute-start(f32[128,1536]{1,0:T(8,128)S(1)} %get-tuple-element.109), channel_id=1, source_target_pairs={{0,8},{1,25},{2,10},{3,27},{4,12},{5,29},{6,14},{7,31},{8,0},{9,17... | collective-permute-start | bytes 2359304 | tf_op jit(solution)/shard_map/ppermute | solution.py:177
  165.9 12.0 %collective-permute-start.33 = (f32[128,1536]{1,0:T(8,128)S(1)}, f32[128,1536]{1,0:T(8,128)S(1)}, u32[]{:S(2)}, u32[]{:S(2)}) collective-permute-start(f32[128,1536]{1,0:T(8,128)S(1)} %get-tuple-element.110), channel_id=1, source_target_pairs={{0,32},{1,97},{2,34},{3,99},{4,36},{5,101},{6,38},{7,103},{8,40},{... | collective-permute-start | bytes 2359304 | tf_op jit(solution)/shard_map/ppermute | solution.py:177
  (27 other events, 628.2 us)
